TPU v7x, 32 devices: a whole 2x2x4 slice. The times are simulated.
32 devices in a mesh: items: 8 (over z, core), rows: 4 (over y, x).
Axes of the slice: x: 2, y: 2, z: 4, core: 2. Of those that a mesh axis runs over, the one named last changes fastest.
Arguments:
- tokens: bfloat16 [24, 1280, 768], P('items', 'rows'), may hold values from -6 to 6
- valid_rows: int32 [24], P('items'), may hold values from 16 to 30, as said below
- dataset_ids: int32 [24], P('items'), may hold values from 0 to 7
- shift_flags: int32 [24], P('items'), may hold values 0 or 1
- norm_gains: float32 [2, 768], replicated, may hold values from 0.5 to 1.5
- norm_biases: float32 [2, 768], replicated, may hold values from -4 to 4
- qkv_weight: bfloat16 [768, 2304], replicated, may hold values from -0.21875 to 0.21875
- qv_bias: float32 [1536], replicated, may hold values from -4 to 4
- out_weight: bfloat16 [768, 768], replicated, may hold values from -6 to 6
- out_bias: float32 [768], replicated, may hold values from -4 to 4
- fc1_weight: bfloat16 [768, 3072], replicated, may hold values from -0.21875 to 0.21875
- fc1_bias: float32 [3072], replicated, may hold values from -4 to 4
- fc2_weight: bfloat16 [3072, 768], replicated, may hold values from -0.109375 to 0.109375
- fc2_bias: float32 [768], replicated, may hold values from -4 to 4
- tap_weight: bfloat16 [768, 256], replicated, may hold values from -0.21875 to 0.21875
- tap_bias: float32 [256], replicated, may hold values from -4 to 4
- conv_weights: bfloat16 [4, 2304, 256], replicated, may hold values from -0.125 to 0.125
- conv_biases: float32 [4, 256], replicated, may hold values from -4 to 4
- table_gain: float32 [8, 256], replicated, may hold values from 0.1 to 1.9
- table_shift: float32 [8, 256], replicated, may hold values from -6 to 6
- token_cotangent: bfloat16 [24, 1280, 768], P('items', 'rows'), may hold values from -6 to 6
- joined_cotangent: bfloat16 [24, 64, 80, 256], P('items', 'rows'), may hold values from -6 to 6
Outputs:
- out_tokens: bfloat16 [24, 1280, 768], P('items', 'rows')
- joined: bfloat16 [24, 64, 80, 256], P('items', 'rows')
- grad_tokens: float32 [24, 1280, 768], P('items', 'rows')
- grad_norm_gains: float32 [2, 768], P(None, 'rows')
- grad_norm_biases: float32 [2, 768], P(None, 'rows')
- grad_qkv_weight: float32 [768, 2304], P('rows')
- grad_qv_bias: float32 [1536], P('rows')
- grad_out_weight: float32 [768, 768], P('rows')
- grad_out_bias: float32 [768], P('rows')
- grad_fc1_weight: float32 [768, 3072], P('rows')
- grad_fc1_bias: float32 [3072], P('rows')
- grad_fc2_weight: float32 [3072, 768], P('rows')
- grad_fc2_bias: float32 [768], P('rows')
- grad_tap_weight: float32 [768, 256], P('rows')
- grad_tap_bias: float32 [256], P('rows')
- grad_conv_weights: float32 [4, 2304, 256], P(None, 'rows')
- grad_conv_biases: float32 [4, 256], P(None, 'rows')
- grad_table_gain: float32 [8, 256], P(None, 'rows')
- grad_table_shift: float32 [8, 256], P(None, 'rows')
Inputs may be any that keep to these rules, and one draw needn't show every extreme that they name: `valid_rows`: valid patch rows of each item, counted from the top of its grid; in each aligned block of 3 items one item has the most.
All inputs are finite; a program needn't handle non-finite values. No bound on the sum of `shift_flags` on one device may be relied on, other than what follows from the above.
Results may differ from a plain program's by a relative error of at most 0.022.
Values may be sent and summed in bfloat16 or wider, within the bound.
A program may use at most 384 MiB of HBM per device.

v0:
```python
import jax
import jax.numpy as jnp
from jax import lax
from jax.sharding import PartitionSpec as P

HEAD_DIM = 64
PC = 40


epsilon = 1e-06
highest = lax.Precision.HIGHEST


def padded_2(block, sides, width):
    for axis, dim in sides:
        count = lax.axis_size(axis)
        forward = [(i, i + 1) for i in range(count - 1)]
        backward = [(target, source) for source, target in forward]
        low = lax.ppermute(
            lax.slice_in_dim(block, block.shape[dim] - width, None, axis=dim), axis, forward
        )
        high = lax.ppermute(lax.slice_in_dim(block, 0, width, axis=dim), axis, backward)
        block = jnp.concatenate([low, block, high], axis=dim)
    return block


def layer_norm(values, gain, shift):
    centre = jnp.mean(values, axis=-1, keepdims=True)
    centred = values - centre
    spread = jnp.mean(centred * centred, axis=-1, keepdims=True)
    return centred * lax.rsqrt(spread + epsilon) * gain + shift


def gelu_exact(values):
    return jax.nn.gelu(values, approximate=False)


def norm_back(values, gain, shift, grad_out):
    result, pullback = jax.vjp(layer_norm, values, gain, shift)
    return pullback(grad_out)


def gelu_back(values, grad_out):
    result, pullback = jax.vjp(gelu_exact, values)
    return pullback(grad_out)[0]


def masked_scores(queries, key_block, start, valid_rows):
    raw = jnp.einsum(
        "ithd,ishd->ihts", queries, key_block, preferred_element_type=jnp.float32
    ) * HEAD_DIM ** (-0.5)
    position = start + jnp.arange(key_block.shape[1], dtype=jnp.int32)
    allowed = (position // PC)[None, :] < valid_rows[:, None]
    return jnp.where(allowed[:, None, None, :], raw, -1e30)


def neighbourhood(framed):
    padded = jnp.pad(framed, ((0, 0), (0, 0), (1, 1), (0, 0)))
    rows_out = padded.shape[1] - 2
    cols_out = padded.shape[2] - 2
    pieces = [
        padded[:, row_step : row_step + rows_out, col_step : col_step + cols_out, :]
        for row_step in range(3)
        for col_step in range(3)
    ]
    return jnp.concatenate(pieces, axis=-1)


def forward_patches(acts):
    framed = padded_2(acts, (("rows", 1),), 1)
    return neighbourhood(framed)


def backward_patches(grads):
    framed = padded_2(grads, (("rows", 1),), 1)
    return neighbourhood(framed)


def conv_apply(patches, kernel, bias_row):
    flat = (
        jnp.dot(patches.reshape(-1, patches.shape[-1]), kernel, preferred_element_type=jnp.float32)
        + bias_row
    )
    return flat.reshape(patches.shape[:-1] + (kernel.shape[1],))


def flipped_kernel(weight, channels):
    grid_kernel = weight.reshape(3, 3, channels, channels)
    return jnp.transpose(grid_kernel[::-1, ::-1], (0, 1, 3, 2)).reshape(9 * channels, channels)


def double_with(field, before_edge, after_edge, which_dim):
    length = field.shape[which_dim]
    before = jnp.concatenate(
        [before_edge, lax.slice_in_dim(field, 0, length - 1, axis=which_dim)], which_dim
    )
    after_rows = jnp.concatenate(
        [lax.slice_in_dim(field, 1, length, axis=which_dim), after_edge], which_dim
    )
    even_rows = 0.75 * field + 0.25 * before
    odd_rows = 0.75 * field + 0.25 * after_rows
    paired = jnp.stack([even_rows, odd_rows], which_dim + 1)
    new_shape = field.shape[:which_dim] + (2 * length,) + field.shape[which_dim + 1 :]
    return paired.reshape(new_shape)


def double_back(grad, prev_odd, next_even, which_dim):
    length = grad.shape[which_dim] // 2
    split_shape = grad.shape[:which_dim] + (length, 2) + grad.shape[which_dim + 1 :]
    paired = grad.reshape(split_shape)
    even_part = lax.index_in_dim(paired, 0, which_dim + 1, keepdims=False)
    odd_part = lax.index_in_dim(paired, 1, which_dim + 1, keepdims=False)
    if prev_odd is None:
        prev_odd = lax.slice_in_dim(even_part, 0, 1, axis=which_dim)
        next_even = lax.slice_in_dim(odd_part, length - 1, length, axis=which_dim)
    from_next = jnp.concatenate(
        [lax.slice_in_dim(even_part, 1, length, axis=which_dim), next_even], which_dim
    )
    from_prev = jnp.concatenate(
        [prev_odd, lax.slice_in_dim(odd_part, 0, length - 1, axis=which_dim)], which_dim
    )
    return 0.75 * (even_part + odd_part) + 0.25 * from_next + 0.25 * from_prev


def shards(
    tokens,
    valid_rows,
    dataset_ids,
    shift_flags,
    norm_gains,
    norm_biases,
    qkv_weight,
    qv_bias,
    out_weight,
    out_bias,
    fc1_weight,
    fc1_bias,
    fc2_weight,
    fc2_bias,
    tap_weight,
    tap_bias,
    conv_weights,
    conv_biases,
    table_gain,
    table_shift,
    token_cotangent,
    joined_cotangent,
):
    items_here, tok_here, model_width = tokens.shape
    rows_here = tok_here // PC
    channels = tap_weight.shape[1]
    head_count = model_width // HEAD_DIM
    score_scale = HEAD_DIM ** (-0.5)
    row_index = lax.axis_index("rows")
    last_index = lax.axis_size("rows") - 1
    flat_in = tokens.reshape(-1, model_width).astype(jnp.float32)
    normed_one = layer_norm(flat_in, norm_gains[0], norm_biases[0]).astype(jnp.bfloat16)
    qkv_bias = jnp.concatenate(
        [qv_bias[:model_width], jnp.zeros((model_width,), jnp.float32), qv_bias[model_width:]]
    )
    qkv_low = (
        jnp.dot(normed_one, qkv_weight, preferred_element_type=jnp.float32) + qkv_bias
    ).astype(jnp.bfloat16)
    queries = qkv_low[:, :model_width].reshape(items_here, tok_here, head_count, HEAD_DIM)
    key_rows = qkv_low[:, model_width : 2 * model_width].reshape(items_here, tok_here, model_width)
    values = qkv_low[:, 2 * model_width :].reshape(items_here, tok_here, model_width)

    def fold_keys(update, initial):
        return update(
            initial,
            (
                lax.all_gather(key_rows, "rows", axis=1, tiled=True),
                lax.all_gather(values, "rows", axis=1, tiled=True),
            ),
            jnp.int32(0),
        )

    def fold_totals(carry, piece, start):
        top_run, total_run = carry
        block = masked_scores(
            queries, piece[0].reshape(items_here, -1, head_count, HEAD_DIM), start, valid_rows
        )
        top_new = jnp.maximum(top_run, jnp.max(block, axis=-1))
        total_new = jnp.sum(jnp.exp(block - top_new[..., None]), axis=-1)
        return (top_new, total_new)

    stat_shape = (items_here, head_count, tok_here)
    top_score, sum_score = fold_keys(
        fold_totals, (jnp.full(stat_shape, -1e30, jnp.float32), jnp.zeros(stat_shape, jnp.float32))
    )
    log_total = top_score + jnp.log(sum_score)

    def fold_output(carry, piece, start):
        block = masked_scores(
            queries, piece[0].reshape(items_here, -1, head_count, HEAD_DIM), start, valid_rows
        )
        weights_low = jnp.exp(block - log_total[..., None]).astype(jnp.bfloat16)
        return jnp.einsum(
            "ihts,ishd->ithd",
            weights_low,
            piece[1].reshape(items_here, -1, head_count, HEAD_DIM),
            preferred_element_type=jnp.float32,
        )

    attended = fold_keys(
        fold_output, jnp.zeros((items_here, tok_here, head_count, HEAD_DIM), jnp.float32)
    ).astype(jnp.bfloat16)
    attended_flat = attended.reshape(-1, model_width)
    resid = (
        flat_in + jnp.dot(attended_flat, out_weight, preferred_element_type=jnp.float32) + out_bias
    )
    normed_two = layer_norm(resid, norm_gains[1], norm_biases[1]).astype(jnp.bfloat16)
    hidden_pre = jnp.dot(normed_two, fc1_weight, preferred_element_type=jnp.float32) + fc1_bias
    hidden = gelu_exact(hidden_pre).astype(jnp.bfloat16)
    output = resid + jnp.dot(hidden, fc2_weight, preferred_element_type=jnp.float32) + fc2_bias
    output_low = output.astype(jnp.bfloat16)
    grid_rows = row_index * rows_here + jnp.arange(rows_here, dtype=jnp.int32)
    row_valid = (grid_rows[None, :] < valid_rows[:, None]).astype(jnp.float32)
    token_valid = jnp.broadcast_to(row_valid[:, :, None], (items_here, rows_here, PC)).reshape(
        -1, 1
    )
    tap_pre = jnp.dot(output_low, tap_weight, preferred_element_type=jnp.float32) + tap_bias
    field = (tap_pre * token_valid).reshape(items_here, rows_here, PC, channels)
    saved = []
    for unit_index in range(2):
        act_one = gelu_exact(field).astype(jnp.bfloat16)
        patch_one = forward_patches(act_one)
        conv_one = conv_apply(patch_one, conv_weights[2 * unit_index], conv_biases[2 * unit_index])
        act_two = gelu_exact(conv_one).astype(jnp.bfloat16)
        patch_two = forward_patches(act_two)
        conv_two = conv_apply(
            patch_two, conv_weights[2 * unit_index + 1], conv_biases[2 * unit_index + 1]
        )
        saved.append((field, patch_one, conv_one, patch_two))
        field = field + conv_two
    framed = padded_2(field.astype(jnp.bfloat16), (("rows", 1),), 1).astype(field.dtype)
    above = jnp.where(row_index == 0, field[:, :1], framed[:, :1])
    below = jnp.where(row_index == last_index, field[:, -1:], framed[:, -1:])
    tall = double_with(field, above, below, 1)
    wide = double_with(tall, tall[:, :, :1], tall[:, :, -1:], 2)
    choose = (
        dataset_ids[:, None] == jnp.arange(table_gain.shape[0], dtype=jnp.int32)[None, :]
    ).astype(jnp.float32)
    flag_value = shift_flags.astype(jnp.float32)[:, None]
    gain_pick = jnp.dot(choose, table_gain, precision=highest)
    shift_pick = jnp.dot(choose, table_shift, precision=highest)
    factor = 1.0 + flag_value * (gain_pick - 1.0)
    offset = flag_value * shift_pick
    joined = (wide * factor[:, None, None, :] + offset[:, None, None, :]).astype(jnp.bfloat16)
    joined_grad = joined_cotangent.astype(jnp.float32)
    grad_gain_pick = flag_value * jnp.sum(joined_grad * wide, axis=(1, 2))
    grad_shift_pick = flag_value * jnp.sum(joined_grad, axis=(1, 2))
    grad_table_gain = jnp.dot(choose.T, grad_gain_pick, precision=highest)
    grad_table_shift = jnp.dot(choose.T, grad_shift_pick, precision=highest)
    grad_wide = joined_grad * factor[:, None, None, :]
    grad_tall = double_back(grad_wide, None, None, 2)
    framed_grad = padded_2(grad_tall.astype(jnp.bfloat16), (("rows", 1),), 1).astype(
        grad_tall.dtype
    )
    prev_odd = jnp.where(row_index == 0, framed_grad[:, 1:2], framed_grad[:, :1])
    next_even = jnp.where(row_index == last_index, framed_grad[:, -2:-1], framed_grad[:, -1:])
    grad_field = double_back(grad_tall, prev_odd, next_even, 1)
    conv_weight_grads = [None, None, None, None]
    conv_bias_grads = [None, None, None, None]
    for unit_index in (1, 0):
        field_in, patch_one, conv_one, patch_two = saved[unit_index]
        second = 2 * unit_index + 1
        first_conv = 2 * unit_index
        grad_two = grad_field.astype(jnp.bfloat16)
        conv_weight_grads[second] = jnp.einsum(
            "pk,pc->kc",
            patch_two.reshape(-1, 9 * channels),
            grad_two.reshape(-1, channels),
            preferred_element_type=jnp.float32,
        )
        conv_bias_grads[second] = jnp.sum(grad_two.astype(jnp.float32), axis=(0, 1, 2))
        grad_act_two = conv_apply(
            backward_patches(grad_two), flipped_kernel(conv_weights[second], channels), 0.0
        )
        grad_one = gelu_back(conv_one, grad_act_two).astype(jnp.bfloat16)
        conv_weight_grads[first_conv] = jnp.einsum(
            "pk,pc->kc",
            patch_one.reshape(-1, 9 * channels),
            grad_one.reshape(-1, channels),
            preferred_element_type=jnp.float32,
        )
        conv_bias_grads[first_conv] = jnp.sum(grad_one.astype(jnp.float32), axis=(0, 1, 2))
        grad_act_one = conv_apply(
            backward_patches(grad_one), flipped_kernel(conv_weights[first_conv], channels), 0.0
        )
        grad_field = grad_field + gelu_back(field_in, grad_act_one)
    grad_tap = (grad_field.reshape(-1, channels) * token_valid).astype(jnp.bfloat16)
    grad_tap_weight = jnp.einsum(
        "pd,pc->dc", output_low, grad_tap, preferred_element_type=jnp.float32
    )
    grad_tap_bias = jnp.sum(grad_tap.astype(jnp.float32), axis=0)
    grad_output = token_cotangent.reshape(-1, model_width).astype(jnp.float32) + jnp.einsum(
        "pc,dc->pd", grad_tap, tap_weight, preferred_element_type=jnp.float32
    )
    grad_mlp = grad_output.astype(jnp.bfloat16)
    grad_fc2_weight = jnp.einsum("pf,pd->fd", hidden, grad_mlp, preferred_element_type=jnp.float32)
    grad_fc2_bias = jnp.sum(grad_mlp.astype(jnp.float32), axis=0)
    grad_hidden = jnp.einsum("pd,fd->pf", grad_mlp, fc2_weight, preferred_element_type=jnp.float32)
    grad_pre = gelu_back(hidden_pre, grad_hidden).astype(jnp.bfloat16)
    grad_fc1_weight = jnp.einsum(
        "pd,pf->df", normed_two, grad_pre, preferred_element_type=jnp.float32
    )
    grad_fc1_bias = jnp.sum(grad_pre.astype(jnp.float32), axis=0)
    grad_normed_two = jnp.einsum(
        "pf,df->pd", grad_pre, fc1_weight, preferred_element_type=jnp.float32
    )
    grad_resid_norm, grad_gain_two, grad_shift_two = norm_back(
        resid, norm_gains[1], norm_biases[1], grad_normed_two
    )
    grad_resid = grad_output + grad_resid_norm
    grad_branch = grad_resid.astype(jnp.bfloat16)
    grad_out_weight = jnp.einsum(
        "pd,pe->de", attended_flat, grad_branch, preferred_element_type=jnp.float32
    )
    grad_out_bias = jnp.sum(grad_branch.astype(jnp.float32), axis=0)
    grad_attended = jnp.einsum(
        "pe,de->pd", grad_branch, out_weight, preferred_element_type=jnp.float32
    ).astype(jnp.bfloat16)
    grad_heads = grad_attended.reshape(items_here, tok_here, head_count, HEAD_DIM)
    key_all, value_all = (
        lax.all_gather(key_rows, "rows", axis=1, tiled=True),
        lax.all_gather(values, "rows", axis=1, tiled=True),
    )
    full_keys = key_all.reshape(items_here, -1, head_count, HEAD_DIM)
    full_values = value_all.reshape(items_here, -1, head_count, HEAD_DIM)
    scores = masked_scores(queries, full_keys, 0, valid_rows)
    probs = jnp.exp(scores - log_total[..., None])
    grad_probs = jnp.einsum(
        "ithd,ishd->ihts", grad_heads, full_values, preferred_element_type=jnp.float32
    )
    row_dots = jnp.sum(grad_probs * probs, axis=-1)
    grad_scores = (probs * (grad_probs - row_dots[..., None])).astype(jnp.bfloat16)
    grad_queries = (
        jnp.einsum("ihts,ishd->ithd", grad_scores, full_keys, preferred_element_type=jnp.float32)
        * score_scale
    )
    grad_keys_all = (
        jnp.einsum("ihts,ithd->ishd", grad_scores, queries, preferred_element_type=jnp.float32)
        * score_scale
    )
    grad_values_all = jnp.einsum(
        "ihts,ithd->ishd",
        probs.astype(jnp.bfloat16),
        grad_heads,
        preferred_element_type=jnp.float32,
    )
    grad_keys, grad_values = (
        lax.psum_scatter(
            grad_keys_all.reshape(items_here, -1, model_width).astype(jnp.bfloat16),
            "rows",
            scatter_dimension=1,
            tiled=True,
        ).astype(jnp.float32),
        lax.psum_scatter(
            grad_values_all.reshape(items_here, -1, model_width).astype(jnp.bfloat16),
            "rows",
            scatter_dimension=1,
            tiled=True,
        ).astype(jnp.float32),
    )
    grad_qkv = jnp.concatenate(
        [
            grad_queries.reshape(-1, model_width),
            grad_keys.reshape(-1, model_width),
            grad_values.reshape(-1, model_width),
        ],
        axis=-1,
    ).astype(jnp.bfloat16)
    grad_qkv_weight = jnp.einsum(
        "pd,pe->de", normed_one, grad_qkv, preferred_element_type=jnp.float32
    )
    column_sums = jnp.sum(grad_qkv.astype(jnp.float32), axis=0)
    grad_qv_bias = jnp.concatenate([column_sums[:model_width], column_sums[2 * model_width :]])
    grad_normed_one = jnp.einsum(
        "pe,de->pd", grad_qkv, qkv_weight, preferred_element_type=jnp.float32
    )
    grad_in_norm, grad_gain_one, grad_shift_one = norm_back(
        flat_in, norm_gains[0], norm_biases[0], grad_normed_one
    )
    grad_tokens = (grad_resid + grad_in_norm).reshape(items_here, tok_here, model_width)
    grad_norm_gains = jnp.stack([grad_gain_one, grad_gain_two])
    grad_norm_biases = jnp.stack([grad_shift_one, grad_shift_two])
    grad_conv_weights = jnp.stack(conv_weight_grads)
    grad_conv_biases = jnp.stack(conv_bias_grads)
    summed = (
        lax.psum(grad_norm_gains.astype(jnp.bfloat16), "items").astype(jnp.float32),
        lax.psum(grad_norm_biases.astype(jnp.bfloat16), "items").astype(jnp.float32),
        lax.psum(grad_qkv_weight.astype(jnp.bfloat16), "items").astype(jnp.float32),
        lax.psum(grad_qv_bias.astype(jnp.bfloat16), "items").astype(jnp.float32),
        lax.psum(grad_out_weight.astype(jnp.bfloat16), "items").astype(jnp.float32),
        lax.psum(grad_out_bias.astype(jnp.bfloat16), "items").astype(jnp.float32),
        lax.psum(grad_fc1_weight.astype(jnp.bfloat16), "items").astype(jnp.float32),
        lax.psum(grad_fc1_bias.astype(jnp.bfloat16), "items").astype(jnp.float32),
        lax.psum(grad_fc2_weight.astype(jnp.bfloat16), "items").astype(jnp.float32),
        lax.psum(grad_fc2_bias.astype(jnp.bfloat16), "items").astype(jnp.float32),
        lax.psum(grad_tap_weight.astype(jnp.bfloat16), "items").astype(jnp.float32),
        lax.psum(grad_tap_bias.astype(jnp.bfloat16), "items").astype(jnp.float32),
        lax.psum(grad_conv_weights.astype(jnp.bfloat16), "items").astype(jnp.float32),
        lax.psum(grad_conv_biases.astype(jnp.bfloat16), "items").astype(jnp.float32),
        lax.psum(grad_table_gain.astype(jnp.bfloat16), "items").astype(jnp.float32),
        lax.psum(grad_table_shift.astype(jnp.bfloat16), "items").astype(jnp.float32),
    )
    shared = (
        lax.psum_scatter(
            summed[0].astype(jnp.bfloat16), "rows", scatter_dimension=1, tiled=True
        ).astype(jnp.float32),
        lax.psum_scatter(
            summed[1].astype(jnp.bfloat16), "rows", scatter_dimension=1, tiled=True
        ).astype(jnp.float32),
        lax.psum_scatter(
            summed[2].astype(jnp.bfloat16), "rows", scatter_dimension=0, tiled=True
        ).astype(jnp.float32),
        lax.psum_scatter(
            summed[3].astype(jnp.bfloat16), "rows", scatter_dimension=0, tiled=True
        ).astype(jnp.float32),
        lax.psum_scatter(
            summed[4].astype(jnp.bfloat16), "rows", scatter_dimension=0, tiled=True
        ).astype(jnp.float32),
        lax.psum_scatter(
            summed[5].astype(jnp.bfloat16), "rows", scatter_dimension=0, tiled=True
        ).astype(jnp.float32),
        lax.psum_scatter(
            summed[6].astype(jnp.bfloat16), "rows", scatter_dimension=0, tiled=True
        ).astype(jnp.float32),
        lax.psum_scatter(
            summed[7].astype(jnp.bfloat16), "rows", scatter_dimension=0, tiled=True
        ).astype(jnp.float32),
        lax.psum_scatter(
            summed[8].astype(jnp.bfloat16), "rows", scatter_dimension=0, tiled=True
        ).astype(jnp.float32),
        lax.psum_scatter(
            summed[9].astype(jnp.bfloat16), "rows", scatter_dimension=0, tiled=True
        ).astype(jnp.float32),
        lax.psum_scatter(
            summed[10].astype(jnp.bfloat16), "rows", scatter_dimension=0, tiled=True
        ).astype(jnp.float32),
        lax.psum_scatter(
            summed[11].astype(jnp.bfloat16), "rows", scatter_dimension=0, tiled=True
        ).astype(jnp.float32),
        lax.psum_scatter(
            summed[12].astype(jnp.bfloat16), "rows", scatter_dimension=1, tiled=True
        ).astype(jnp.float32),
        lax.psum_scatter(
            summed[13].astype(jnp.bfloat16), "rows", scatter_dimension=1, tiled=True
        ).astype(jnp.float32),
        lax.psum_scatter(
            summed[14].astype(jnp.bfloat16), "rows", scatter_dimension=1, tiled=True
        ).astype(jnp.float32),
        lax.psum_scatter(
            summed[15].astype(jnp.bfloat16), "rows", scatter_dimension=1, tiled=True
        ).astype(jnp.float32),
    )
    out_tokens = output_low.reshape(items_here, tok_here, model_width)
    return (
        out_tokens,
        joined,
        grad_tokens,
        shared[0],
        shared[1],
        shared[2],
        shared[3],
        shared[4],
        shared[5],
        shared[6],
        shared[7],
        shared[8],
        shared[9],
        shared[10],
        shared[11],
        shared[12],
        shared[13],
        shared[14],
        shared[15],
    )


def solution(mesh):
    return jax.shard_map(
        shards,
        mesh=mesh,
        in_specs=(
            P("items", "rows", None),
            P("items"),
            P("items"),
            P("items"),
            P(),
            P(),
            P(),
            P(),
            P(),
            P(),
            P(),
            P(),
            P(),
            P(),
            P(),
            P(),
            P(),
            P(),
            P(),
            P(),
            P("items", "rows", None),
            P("items", "rows", None, None),
        ),
        out_specs=(
            P("items", "rows", None),
            P("items", "rows", None, None),
            P("items", "rows", None),
            P(None, "rows"),
            P(None, "rows"),
            P("rows", None),
            P("rows"),
            P("rows", None),
            P("rows"),
            P("rows", None),
            P("rows"),
            P("rows", None),
            P("rows"),
            P("rows", None),
            P("rows"),
            P(None, "rows", None),
            P(None, "rows"),
            P(None, "rows"),
            P(None, "rows"),
        ),
        check_vma=False,
    )
```

profile of v0, /device:TPU:0, one launch (start us, length us, event | category | flops | bytes accessed | tf_op | source)
XLA Modules:
  0.0 1257.4 jit_solution(3363566249056475184)
XLA Ops:
  39.8 55.4 %all-gather.5.cloned.1.call-done = bf16[3,1280,768]{2,1,0:T(8,128)(2,1)} async-done(((bf16[3,320,768]{2,1,0:T(8,128)(2,1)}), bf16[3,1280,768]{2,1,0:T(8,128)(2,1)}) %all-gather.5.cloned.1.call-update) | async-done | bytes 5898256 | tf_op jit(solution)/shard_map/all_gather | solution.py:172
  104.1 24.4 %fusion.147 = (f32[3,12,320]{2,1,0:T(8,128)S(1)}, f32[3,12,320,1280]{3,2,1,0:T(8,128)}) fusion(bf16[3,320,12,64]{1,3,2,0:T(8,128)(2,1)} %copy.132, bf16[3,1280,12,64]{1,3,2,0:T(8,128)(2,1)} %bitcast.268, pred[3,1280]{1,0:T(4,128)(4,1)S(1)} %broadcast_compare_fusion), kind=kOutput, calls=%fused_computation.407 | convolution fusion | flops 1931662080 | bytes 66405120 | tf_op jit(solution)/shard_map/ithd,ishd->ihts/dot_general | solution.py:49
  129.7 23.0 %exponential_reduce_fusion = f32[3,12,320]{2,1,0:T(8,128)} fusion(f32[3,12,320,1280]{3,2,1,0:T(8,128)} %get-tuple-element.199, f32[3,12,320]{2,1,0:T(8,128)} %broadcast_maximum_fusion), kind=kLoop, calls=%fused_computation.3 | loop fusion | flops 29479680 | bytes 59074560 | tf_op jit(solution)/shard_map/reduce_sum | solution.py:184
  173.4 23.4 %convert_bitcast_fusion = bf16[3,320,12,64]{1,3,2,0:T(8,128)(2,1)} fusion(bf16[3,1280,12,64]{1,3,2,0:T(8,128)(2,1)} %bitcast.266, f32[3,12,320,1280]{3,2,1,0:T(8,128)} %get-tuple-element.199, f32[3,12,320]{2,1,0:T(8,128)} %log_add_fusion), kind=kOutput, calls=%fused_computation.97 | convolution fusion | flops 1917665280 | bytes 66401280 | tf_op jit(solution)/shard_map/ihts,ishd->ithd/dot_general | solution.py:198
  211.5 37.1 %multiply_convert_fusion.2 = (bf16[960,3072]{1,0:T(8,128)(2,1)S(1)}, f32[960,3072]{1,0:T(8,128)}, f32[960,3072]{1,0:T(8,128)}) fusion(f32[3072]{0:T(1024)S(1)} %copy-done.97, bf16[768,3072]{1,0:T(8,128)(2,1)} %param.32, f32[960,768]{1,0:T(8,128)S(1)} %bitcast_add_fusion, f32[768]{0:T(1024)S(1)} %copy-done.89, f32[768]{0:T(1024)S(1)} %get-tuple-element.214, ...), kind=kOutput, calls=%fused_computation.10 | convolution fusion | flops 4728913920 | bytes 37188096 | tf_op jit(solution)/shard_map/dot_general | solution.py:213
  438.7 18.2 %fusion.126 = (bf16[3072]{0:T(1024)(128)(2,1)}, bf16[960,3072]{1,0:T(8,128)(2,1)}) fusion(f32[960,3072]{1,0:T(8,128)} %get-tuple-element.123, f32[960,3072]{1,0:T(8,128)} %get-tuple-element.200, f32[3072]{0:T(1024)S(1)} %copy-done.98, bf16[960,768]{1,0:T(8,128)(2,1)} %get-tuple-element.115, bf16[3072,768]{1,0:T(8,128)(2,1)} %param.34), kind=kOutput, calls=%fused_computation.387 | convolution fusion | flops 4577031168 | bytes 35702784 | tf_op jit(solution)/shard_map/pd,fd->pf/dot_general | solution.py:303
  485.2 24.5 %fusion.11 = bf16[3,12,64,1280]{3,2,1,0:T(8,128)(2,1)} fusion(bf16[3,320,12,64]{1,3,2,0:T(8,128)(2,1)} %copy.154, f32[3,12,320,1280]{3,2,1,0:T(8,128)} %get-tuple-element.199, f32[3,12,320]{2,1,0:T(8,128)} %log_add_fusion), kind=kOutput, calls=%fused_computation.30 | convolution fusion | flops 1919877120 | bytes 66401280 | tf_op jit(solution)/shard_map/ihts,ithd->ishd/dot_general | solution.py:346
  509.7 43.3 %multiply_reduce_fusion = (f32[3,12,320]{2,1,0:T(8,128)}, f32[3,12,320,1280]{3,2,1,0:T(8,128)}) fusion(f32[3,12,320,1280]{3,2,1,0:T(8,128)} %get-tuple-element.199, f32[3,12,320]{2,1,0:T(8,128)} %log_add_fusion, bf16[3,320,12,64]{1,3,2,0:T(8,128)(2,1)} %copy.154, bf16[3,1280,12,64]{1,3,2,0:T(8,128)(2,1)} %bitcast.267), kind=kOutput, calls=%fused_computation.1 | convolution fusion | flops 1931662080 | bytes 125429760 | tf_op jit(solution)/shard_map/ithd,ishd->ihts/dot_general | solution.py:333
  561.9 49.3 %multiply_convert_fusion = bf16[3,12,320,1280]{3,2,1,0:T(8,128)(2,1)} fusion(f32[3,12,320,1280]{3,2,1,0:T(8,128)} %get-tuple-element.209, f32[3,12,320,1280]{3,2,1,0:T(8,128)} %get-tuple-element.199, f32[3,12,320]{2,1,0:T(8,128)} %get-tuple-element.208, f32[3,12,320]{2,1,0:T(8,128)} %log_add_fusion), kind=kLoop, calls=%fused_computation | loop fusion | flops 58982400 | bytes 147548160 | tf_op jit(solution)/shard_map/convert_element_type | solution.py:337
  611.2 15.3 %multiply_convert_fusion.1 = bf16[3,12,64,1280]{3,2,1,0:T(8,128)(2,1)} fusion(bf16[3,320,12,64]{1,3,2,0:T(8,128)(2,1)} %copy.132, bf16[3,12,320,1280]{3,2,1,0:T(8,128)(2,1)} %multiply_convert_fusion), kind=kOutput, calls=%fused_computation.8 | convolution fusion | flops 1893335040 | bytes 36864000 | tf_op jit(solution)/shard_map/ihts,ithd->ishd/dot_general | solution.py:343
  667.7 10.4 convolution_convert_fusion.1
  678.4 15.3 %fusion.35 = bf16[3,320,12,64]{1,3,2,0:T(8,128)(2,1)S(1)} fusion(bf16[3,1280,12,64]{1,3,2,0:T(8,128)(2,1)} %bitcast.269, bf16[3,12,320,1280]{3,2,1,0:T(8,128)(2,1)} %multiply_convert_fusion), kind=kOutput, calls=%fused_computation.99 | convolution fusion | flops 1888911360 | bytes 36864000 | tf_op jit(solution)/shard_map/ihts,ishd->ithd/dot_general | solution.py:339
  743.5 17.3 %reduce-scatter.30.cloned.1.call-done = bf16[192,768]{1,0:T(8,128)(2,1)} async-done(((bf16[768,768]{1,0:T(8,128)(2,1)}), bf16[192,768]{1,0:T(8,128)(2,1)}) %reduce-scatter.30.cloned.1.call-update) | async-done | bytes 294928 | tf_op jit(solution)/shard_map/reduce_scatter | solution.py:421
  760.8 60.1 %reduce-scatter.38.cloned.1.call-done = bf16[4,576,256]{2,1,0:T(8,128)(2,1)} async-done(((bf16[4,2304,256]{2,1,0:T(8,128)(2,1)}), bf16[4,576,256]{2,1,0:T(8,128)(2,1)}) %reduce-scatter.38.cloned.1.call-update) | async-done | bytes 1179664 | tf_op jit(solution)/shard_map/reduce_scatter | solution.py:445
  821.0 60.1 %reduce-scatter.34.cloned.1.call-done = bf16[768,768]{1,0:T(8,128)(2,1)} async-done(((bf16[3072,768]{1,0:T(8,128)(2,1)}), bf16[768,768]{1,0:T(8,128)(2,1)}) %reduce-scatter.34.cloned.1.call-update) | async-done | bytes 1179664 | tf_op jit(solution)/shard_map/reduce_scatter | solution.py:433
  881.1 60.1 %reduce-scatter.32.cloned.1.call-done = bf16[192,3072]{1,0:T(8,128)(2,1)} async-done(((bf16[768,3072]{1,0:T(8,128)(2,1)}), bf16[192,3072]{1,0:T(8,128)(2,1)}) %reduce-scatter.32.cloned.1.call-update) | async-done | bytes 1179664 | tf_op jit(solution)/shard_map/reduce_scatter | solution.py:427
  941.2 50.2 %reduce-scatter.28.cloned.1.call-done = bf16[192,2304]{1,0:T(8,128)(2,1)} async-done(((bf16[768,2304]{1,0:T(8,128)(2,1)}), bf16[192,2304]{1,0:T(8,128)(2,1)}) %reduce-scatter.28.cloned.1.call-update) | async-done | bytes 884752 | tf_op jit(solution)/shard_map/reduce_scatter | solution.py:415
  998.8 19.0 %reduce-scatter.46.cloned.1.call-done = bf16[64,8]{1,0:T(8,128)(2,1)} async-done(((bf16[256,8]{1,0:T(8,128)(2,1)}), bf16[64,8]{1,0:T(8,128)(2,1)}) %reduce-scatter.46.cloned.1.call-update) | async-done | bytes 1040
  1019.2 25.2 %reduce-scatter.48.cloned.1.call-done = bf16[64,8]{1,0:T(8,128)(2,1)} async-done(((bf16[256,8]{1,0:T(8,128)(2,1)}), bf16[64,8]{1,0:T(8,128)(2,1)}) %reduce-scatter.48.cloned.1.call-update) | async-done | bytes 1040
  1045.7 25.1 %reduce-scatter.44.cloned.1.call-done = bf16[64,4]{1,0:T(8,128)(2,1)} async-done(((bf16[256,4]{1,0:T(8,128)(2,1)}), bf16[64,4]{1,0:T(8,128)(2,1)}) %reduce-scatter.44.cloned.1.call-update) | async-done | bytes 528
  1075.7 16.3 %all-reduce.15 = (bf16[1536]{0:T(1024)(128)(2,1)}, bf16[768]{0:T(1024)(128)(2,1)}, bf16[3072]{0:T(1024)(128)(2,1)}, bf16[768]{0:T(1024)(128)(2,1)}, bf16[256]{0:T(256)(128)(2,1)}) all-reduce(bf16[1536]{0:T(1024)(128)(2,1)} %pad_maximum_fusion.27, ...), channel_id=7, replica_groups=mesh['items'=8,'rows'=4] {'rows'}, use_global_device_ids=true, to_apply=%region_25.26.clone | all-reduce | flops 6400 | bytes 25600
  1110.8 14.9 %reduce-scatter.42.cloned.1.call-done = bf16[192,2]{1,0:T(8,128)(2,1)} async-done(((bf16[768,2]{1,0:T(8,128)(2,1)}), bf16[192,2]{1,0:T(8,128)(2,1)}) %reduce-scatter.42.cloned.1.call-update) | async-done | bytes 784
  1127.2 29.4 %all-reduce.13 = (bf16[2,192]{1,0:T(2,128)(2,1)}, bf16[2,192]{1,0:T(2,128)(2,1)}, bf16[384]{0:T(512)(128)(2,1)}, bf16[192]{0:T(256)(128)(2,1)}, bf16[768]{0:T(10...) all-reduce(bf16[2,192]{1,0:T(2,128)(2,1)} %copy.175, ...), channel_id=1, replica_groups=mesh['items'=8,'rows'=4] {'items'}, use_global_device_ids=true, to_apply=%region_15.16 | all-reduce | flops 3648 | bytes 14592 | tf_op jit(solution)/shard_map/psum | solution.py:391
  1169.0 70.6 %all-reduce.18.cloned.1.call-done = (bf16[192,2304]{1,0:T(8,128)(2,1)}, bf16[192,768]{1,0:T(8,128)(2,1)}, bf16[192,3072]{1,0:T(8,128)(2,1)}, bf16[768,768]{1,0:T...) async-done(((bf16[192,2304]{1,0:T(8,128)(2,1)}, bf16[192,768]{1,0:T(8,128)(2,1)}, bf16[192,3072]{1,0:T(8,128)(2,1)}, bf16[768,768]{1,0:T(8,128)(2,1)}, ...) | async-done | bytes 4816912 | tf_op jit(solution)/shard_map/psum | solution.py:393
  (563 shorter events, 450.5 us)
Async XLA Ops:
  7.2 88.0 %all-gather.5.cloned.1.call-start = ((), (), s32[]{:S(2)}) async-start(), calls=%async_computation.14 | async-start | bytes 7372800 | tf_op jit(solution)/shard_map/all_gather | solution.py:172
  25.5 139.1 %all-gather.3.cloned.1.call-start = ((), (), s32[]{:S(2)}) async-start(), calls=%async_computation.13 | async-start | bytes 7372800 | tf_op jit(solution)/shard_map/all_gather | solution.py:173
  26.2 675.8 %reduce-scatter.26.cloned.1.call-start = ((), (), s32[]{:S(2)}) async-start(), calls=%async_computation.16 | async-start | bytes 7372800 | tf_op jit(solution)/shard_map/reduce_scatter | solution.py:359
  271.9 8.0 collective-permute-start.2
  307.2 6.4 collective-permute-start.7
  357.2 8.4 collective-permute-start.12
  360.8 6.4 collective-permute-start.13
  376.4 8.4 collective-permute-start.14
  380.1 6.4 collective-permute-start.15
  397.7 8.4 collective-permute-start.16
  416.9 8.5 collective-permute-start.18
  561.8 142.8 %reduce-scatter.24.cloned.1.call-start = ((), (), s32[]{:S(2)}) async-start(), calls=%async_computation.15 | async-start | bytes 7372800 | tf_op jit(solution)/shard_map/reduce_scatter | solution.py:353
  635.4 108.2 %reduce-scatter.36.cloned.1.call-start = ((), (), s32[]{:S(2)}) async-start(), calls=%async_computation.21 | async-start | bytes 491520 | tf_op jit(solution)/shard_map/reduce_scatter | solution.py:439
  638.3 122.5 %reduce-scatter.30.cloned.1.call-start = ((), (), s32[]{:S(2)}) async-start(), calls=%async_computation.18 | async-start | bytes 1474560 | tf_op jit(solution)/shard_map/reduce_scatter | solution.py:421
  645.8 175.1 %reduce-scatter.38.cloned.1.call-start = ((), (), s32[]{:S(2)}) async-start(), calls=%async_computation.22 | async-start | bytes 5898240 | tf_op jit(solution)/shard_map/reduce_scatter | solution.py:445
  658.0 223.1 %reduce-scatter.34.cloned.1.call-start = ((), (), s32[]{:S(2)}) async-start(), calls=%async_computation.20 | async-start | bytes 5898240 | tf_op jit(solution)/shard_map/reduce_scatter | solution.py:433
  667.1 274.1 %reduce-scatter.32.cloned.1.call-start = ((), (), s32[]{:S(2)}) async-start(), calls=%async_computation.19 | async-start | bytes 5898240 | tf_op jit(solution)/shard_map/reduce_scatter | solution.py:427
  678.2 313.3 %reduce-scatter.28.cloned.1.call-start = ((), (), s32[]{:S(2)}) async-start(), calls=%async_computation.17 | async-start | bytes 4423680 | tf_op jit(solution)/shard_map/reduce_scatter | solution.py:415
  715.8 302.1 %reduce-scatter.46.cloned.1.call-start = ((), (), s32[]{:S(2)}) async-start(), calls=%async_computation.26 | async-start | bytes 81920
  718.8 325.5 %reduce-scatter.48.cloned.1.call-start = ((), (), s32[]{:S(2)}) async-start(), calls=%async_computation.27 | async-start | bytes 81920
  721.9 348.9 %reduce-scatter.44.cloned.1.call-start = ((), (), s32[]{:S(2)}) async-start(), calls=%async_computation.25 | async-start | bytes 81920
  727.3 382.0 %reduce-scatter.40.cloned.1.call-start = ((), (), s32[]{:S(2)}) async-start(), calls=%async_computation.23 | async-start | bytes 245760
  740.6 385.1 %reduce-scatter.42.cloned.1.call-start = ((), (), s32[]{:S(2)}) async-start(), calls=%async_computation.24 | async-start | bytes 245760
  743.5 496.2 %all-reduce.18.cloned.1.call-start = ((), (), s32[]{:S(2)}) async-start(), calls=%async_computation.28 | async-start | bytes 9633792 | tf_op jit(solution)/shard_map/psum | solution.py:393
  (126 other events, 1324.0 us)
Sparse Core Ops, SparseCore 0:
  25.6 69.5 all-gather.4
  97.6 66.8 all-gather.2
  561.9 66.7 reduce-scatter.25
  635.5 66.2 reduce-scatter.23
  704.4 24.4 reduce-scatter.35
  732.2 28.5 reduce-scatter.29
  763.8 57.0 reduce-scatter.37
  823.9 57.0 reduce-scatter.33
  884.1 57.0 reduce-scatter.31
  944.1 47.2 reduce-scatter.27
  994.2 23.6 reduce-scatter.45
  1020.6 23.6 reduce-scatter.47
  1047.1 23.6 reduce-scatter.43
  1074.2 23.9 reduce-scatter.39
  1101.7 23.9 reduce-scatter.41
  1128.6 110.9 all-reduce.17
where the time goes:
time: 1260 us
  waiting for transfers between devices  500 us (40%)
  matrix products  315 us (25%)
  other arithmetic  172 us (14%)
  local copies, waits for them, and re-layouts  157 us (12%)
  starting transfers between devices  48.5 us (4%)
  blocking collectives  45.7 us (4%)
  between operations  19.1 us (2%)
    unnamed x21, waiting for transfers between devices  85.1 us
    psum x1, waiting for transfers between devices, shards(): lax.psum(grad_qkv_weight.astype(jnp.bfloat16), 'items').astype(jnp.float32)  70.6 us
    reduce_scatter x1, waiting for transfers between devices, shards(): lax.psum_scatter(summed[6].astype(jnp.bfloat16), 'rows', scatter_dimensio...  60.1 us
    reduce_scatter x1, waiting for transfers between devices, shards(): lax.psum_scatter(summed[8].astype(jnp.bfloat16), 'rows', scatter_dimensio...  60.1 us
    reduce_scatter x1, waiting for transfers between devices, shards(): lax.psum_scatter(summed[12].astype(jnp.bfloat16), 'rows', scatter_dimensi...  60.1 us
    all_gather x1, waiting for transfers between devices, fold_keys(): lax.all_gather(key_rows, 'rows', axis=1, tiled=True)  55.4 us
    reduce_scatter x1, waiting for transfers between devices, shards(): lax.psum_scatter(summed[2].astype(jnp.bfloat16), 'rows', scatter_dimensio...  50.2 us
    convert_element_type x1, other arithmetic, shards(): (probs * (grad_probs - row_dots[..., None])).astype(jnp.bfloat16)  49.3 us
  transfers between devices with their start and end apart: 36, of which 24 were waited for; matrix products, arithmetic and copies ran while one was open for 25% of the time, Pallas kernels for 0%

commit v1 on v0

v1 whole, which is shorter than its diff:
```python
import functools

import jax
import jax.numpy as jnp
from jax import lax
from jax.experimental import pallas as pl
from jax.experimental.pallas import tpu as pltpu
from jax.sharding import PartitionSpec as P

HEAD_DIM = 64
PC = 40
GROUP = 256
HEADS_PER_GROUP = GROUP // HEAD_DIM

BF = jnp.bfloat16
F32 = jnp.float32
LOG2E = 1.4426950408889634
MASKED = -1e30
NN = (((1,), (0,)), ((), ()))
NT = (((1,), (1,)), ((), ()))
TN = (((0,), (0,)), ((), ()))

epsilon = 1e-06
highest = lax.Precision.HIGHEST


def mm(left, right, dims=NN):
    return lax.dot_general(left, right, dims, preferred_element_type=F32)


def normal_parts(values):
    bell = jnp.exp2(values * values * (-0.5 * LOG2E))
    t = 1.0 / (1.0 + (0.3275911 * 0.7071067811865476) * jnp.abs(values))
    poly = t * (
        0.5 * 0.254829592
        + t
        * (
            0.5 * -0.284496736
            + t * (0.5 * 1.421413741 + t * (0.5 * -1.453152027 + t * (0.5 * 1.061405429)))
        )
    )
    tail = poly * bell
    cdf = jnp.where(values >= 0.0, 1.0 - tail, tail)
    return cdf, values * bell * 0.3989422804014327


def gelu_exact(values):
    return values * normal_parts(values)[0]


def gelu_slope(values):
    cdf, slope = normal_parts(values)
    return cdf + slope


def gelu_back(values, grad_out):
    return gelu_slope(values) * grad_out


def norm_stats(values):
    centre = jnp.mean(values, axis=-1, keepdims=True)
    centred = values - centre
    spread = jnp.mean(centred * centred, axis=-1, keepdims=True)
    rstd = lax.rsqrt(spread + epsilon)
    return centred * rstd, rstd


def layer_norm(values, gain, shift):
    return norm_stats(values)[0] * gain + shift


def norm_back(values, gain, grad_out):
    unit, rstd = norm_stats(values)
    scaled = grad_out * gain
    mean_one = jnp.mean(scaled, axis=-1, keepdims=True)
    mean_two = jnp.mean(scaled * unit, axis=-1, keepdims=True)
    result = rstd * (scaled - mean_one - unit * mean_two)
    return result, jnp.sum(grad_out * unit, axis=0), jnp.sum(grad_out, axis=0)


def swap(block, axis, mask):
    count = lax.axis_size(axis)
    return lax.ppermute(block, axis, [(i, i ^ mask) for i in range(count)])


def axis_bits(axis):
    return (lax.axis_size(axis) - 1).bit_length()


def gather_blocks(block):
    bits = axis_bits("rows")
    half = block.shape[0] // 2
    halves = []
    for order, part in (
        (range(bits), block[:half]),
        (range(bits - 1, -1, -1), block[half:]),
    ):
        held = {0: part}
        for bit in order:
            keys = sorted(held)
            sent = jnp.concatenate([held[key] for key in keys]) if len(keys) > 1 else held[keys[0]]
            got = swap(sent, "rows", 1 << bit)
            for place, key in enumerate(keys):
                held[key | (1 << bit)] = got[place * half : (place + 1) * half]
        halves.append(held)
    blocks = []
    for j in range(1 << bits):
        blocks += [halves[0][j], halves[1][j]]
    return jnp.concatenate(blocks)


def scatter_blocks(whole):
    bits = axis_bits("rows")
    count = 1 << bits
    block = whole.shape[0] // count
    half = block // 2
    results = []
    for which, order in ((0, range(bits - 1, -1, -1)), (1, range(bits))):
        held = {
            j: whole[j * block + which * half : j * block + (which + 1) * half]
            for j in range(count)
        }
        for bit in order:
            sent_keys = sorted(key for key in held if key >> bit & 1)
            sent = (
                jnp.concatenate([held[key] for key in sent_keys])
                if len(sent_keys) > 1
                else held[sent_keys[0]]
            )
            got = swap(sent, "rows", 1 << bit)
            held = {
                key ^ (1 << bit): held[key ^ (1 << bit)].astype(F32)
                + got[place * half : (place + 1) * half].astype(F32)
                for place, key in enumerate(sent_keys)
            }
            if len(held) > 1:
                held = {key: value.astype(BF) for key, value in held.items()}
        results.append(held[0])
    return jnp.concatenate(results)


def add_low(first, second):
    return (first.astype(F32) + second.astype(F32)).astype(BF)


def head_mask(shape, head):
    lane = lax.broadcasted_iota(jnp.int32, shape, 1)
    return lane // HEAD_DIM == head


def spread_heads(block):
    zero = jnp.zeros_like(block)
    return jnp.concatenate(
        [jnp.where(head_mask(block.shape, h), block, zero) for h in range(HEADS_PER_GROUP)],
        axis=0,
    )


def key_bias(index, dim, length, block, info_ref):
    start = jnp.full_like(index, info_ref[1])
    for j in range(1, length // block):
        start = jnp.where(index >= j * block, info_ref[1 + j] - j * block, start)
    return jnp.where(index + start < info_ref[0], 0.0, MASKED).astype(F32)


def attention_forward_kernel(info_ref, q_ref, k_ref, v_ref, o_ref, lse_ref):
    t, n = q_ref.shape[0], k_ref.shape[0]
    bias = key_bias(lax.broadcasted_iota(jnp.int32, (1, n), 1), 1, n, t, info_ref)
    keys, values = k_ref[...], v_ref[...]
    queries = q_ref[...] * jnp.asarray(HEAD_DIM**-0.5, BF)
    out = jnp.zeros((t, GROUP), F32)
    for h in range(HEADS_PER_GROUP):
        mask = head_mask((t, GROUP), h)
        one = jnp.where(mask, queries, jnp.zeros_like(queries))
        scores = mm(one, keys, NT) + bias
        top = jnp.max(scores, axis=1, keepdims=True)
        probs = jnp.exp2((scores - top) * LOG2E)
        total = jnp.sum(probs, axis=1, keepdims=True)
        weighted = mm(probs.astype(BF), values)
        out = jnp.where(mask, weighted * (1.0 / total), out)
        lse = top * LOG2E + jnp.log2(total)
        lse_ref[0, :, pl.ds(h * t, t)] = jnp.transpose(jnp.broadcast_to(lse, (t, 128)))[:8]
    o_ref[...] = out.astype(BF)


def attention_forward(info, queries, keyvals):
    t, d = queries.shape
    n = keyvals.shape[0]
    groups = d // GROUP
    return pl.pallas_call(
        attention_forward_kernel,
        grid=(groups,),
        in_specs=[
            pl.BlockSpec(memory_space=pltpu.SMEM),
            pl.BlockSpec((t, GROUP), lambda i: (0, i)),
            pl.BlockSpec((n, GROUP), lambda i: (0, i)),
            pl.BlockSpec((n, GROUP), lambda i: (0, i + groups)),
        ],
        out_specs=[
            pl.BlockSpec((t, GROUP), lambda i: (0, i)),
            pl.BlockSpec((1, 8, HEADS_PER_GROUP * t), lambda i: (i, 0, 0)),
        ],
        out_shape=[
            jax.ShapeDtypeStruct((t, d), BF),
            jax.ShapeDtypeStruct((groups, 8, HEADS_PER_GROUP * t), F32),
        ],
        compiler_params=pltpu.CompilerParams(vmem_limit_bytes=40 << 20),
        cost_estimate=pl.CostEstimate(
            flops=16 * t * n * d, bytes_accessed=4 * t * d + 4 * n * d, transcendentals=12 * t * n
        ),
        name="attention_forward",
    )(info, queries, keyvals, keyvals)


def attention_backward_kernel(
    info_ref, q_ref, k_ref, v_ref, g_ref, o_ref, lse_ref, dq_ref, dk_ref, dv_ref, q4, g4, acc, *, kb
):
    t, n = q_ref.shape[0], k_ref.shape[0]
    q4[...] = spread_heads(q_ref[...] * jnp.asarray(HEAD_DIM**-0.5, BF))
    grads = spread_heads(g_ref[...])
    g4[...] = grads
    outs = jnp.concatenate([o_ref[...].astype(F32)] * HEADS_PER_GROUP, axis=0)
    product = grads.astype(F32) * outs
    high = product.astype(BF)
    low = (product - high.astype(F32)).astype(BF)
    ones = jnp.ones((8, GROUP), BF)
    dots = (mm(ones, high, NT) + mm(ones, low, NT))[:1]
    lse = lse_ref[0, :1, :]
    acc[...] = jnp.zeros_like(acc)

    def step(b, carry):
        at = pl.ds(pl.multiple_of(b * kb, kb), kb)
        keys, values = k_ref[at, :], v_ref[at, :]
        index = b * kb + lax.broadcasted_iota(jnp.int32, (kb, 1), 0)
        bias = key_bias(index, 0, n, t, info_ref)
        scores = mm(keys, q4[...], NT)
        probs = jnp.exp2((scores * LOG2E + bias) - lse)
        grad_probs = mm(values, g4[...], NT)
        grad_scores = (probs * (grad_probs - dots)).astype(BF)
        dv_ref[at, :] = mm(probs.astype(BF), g4[...]).astype(BF)
        dk_ref[at, :] = mm(grad_scores, q4[...]).astype(BF)
        acc[...] += mm(grad_scores, keys, TN)
        return carry

    lax.fori_loop(0, n // kb, step, 0)
    out = jnp.zeros((t, GROUP), F32)
    for h in range(HEADS_PER_GROUP):
        out = jnp.where(head_mask((t, GROUP), h), acc[pl.ds(h * t, t), :], out)
    dq_ref[...] = (out * HEAD_DIM**-0.5).astype(BF)


def attention_backward(info, queries, keyvals, grads, outs, lse):
    t, d = queries.shape
    n = keyvals.shape[0]
    groups = d // GROUP
    rows4 = HEADS_PER_GROUP * t
    query_spec = pl.BlockSpec((t, GROUP), lambda i: (0, i))
    key_spec = pl.BlockSpec((n, GROUP), lambda i: (0, i))
    return pl.pallas_call(
        functools.partial(attention_backward_kernel, kb=n // 2),
        grid=(groups,),
        in_specs=[
            pl.BlockSpec(memory_space=pltpu.SMEM),
            query_spec,
            key_spec,
            pl.BlockSpec((n, GROUP), lambda i: (0, i + groups)),
            query_spec,
            query_spec,
            pl.BlockSpec((1, 8, rows4), lambda i: (i, 0, 0)),
        ],
        out_specs=[query_spec, key_spec, key_spec],
        out_shape=[
            jax.ShapeDtypeStruct((t, d), BF),
            jax.ShapeDtypeStruct((n, d), BF),
            jax.ShapeDtypeStruct((n, d), BF),
        ],
        scratch_shapes=[
            pltpu.VMEM((rows4, GROUP), BF),
            pltpu.VMEM((rows4, GROUP), BF),
            pltpu.VMEM((rows4, GROUP), F32),
        ],
        compiler_params=pltpu.CompilerParams(vmem_limit_bytes=48 << 20),
        cost_estimate=pl.CostEstimate(
            flops=40 * t * n * d, bytes_accessed=8 * t * d + 8 * n * d, transcendentals=12 * t * n
        ),
        name="attention_backward",
    )(info, queries, keyvals, keyvals, grads, outs, lse)


WIDE = 48
EDGES = 10
FIELD_EDGE, TALL_EDGE = 4, 5


def refine_kernel(
    field_ref,
    weight_ref,
    bias_ref,
    factor_ref,
    offset_ref,
    cot_ref,
    joined_ref,
    grad_ref,
    dw_ref,
    db_ref,
    sums_ref,
    acts,
    slopes,
    grads3,
    work,
    frame,
    tall,
    lane2,
    edge,
    halo,
    send_sem,
    recv_sem,
    *,
    items,
    rows,
    count,
):
    me = lax.axis_index("rows")
    here = lax.axis_index("items")
    channels = field_ref.shape[-1]
    flat = items * rows * WIDE
    lanes = channels // 128
    column = lax.broadcasted_iota(jnp.int32, (WIDE, channels), 0)
    inside = column < PC

    barrier = pltpu.get_barrier_semaphore()
    for step in (-1, 1):

        @pl.when((me + step >= 0) & (me + step < count))
        def _():
            pl.semaphore_signal(
                barrier, inc=1, device_id=(here, me + step), device_id_type=pl.DeviceIdType.MESH
            )

    @pl.when((me > 0) & (me < count - 1))
    def _():
        pl.semaphore_wait(barrier, 2)

    @pl.when((me == 0) | (me == count - 1))
    def _():
        pl.semaphore_wait(barrier, 1)

    def each(side):
        return (me > 0) if side == 0 else (me < count - 1)

    def copy(e, side):
        return pltpu.make_async_remote_copy(
            src_ref=edge.at[e, side],
            dst_ref=halo.at[e, 1 - side],
            send_sem=send_sem.at[e, side],
            recv_sem=recv_sem.at[e, 1 - side],
            device_id=(here, me + (2 * side - 1)),
            device_id_type=pl.DeviceIdType.MESH,
        )

    def send(e):
        for side in (0, 1):

            @pl.when(each(side))
            def _():
                copy(e, side).start()

    def receive(e):
        for side in (0, 1):

            @pl.when(each(side))
            def _():
                pltpu.make_async_remote_copy(
                    src_ref=edge.at[e, side],
                    dst_ref=halo.at[e, side],
                    send_sem=send_sem.at[e, side],
                    recv_sem=recv_sem.at[e, side],
                    device_id=(here, me + (2 * side - 1)),
                    device_id_type=pl.DeviceIdType.MESH,
                ).wait_recv()

            @pl.when(jnp.logical_not(each(side)))
            def _():
                halo[e, side] = jnp.zeros(halo.shape[2:], BF)

    def shifted(values, flip):
        before = pltpu.roll(values, 1, 0)
        after = pltpu.roll(values, WIDE - 1, 0)
        parts = [after, values, before] if flip else [before, values, after]
        return jnp.concatenate([part.astype(BF) for part in parts], axis=1)

    def all_rows(body, e):
        for item in range(items):
            for row, side in ((0, 0), (rows - 1, 1)):
                body(item, row, (e, side))
        send(e)

        def step(row, carry):
            for item in range(items):
                body(item, row, None)
            return carry

        lax.fori_loop(1, rows - 1, step, 0)

    def spread_halo(target, e, flip):
        for side, row in ((0, 0), (1, rows + 1)):
            for item in range(items):
                target[item, row] = shifted(halo[e, side, item].astype(F32), flip)

    for item in range(items):
        factor = factor_ref[pl.ds(item, 1), :]

        def back(row, carry, item=item, factor=factor):
            whole = cot_ref[item, row].astype(F32) * factor
            for part in range(lanes):
                lane2[part, pl.ds(0, 2 * PC), :] = whole[:, part * 128 : (part + 1) * 128]
            even, odd = (
                jnp.concatenate(
                    [lane2[part, pl.ds(start, PC, stride=2), :] for part in range(lanes)], axis=1
                )
                for start in (0, 1)
            )
            place = lax.broadcasted_iota(jnp.int32, (PC, channels), 0)
            even_next = jnp.where(place == PC - 1, odd, pltpu.roll(even, PC - 1, 0))
            odd_prev = jnp.where(place == 0, even, pltpu.roll(odd, 1, 0))
            tall[item, row + 1, pl.ds(0, PC), :] = 0.75 * (even + odd) + 0.25 * (
                even_next + odd_prev
            )
            tall[item, row + 1, pl.ds(PC, WIDE - PC), :] = jnp.zeros((WIDE - PC, channels), F32)
            return carry

        lax.fori_loop(0, 2 * rows, back, 0)
        edge[TALL_EDGE, 0, item] = tall[item, 1].astype(BF)
        edge[TALL_EDGE, 1, item] = tall[item, 2 * rows].astype(BF)
    send(TALL_EDGE)

    def activate(source, which):
        def body(item, row, out):
            values = source[item, row]
            cdf, rest = normal_parts(values)
            act = jnp.where(inside, values * cdf, 0.0)
            slopes[which, item, row] = cdf + rest
            acts[which, item, row + 1] = shifted(act, False)
            if out is not None:
                edge[out[0], out[1], item] = act.astype(BF)

        all_rows(body, which)

    def weight_of(conv, kr):
        return weight_ref[conv, pl.ds(kr * 3 * channels, 3 * channels), :]

    def lhs(source, item, first, number):
        return source[item, pl.ds(first, number)].reshape(number * WIDE, -1)

    def forward(conv, add):
        bias = bias_ref[pl.ds(conv, 1), :]
        for item in range(items):
            centre = mm(lhs(acts.at[conv], item, 1, rows), weight_of(conv, 1)) + bias
            if add:
                centre = centre + frame[item, pl.ds(1, rows)].reshape(rows * WIDE, channels)
            work[item] = centre.reshape(rows, WIDE, channels)
            upper = mm(lhs(acts.at[conv], item, 1, rows - 1), weight_of(conv, 0))
            work[item, pl.ds(1, rows - 1)] += upper.reshape(rows - 1, WIDE, channels)
            lower = mm(lhs(acts.at[conv], item, 2, rows - 1), weight_of(conv, 2))
            work[item, pl.ds(0, rows - 1)] += lower.reshape(rows - 1, WIDE, channels)
        receive(conv)
        spread_halo(acts.at[conv], conv, False)
        for kr, source, row in ((0, 0, 0), (2, rows + 1, rows - 1)):
            block = jnp.concatenate([acts[conv, item, source] for item in range(items)], axis=0)
            extra = mm(block, weight_of(conv, kr))
            for item in range(items):
                work[item, row] += extra[item * WIDE : (item + 1) * WIDE]

    def keep_field(source):
        for item in range(items):
            frame[item, pl.ds(1, rows)] = source[item]

    keep_field(field_ref)
    for unit in (0, 1):
        activate(field_ref if unit == 0 else work, 2 * unit)
        forward(2 * unit, False)
        activate(work, 2 * unit + 1)
        forward(2 * unit + 1, True)
        keep_field(work)

    for item in range(items):
        edge[FIELD_EDGE, 0, item] = frame[item, 1].astype(BF)
        edge[FIELD_EDGE, 1, item] = frame[item, rows].astype(BF)
    send(FIELD_EDGE)

    receive(TALL_EDGE)
    for item in range(items):
        tall[item, 0] = jnp.where(me == 0, tall[item, 1], halo[TALL_EDGE, 0, item].astype(F32))
        tall[item, 2 * rows + 1] = jnp.where(
            me == count - 1, tall[item, 2 * rows], halo[TALL_EDGE, 1, item].astype(F32)
        )

        def fold(row, carry, item=item):
            grad_ref[item, row] = 0.75 * (
                tall[item, 2 * row + 1] + tall[item, 2 * row + 2]
            ) + 0.25 * (tall[item, 2 * row] + tall[item, 2 * row + 3])
            return carry

        lax.fori_loop(0, rows, fold, 0)

    receive(FIELD_EDGE)
    for item in range(items):
        frame[item, 0] = jnp.where(me == 0, frame[item, 1], halo[FIELD_EDGE, 0, item].astype(F32))
        frame[item, rows + 1] = jnp.where(
            me == count - 1, frame[item, rows], halo[FIELD_EDGE, 1, item].astype(F32)
        )
        factor = factor_ref[pl.ds(item, 1), :]
        offset = offset_ref[pl.ds(item, 1), :]

        def widen(row, carry, item=item, factor=factor, offset=offset):
            gain_sum, shift_sum = carry
            centre = frame[item, row + 1]
            for half in (0, 1):
                line = 0.75 * centre + 0.25 * frame[item, row + 2 * half]
                before = jnp.where(column == 0, line, pltpu.roll(line, 1, 0))
                after = jnp.where(column == PC - 1, line, pltpu.roll(line, WIDE - 1, 0))
                for start, side in ((0, before), (1, after)):
                    mixed = 0.75 * line + 0.25 * side
                    for part in range(lanes):
                        lane2[part, pl.ds(start, WIDE, stride=2), :] = mixed[
                            :, part * 128 : (part + 1) * 128
                        ]
                wide = jnp.concatenate(
                    [lane2[part, pl.ds(0, 2 * PC), :] for part in range(lanes)], axis=1
                )
                joined_ref[item, 2 * row + half] = (wide * factor + offset).astype(BF)
                cot = cot_ref[item, 2 * row + half].astype(F32)
                gain_sum = gain_sum + jnp.sum((cot * wide).reshape(-1, 8, channels), axis=0)
                shift_sum = shift_sum + jnp.sum(cot.reshape(-1, 8, channels), axis=0)
            return gain_sum, shift_sum

        zero = jnp.zeros((8, channels), F32)
        gain_sum, shift_sum = lax.fori_loop(0, rows, widen, (zero, zero))
        sums_ref[0, pl.ds(item, 1), :] = jnp.sum(gain_sum, axis=0, keepdims=True)
        sums_ref[1, pl.ds(item, 1), :] = jnp.sum(shift_sum, axis=0, keepdims=True)

    def grad_pass(conv, make):
        e = 6 + conv

        def body(item, row, out):
            values = jnp.where(inside, make(item, row), 0.0).astype(BF).astype(F32)
            grads3[item, row + 1] = shifted(values, True)
            if out is not None:
                edge[out[0], out[1], item] = values.astype(BF)

        all_rows(body, e)
        middle = jnp.concatenate(
            [
                grads3[item, pl.ds(1, rows), :, pl.ds(channels, channels)].reshape(
                    rows * WIDE, channels
                )
                for item in range(items)
            ],
            axis=0,
        )
        for kr in range(3):
            block = jnp.concatenate(
                [lhs(acts.at[conv], item, kr, rows) for item in range(items)], axis=0
            )
            dw_ref[conv, pl.ds(kr * 3 * channels, 3 * channels), :] = mm(block, middle, TN).astype(BF)
        ones = jnp.ones((8, flat), BF)
        db_ref[pl.ds(conv, 1), :] = mm(ones, middle)[:1]

        def product(block, kr):
            total = None
            for kc in range(3):
                part = mm(
                    block[:, kc * channels : (kc + 1) * channels],
                    weight_ref[conv, pl.ds((kr * 3 + kc) * channels, channels), :],
                    NT,
                )
                total = part if total is None else total + part
            return total

        for item in range(items):
            work[item] = product(lhs(grads3, item, 1, rows), 1).reshape(rows, WIDE, channels)
            work[item, pl.ds(1, rows - 1)] += product(lhs(grads3, item, 1, rows - 1), 2).reshape(
                rows - 1, WIDE, channels
            )
            work[item, pl.ds(0, rows - 1)] += product(lhs(grads3, item, 2, rows - 1), 0).reshape(
                rows - 1, WIDE, channels
            )
        receive(e)
        spread_halo(grads3, e, True)
        for kr, source, row in ((2, 0, 0), (0, rows + 1, rows - 1)):
            block = jnp.concatenate([grads3[item, source] for item in range(items)], axis=0)
            extra = product(block, kr)
            for item in range(items):
                work[item, row] += extra[item * WIDE : (item + 1) * WIDE]

    for unit in (1, 0):
        first, second = 2 * unit, 2 * unit + 1
        grad_pass(second, lambda item, row: grad_ref[item, row])
        grad_pass(first, lambda item, row: work[item, row] * slopes[second, item, row])

        def gather(row, carry, first=first):
            for item in range(items):
                grad_ref[item, row] += work[item, row] * slopes[first, item, row]
            return carry

        lax.fori_loop(0, rows, gather, 0)

    for e in range(EDGES):
        for side in (0, 1):

            @pl.when(each(side))
            def _():
                copy(e, side).wait_send()


def refine(field, conv_weights, conv_biases, factor, offset, cotangent):
    items, rows, _, channels = field.shape
    count = lax.axis_size("rows")
    padded = jnp.pad(field, ((0, 0), (0, 0), (0, WIDE - PC), (0, 0)))
    vmem = pl.BlockSpec(memory_space=pltpu.VMEM)
    pixels = items * rows * PC
    outs = pl.pallas_call(
        functools.partial(refine_kernel, items=items, rows=rows, count=count),
        in_specs=[vmem] * 6,
        out_specs=[vmem] * 5,
        out_shape=[
            jax.ShapeDtypeStruct((items, 2 * rows, 2 * PC, channels), BF),
            jax.ShapeDtypeStruct((items, rows, WIDE, channels), F32),
            jax.ShapeDtypeStruct(conv_weights.shape, BF),
            jax.ShapeDtypeStruct(conv_biases.shape, F32),
            jax.ShapeDtypeStruct((2, items, channels), F32),
        ],
        scratch_shapes=[
            pltpu.VMEM((4, items, rows + 2, WIDE, 3 * channels), BF),
            pltpu.VMEM((4, items, rows, WIDE, channels), F32),
            pltpu.VMEM((items, rows + 2, WIDE, 3 * channels), BF),
            pltpu.VMEM((items, rows, WIDE, channels), F32),
            pltpu.VMEM((items, rows + 2, WIDE, channels), F32),
            pltpu.VMEM((items, 2 * rows + 2, WIDE, channels), F32),
            pltpu.VMEM((channels // 128, 2 * WIDE, 128), F32),
            pltpu.VMEM((EDGES, 2, items, WIDE, channels), BF),
            pltpu.VMEM((EDGES, 2, items, WIDE, channels), BF),
            pltpu.SemaphoreType.DMA((EDGES, 2)),
            pltpu.SemaphoreType.DMA((EDGES, 2)),
        ],
        compiler_params=pltpu.CompilerParams(
            vmem_limit_bytes=56 << 20, collective_id=0, has_side_effects=True
        ),
        cost_estimate=pl.CostEstimate(
            flops=2 * 12 * pixels * 9 * channels * channels,
            bytes_accessed=20 << 20,
            transcendentals=8 * pixels * channels,
        ),
        name="refine",
    )(padded, conv_weights, conv_biases, factor, offset, cotangent)
    return outs


MESH = pl.DeviceIdType.MESH
STRIP = 256
LAG = 3


def flip(index, bit):
    return index + (1 - 2 * (index // (1 << bit) % 2)) * (1 << bit)


class Reducer:
    def __init__(self, chunks, depth, row_bits, item_bits):
        self.chunks, self.depth = chunks, depth
        self.row_bits, self.item_bits = row_bits, item_bits
        self.orders = (tuple(range(row_bits - 1, -1, -1)), tuple(range(row_bits)))
        self.far = max(item_bits - 2, 0)
        self.phases = 1 + row_bits + 1 + self.far + 1 + 1

    def scratch(self):
        c, half = self.chunks, self.depth // 2
        shares = (2,) * self.row_bits
        slots = [
            pltpu.VMEM((c,) + shares + (self.depth, 128), BF),
            pltpu.VMEM((c,) + shares + (self.depth, 128), BF),
        ]
        for stage in range(self.row_bits):
            for _ in (0, 1):
                slots.append(pltpu.VMEM((c,) + (2,) * (self.row_bits - 1 - stage) + (half, 128), BF))
        slots.append(pltpu.VMEM((c, half, 128), BF))
        for _ in range(self.far):
            slots.append(pltpu.VMEM((c, half, 128), BF))
            slots.append(pltpu.VMEM((c, half, 128), BF))
        arrivals = 1 + 1 + 2 * self.row_bits + 1 + self.far + 1 + 1
        sends = 1 + 2 * self.row_bits + 1 + self.far + 1 + 1
        return slots + [pltpu.SemaphoreType.DMA((arrivals, c)), pltpu.SemaphoreType.DMA((sends,))]

    def out_shape(self):
        return jax.ShapeDtypeStruct((2, self.chunks, self.depth, 128), BF)

    def bind(self, out_ref, slots):
        slots = list(slots)
        self.out = out_ref
        self.mine, self.core_in = slots[0], slots[1]
        self.row_in = [
            (slots[2 + 2 * stage], slots[3 + 2 * stage]) for stage in range(self.row_bits)
        ]
        rest = slots[2 + 2 * self.row_bits :]
        self.near_in = rest[0]
        self.far_out = [rest[1 + 2 * k] for k in range(self.far)]
        self.far_in = [rest[2 + 2 * k] for k in range(self.far)]
        self.recv_sem, self.send_sem = rest[-2], rest[-1]
        self.me = lax.axis_index("rows")
        self.at = lax.axis_index("items")
        self.core = self.at % 2
        self.near = self.at // 2 % 2

    def peers(self):
        found = [(flip(self.at, bit), self.me) for bit in range(self.item_bits)]
        return found + [(self.at, flip(self.me, bit)) for bit in range(self.row_bits)]

    def greet(self):
        barrier = pltpu.get_barrier_semaphore()
        for peer in self.peers():
            pl.semaphore_signal(barrier, inc=1, device_id=peer, device_id_type=MESH)
        pl.semaphore_wait(barrier, len(self.peers()))

    def remote(self, source, target, arrival, sent, chunk, peer):
        return pltpu.make_async_remote_copy(
            src_ref=source,
            dst_ref=target,
            send_sem=self.send_sem.at[sent],
            recv_sem=self.recv_sem.at[arrival, chunk],
            device_id=peer,
            device_id_type=MESH,
        )

    def first(self, view, column, chunk):
        lead = (slice(None),) * (self.row_bits + 1)
        theirs = view.at[lead + (pl.ds(pl.multiple_of(column + (1 - self.core) * 128, 128), 128),)]
        ours = view.at[lead + (pl.ds(pl.multiple_of(column + self.core * 128, 128), 128),)]
        self.remote(
            theirs, self.core_in.at[chunk], 0, 0, chunk, (flip(self.at, 0), self.me)
        ).start()
        pltpu.make_async_copy(ours, self.mine.at[chunk], self.recv_sem.at[1, chunk]).start()

    def bit(self, which):
        return self.me // (1 << which) % 2

    def shares(self, half, stage, sent):
        order = self.orders[half]
        index = [slice(None)] * self.row_bits
        for done in order[:stage]:
            index[self.row_bits - 1 - done] = self.bit(done)
        now = order[stage]
        index[self.row_bits - 1 - now] = 1 - self.bit(now) if sent else self.bit(now)
        return tuple(index)

    def rows(self, half):
        depth = self.depth // 2
        return pl.ds(half * depth, depth)

    def row_copy(self, stage, half, chunk):
        source = self.mine.at[(chunk,) + self.shares(half, stage, True) + (self.rows(half),)]
        return self.remote(
            source,
            self.row_in[stage][half].at[chunk],
            2 + 2 * stage + half,
            1 + 2 * stage + half,
            chunk,
            (self.at, flip(self.me, self.orders[half][stage])),
        )

    def own(self, chunk, rows):
        return (chunk,) + tuple(self.bit(b) for b in range(self.row_bits - 1, -1, -1)) + (rows,)

    def near_rows(self, mine):
        half = self.depth // 2
        place = self.near if mine else 1 - self.near
        return pl.ds(pl.multiple_of(place * half, half), half)

    def near_copy(self, chunk):
        return self.remote(
            self.mine.at[self.own(chunk, self.near_rows(False))],
            self.near_in.at[chunk],
            2 + 2 * self.row_bits,
            1 + 2 * self.row_bits,
            chunk,
            (flip(self.at, 1), self.me),
        )

    def far_copy(self, k, chunk):
        return self.remote(
            self.far_out[k].at[chunk],
            self.far_in[k].at[chunk],
            3 + 2 * self.row_bits + k,
            2 + 2 * self.row_bits + k,
            chunk,
            (flip(self.at, 2 + k), self.me),
        )

    def back_copy(self, chunk):
        place = self.out.at[self.core, chunk, self.near_rows(True)]
        return self.remote(
            place,
            place,
            3 + 2 * self.row_bits + self.far,
            2 + 2 * self.row_bits + self.far,
            chunk,
            (flip(self.at, 1), self.me),
        )

    def last_copy(self, chunk):
        place = self.out.at[self.core, chunk]
        return self.remote(
            place,
            place,
            4 + 2 * self.row_bits + self.far,
            3 + 2 * self.row_bits + self.far,
            chunk,
            (flip(self.at, 0), self.me),
        )

    def phase(self, number, chunk):
        bits, half = self.row_bits, self.depth // 2
        if number == 0:
            self.remote(
                self.core_in.at[chunk], self.core_in.at[chunk], 0, 0, chunk, (flip(self.at, 0), self.me)
            ).wait_recv()
            pltpu.make_async_copy(
                self.core_in.at[chunk], self.mine.at[chunk], self.recv_sem.at[1, chunk]
            ).wait()
            self.mine[chunk] = add_low(self.mine[chunk], self.core_in[chunk])
            for side in (0, 1):
                self.row_copy(0, side, chunk).start()
        elif number <= bits:
            stage = number - 1
            for side in (0, 1):
                self.row_copy(stage, side, chunk).wait_recv()
                at = (chunk,) + self.shares(side, stage, False) + (self.rows(side),)
                self.mine[at] = add_low(self.mine[at], self.row_in[stage][side][chunk])
                if stage + 1 < bits:
                    self.row_copy(stage + 1, side, chunk).start()
            if stage + 1 == bits:
                self.near_copy(chunk).start()
        elif number == bits + 1:
            self.near_copy(chunk).wait_recv()
            total = add_low(
                self.mine[self.own(chunk, self.near_rows(True))], self.near_in[chunk]
            )
            self.pass_on(0, chunk, total)
        elif number <= bits + 1 + self.far:
            k = number - bits - 2
            self.far_copy(k, chunk).wait_recv()
            self.pass_on(k + 1, chunk, add_low(self.far_out[k][chunk], self.far_in[k][chunk]))
        elif number == bits + 2 + self.far:
            self.back_copy_arrived(chunk)
            self.last_copy(chunk).start()
        else:
            self.last_arrived(chunk)

    def pass_on(self, k, chunk, total):
        if k < self.far:
            self.far_out[k][chunk] = total
            self.far_copy(k, chunk).start()
        else:
            self.out[self.core, chunk, self.near_rows(True)] = total
            self.back_copy(chunk).start()

    def back_copy_arrived(self, chunk):
        place = self.out.at[self.core, chunk, self.near_rows(False)]
        self.remote(
            place,
            place,
            3 + 2 * self.row_bits + self.far,
            2 + 2 * self.row_bits + self.far,
            chunk,
            (flip(self.at, 1), self.me),
        ).wait_recv()

    def last_arrived(self, chunk):
        place = self.out.at[1 - self.core, chunk]
        self.remote(
            place,
            place,
            4 + 2 * self.row_bits + self.far,
            3 + 2 * self.row_bits + self.far,
            chunk,
            (flip(self.at, 0), self.me),
        ).wait_recv()

    def step(self, t):
        for number in range(self.phases - 1, -1, -1):
            chunk = t - LAG * number

            @pl.when((chunk >= 0) & (chunk < self.chunks))
            def _():
                self.phase(number, jnp.clip(chunk, 0, self.chunks - 1))

    @property
    def steps(self):
        return self.chunks + LAG * (self.phases - 1)

    def finish(self):
        def drain(sem, ref):
            pltpu.make_async_copy(ref, ref, self.send_sem.at[sem]).wait()

        drain(0, self.core_in)
        for stage in range(self.row_bits):
            for side in (0, 1):
                drain(1 + 2 * stage + side, self.row_in[stage][side])
        base = 1 + 2 * self.row_bits
        drain(base, self.near_in)
        for k in range(self.far):
            drain(base + 1 + k, self.far_in[k])
        drain(base + 1 + self.far, self.near_in)
        drain(base + 2 + self.far, self.out.at[0])


def chunk_list(arrays, depth):
    found = []
    for number, array in enumerate(arrays):
        rows, columns = array.shape[-2:]
        lead = array.shape[0] if array.ndim == 3 else None
        for outer in range(lead or 1):
            for row in range(0, rows // lax.axis_size("rows"), depth):
                for column in range(0, columns, STRIP):
                    found.append((number, outer if lead else None, row, column))
    return found


def reduce_kernel(*refs, reducer, table, arrays):
    sources, out_ref, slots = refs[:arrays], refs[arrays], refs[arrays + 1 :]
    reducer.bind(out_ref, slots)
    reducer.greet()
    lead = (slice(None),) * reducer.row_bits
    for chunk, (number, outer, row, column) in enumerate(table):
        ref = sources[number] if outer is None else sources[number].at[outer]
        reducer.first(ref.at[lead + (pl.ds(row, reducer.depth), slice(None))], column, chunk)

    def step(t, carry):
        reducer.step(t)
        return carry

    lax.fori_loop(0, reducer.steps, step, 0)
    reducer.finish()


def share_views(arrays):
    bits = axis_bits("rows")
    views = []
    for array in arrays:
        lead = array.shape[:-2]
        views.append(
            array.reshape(lead + (2,) * bits + (array.shape[-2] >> bits, array.shape[-1]))
        )
    return views


def reduce_all(arrays, depth, collective_id):
    table = chunk_list(arrays, depth)
    reducer = Reducer(len(table), depth, axis_bits("rows"), axis_bits("items"))
    out = pl.pallas_call(
        functools.partial(reduce_kernel, reducer=reducer, table=table, arrays=len(arrays)),
        in_specs=[pl.BlockSpec(memory_space=pl.ANY)] * len(arrays),
        out_specs=pl.BlockSpec(memory_space=pltpu.VMEM),
        out_shape=reducer.out_shape(),
        scratch_shapes=reducer.scratch(),
        compiler_params=pltpu.CompilerParams(
            vmem_limit_bytes=58 << 20, collective_id=collective_id, has_side_effects=True
        ),
        name="reduce_weights",
    )(*share_views(arrays))
    return unpack(out, arrays, table, depth)


def unpack_kernel(held_ref, *refs, table, depth, outs):
    targets, (wide, sem) = refs[:outs], refs[outs:]

    def copy(chunk, number, outer, row, column):
        target = targets[number] if outer is None else targets[number].at[outer]
        return pltpu.make_async_copy(
            wide.at[chunk],
            target.at[pl.ds(row, depth), pl.ds(column, STRIP)],
            sem.at[chunk],
        )

    for chunk, entry in enumerate(table):
        wide[chunk] = jnp.concatenate(
            [held_ref[0, chunk].astype(F32), held_ref[1, chunk].astype(F32)], axis=1
        )
        copy(chunk, *entry).start()
    for chunk, entry in enumerate(table):
        copy(chunk, *entry).wait()


def unpack(out, arrays, table, depth):
    count = lax.axis_size("rows")
    shapes = [
        jax.ShapeDtypeStruct(
            array.shape[:-2] + (array.shape[-2] // count, array.shape[-1]), F32
        )
        for array in arrays
    ]
    return pl.pallas_call(
        functools.partial(unpack_kernel, table=table, depth=depth, outs=len(arrays)),
        in_specs=[pl.BlockSpec(memory_space=pltpu.VMEM)],
        out_specs=[pl.BlockSpec(memory_space=pl.ANY)] * len(arrays),
        out_shape=shapes,
        scratch_shapes=[
            pltpu.VMEM((len(table), depth, STRIP), F32),
            pltpu.SemaphoreType.DMA((len(table),)),
        ],
        compiler_params=pltpu.CompilerParams(vmem_limit_bytes=40 << 20),
        name="unpack",
    )(out)


def shards(
    tokens,
    valid_rows,
    dataset_ids,
    shift_flags,
    norm_gains,
    norm_biases,
    qkv_weight,
    qv_bias,
    out_weight,
    out_bias,
    fc1_weight,
    fc1_bias,
    fc2_weight,
    fc2_bias,
    tap_weight,
    tap_bias,
    conv_weights,
    conv_biases,
    table_gain,
    table_shift,
    token_cotangent,
    joined_cotangent,
):
    items_here, tok_here, width = tokens.shape
    rows_here = tok_here // PC
    channels = tap_weight.shape[1]
    row_index = lax.axis_index("rows")
    row_count = lax.axis_size("rows")
    last_index = row_count - 1

    flat_in = tokens.reshape(-1, width).astype(F32)
    normed_one = layer_norm(flat_in, norm_gains[0], norm_biases[0]).astype(BF)
    normed_all = [
        gather_blocks(normed_one[i * tok_here : (i + 1) * tok_here]) for i in range(items_here)
    ]
    starts = jnp.stack([(row_index ^ j) * tok_here for j in range(row_count)]).astype(jnp.int32)
    infos = [
        jnp.concatenate([valid_rows[i : i + 1] * PC, starts]) for i in range(items_here)
    ]
    key_weight = qkv_weight[:, width:]
    key_shift = jnp.concatenate([jnp.zeros((width,), F32), qv_bias[width:]])
    queries = (mm(normed_one, qkv_weight[:, :width]) + qv_bias[:width]).astype(BF)
    queries = [queries[i * tok_here : (i + 1) * tok_here] for i in range(items_here)]
    keyvals, attended, lses = [], [], []
    for i in range(items_here):
        keyvals.append((mm(normed_all[i], key_weight) + key_shift).astype(BF))
        out, lse = attention_forward(infos[i], queries[i], keyvals[i])
        attended.append(out)
        lses.append(lse)
    attended_flat = jnp.concatenate(attended)
    resid = flat_in + mm(attended_flat, out_weight) + out_bias
    normed_two = layer_norm(resid, norm_gains[1], norm_biases[1]).astype(BF)
    hidden_pre = mm(normed_two, fc1_weight) + fc1_bias
    hidden_cdf, hidden_rest = normal_parts(hidden_pre)
    hidden = (hidden_pre * hidden_cdf).astype(BF)
    hidden_slope = (hidden_cdf + hidden_rest).astype(BF)
    output = resid + mm(hidden, fc2_weight) + fc2_bias
    output_low = output.astype(BF)
    grid_rows = row_index * rows_here + jnp.arange(rows_here, dtype=jnp.int32)
    row_valid = (grid_rows[None, :] < valid_rows[:, None]).astype(F32)
    token_valid = jnp.broadcast_to(
        row_valid[:, :, None], (items_here, rows_here, PC)
    ).reshape(-1, 1)
    tap_pre = mm(output_low, tap_weight) + tap_bias
    field = (tap_pre * token_valid).reshape(items_here, rows_here, PC, channels)

    choose = (
        dataset_ids[:, None] == jnp.arange(table_gain.shape[0], dtype=jnp.int32)[None, :]
    ).astype(F32)
    flag_value = shift_flags.astype(F32)[:, None]
    gain_pick = jnp.dot(choose, table_gain, precision=highest)
    shift_pick = jnp.dot(choose, table_shift, precision=highest)
    factor = 1.0 + flag_value * (gain_pick - 1.0)
    offset = flag_value * shift_pick
    joined, grad_field, conv_grads, grad_conv_biases, table_sums = refine(
        field, conv_weights, conv_biases, factor, offset, joined_cotangent
    )
    grad_table_gain = jnp.dot(choose.T, flag_value * table_sums[0], precision=highest)
    grad_table_shift = jnp.dot(choose.T, flag_value * table_sums[1], precision=highest)
    grad_field = grad_field[:, :, :PC]
    grad_tap = (grad_field.reshape(-1, channels) * token_valid).astype(BF)
    tap_grad = mm(output_low, grad_tap, TN).astype(BF)
    grad_tap_bias = jnp.sum(grad_tap.astype(F32), axis=0)
    grad_output = token_cotangent.reshape(-1, width).astype(F32) + mm(grad_tap, tap_weight, NT)
    grad_mlp = grad_output.astype(BF)
    fc2_grad = mm(hidden, grad_mlp, TN).astype(BF)
    grad_fc2_bias = jnp.sum(grad_mlp.astype(F32), axis=0)
    grad_pre = (mm(grad_mlp, fc2_weight, NT) * hidden_slope.astype(F32)).astype(BF)
    fc1_grad = mm(normed_two, grad_pre, TN).astype(BF)
    grad_fc1_bias = jnp.sum(grad_pre.astype(F32), axis=0)
    grad_normed_two = mm(grad_pre, fc1_weight, NT)
    grad_resid_norm, grad_gain_two, grad_shift_two = norm_back(
        resid, norm_gains[1], grad_normed_two
    )
    grad_resid = grad_output + grad_resid_norm
    grad_branch = grad_resid.astype(BF)
    out_grad = mm(attended_flat, grad_branch, TN).astype(BF)
    grad_out_bias = jnp.sum(grad_branch.astype(F32), axis=0)
    grad_attended = mm(grad_branch, out_weight, NT).astype(BF)

    grads_q, grads_k, grads_v, grads_in = [], [], [], []
    for i in range(items_here):
        here = slice(i * tok_here, (i + 1) * tok_here)
        grad_q, grad_k, grad_v = attention_backward(
            infos[i], queries[i], keyvals[i], grad_attended[here], attended[i], lses[i]
        )
        partial = (
            mm(grad_k, qkv_weight[:, width : 2 * width], NT)
            + mm(grad_v, qkv_weight[:, 2 * width :], NT)
        ).astype(BF)
        own = mm(grad_q, qkv_weight[:, :width], NT)
        grads_in.append(scatter_blocks(partial) + own)
        grads_q.append(grad_q)
        grads_k.append(grad_k)
        grads_v.append(grad_v)
    grad_q = jnp.concatenate(grads_q)
    every_norm = jnp.concatenate(normed_all)
    every_k = jnp.concatenate(grads_k)
    every_v = jnp.concatenate(grads_v)
    q_grad = mm(normed_one, grad_q, TN).astype(BF)
    k_grad = mm(every_norm, every_k, TN).astype(BF)
    v_grad = mm(every_norm, every_v, TN).astype(BF)
    qkv_grad = jnp.concatenate([q_grad, k_grad, v_grad], axis=1)
    grad_q_bias = jnp.sum(grad_q.astype(F32), axis=0)
    grad_v_bias = jnp.sum(every_v.astype(F32), axis=0)
    grad_in_norm, grad_gain_one, grad_shift_one = norm_back(
        flat_in, norm_gains[0], jnp.concatenate(grads_in)
    )
    grad_tokens = (grad_resid + grad_in_norm).reshape(tokens.shape)

    small = [
        (jnp.stack([grad_gain_one, grad_gain_two]), 1),
        (jnp.stack([grad_shift_one, grad_shift_two]), 1),
        (jnp.concatenate([grad_q_bias, grad_v_bias]), 0),
        (grad_out_bias, 0),
        (grad_fc1_bias, 0),
        (grad_fc2_bias, 0),
        (grad_tap_bias, 0),
        (grad_conv_biases, 1),
        (grad_table_gain, 1),
        (grad_table_shift, 1),
    ]
    packed, shapes = [], []
    for array, dim in small:
        if array.ndim == 1:
            pieces = array.reshape(row_count, -1)
        else:
            pieces = jnp.swapaxes(
                array.reshape(array.shape[0], row_count, -1), 0, 1
            ).reshape(row_count, -1)
        shapes.append((array.ndim, array.shape[0], pieces.shape[1]))
        packed.append(pieces)
    packed = jnp.concatenate(packed, axis=1)
    depth = width // row_count
    size = packed.shape[1]
    packed = jnp.pad(packed, ((0, 0), (0, depth * STRIP - size))).astype(BF)
    packed = packed.reshape(row_count * depth, STRIP)
    (
        share_conv,
        share_tap,
        share_fc2,
        share_fc1,
        share_out,
        share_qkv,
        summed,
    ) = reduce_all(
        [conv_grads, tap_grad, fc2_grad, fc1_grad, out_grad, qkv_grad, packed], depth, 1
    )
    summed = summed.reshape(-1)
    outs, place = [], 0
    for ndim, lead, length in shapes:
        piece = summed[place : place + length]
        place += length
        outs.append(piece if ndim == 1 else piece.reshape(lead, -1))
    (
        out_gains,
        out_shifts,
        out_qv,
        out_out,
        out_fc1,
        out_fc2,
        out_tap,
        out_conv,
        out_table_gain,
        out_table_shift,
    ) = outs
    return (
        output_low.reshape(tokens.shape),
        joined,
        grad_tokens,
        out_gains,
        out_shifts,
        share_qkv,
        out_qv,
        share_out,
        out_out,
        share_fc1,
        out_fc1,
        share_fc2,
        out_fc2,
        share_tap,
        out_tap,
        share_conv,
        out_conv,
        out_table_gain,
        out_table_shift,
    )


def solution(mesh):
    return jax.shard_map(
        shards,
        mesh=mesh,
        in_specs=(P("items", "rows", None), P("items"), P("items"), P("items"))
        + (P(),) * 16
        + (P("items", "rows", None), P("items", "rows", None, None)),
        out_specs=(
            P("items", "rows", None),
            P("items", "rows", None, None),
            P("items", "rows", None),
            P(None, "rows"),
            P(None, "rows"),
            P("rows", None),
            P("rows"),
            P("rows", None),
            P("rows"),
            P("rows", None),
            P("rows"),
            P("rows", None),
            P("rows"),
            P("rows", None),
            P("rows"),
            P(None, "rows", None),
            P(None, "rows"),
            P(None, "rows"),
            P(None, "rows"),
        ),
        check_vma=False,
    )
```

time: 1260 us -> 556 us (0.44)
  waiting for transfers between devices: 500 us -> 35.9 us
  Pallas kernels: 0 us -> 258 us
  matrix products: 315 us -> 127 us
  other arithmetic: 172 us -> 36.3 us
  local copies, waits for them, and re-layouts: 157 us -> 58.9 us
  blocking collectives: 45.7 us -> 0 us
  starting transfers between devices: 48.5 us -> 30.1 us
  between operations: 19.1 us -> 4.19 us
    pallas_call x0 -> x9, Pallas kernels: none -> 258 us  [the longest x1 106 us: reduce_all(): pl.pallas_call(functools.partial(reduce_kernel, reducer=reducer, table=ta...]
    reduce_scatter x8 -> x0, waiting for transfers between devices: 248 us -> none  [the longest x1 60.1 us: shards(): lax.psum_scatter(summed[6].astype(jnp.bfloat16), 'rows', scatter_dimensio...]
    dot_general x35 -> x30, matrix products: 314 us -> 125 us  [the longest x28 125 us: mm(): return lax.dot_general(left, right, dims, preferred_element_type=F32)]
    unnamed x21 -> x0, waiting for transfers between devices: 85.1 us -> none
    convert_element_type x26 -> x7, other arithmetic: 85.3 us -> 1.04 us  [the longest x1 0.6 us: shards(): normed_one = layer_norm(flat_in, norm_gains[0], norm_biases[0]).astype(BF)]
    psum x1 -> x0, waiting for transfers between devices: 70.6 us -> none  [shards(): lax.psum(grad_qkv_weight.astype(jnp.bfloat16), 'items').astype(jnp.float32)]
    all_gather x2 -> x0, waiting for transfers between devices: 65.6 us -> none  [the longest x1 55.4 us: fold_keys(): lax.all_gather(key_rows, 'rows', axis=1, tiled=True)]
    reshape x12 -> x10, local copies, waits for them, and re-layouts: 42.1 us -> 0.79 us  [the longest x5 0.44 us: shards(): pieces = jnp.swapaxes(array.reshape(array.shape[0], row_count, -1), 0, 1)...]
  transfers between devices with their start and end apart: 36 -> 24, of which waited for: 24 -> 12; matrix products, arithmetic and copies ran while one was open for 25% -> 8% of each run, Pallas kernels for 0% -> 2%
where the time goes in v1:
time: 556 us; the launch traced here: 551 us
  Pallas kernels  258 us (46%)
  matrix products  127 us (23%)
  local copies, waits for them, and re-layouts  58.9 us (11%)
  other arithmetic  36.3 us (7%)
  waiting for transfers between devices  35.9 us (6%)
  starting transfers between devices  30.1 us (5%)
    dot_general x28, matrix products, mm(): return lax.dot_general(left, right, dims, preferred_element_type=F32)  125 us
    pallas_call x1, Pallas kernels, reduce_all(): pl.pallas_call(functools.partial(reduce_kernel, reducer=reducer, table=ta...  106 us
    pallas_call x1, Pallas kernels, refine(): pl.pallas_call(functools.partial(refine_kernel, items=items, rows=rows, c...  59.8 us
    pallas_call x3, Pallas kernels, attention_backward(): pl.pallas_call(functools.partial(attention_backward_kernel, kb=n // 2), g...  57.9 us
    unnamed x233, local copies, waits for them, and re-layouts  40.2 us
    ppermute x24, waiting for transfers between devices, swap(): return lax.ppermute(block, axis, [(i, i ^ mask) for i in range(count)])  35.9 us
    pallas_call x3, Pallas kernels, attention_forward(): pl.pallas_call(attention_forward_kernel, grid=(groups,), in_specs=[pl.Blo...  30.8 us
    ppermute x24, starting transfers between devices, swap(): return lax.ppermute(block, axis, [(i, i ^ mask) for i in range(count)])  30.1 us
  transfers between devices with their start and end apart: 24, of which 12 were waited for; matrix products, arithmetic and copies ran while one was open for 8% of the time, Pallas kernels for 2%

profile of v1, /device:TPU:0, one launch (start us, length us, event | category | flops | bytes accessed | tf_op | source)
XLA Modules:
  0.0 550.8 jit_solution(17817354584961753179)
XLA Ops:
  39.7 4.1 collective-permute-done.2
  50.4 3.9 collective-permute-done.6
  67.6 10.2 %attention_forward.3 = (bf16[320,768]{1,0:T(8,128)(2,1)S(1)}, f32[3,8,1280]{2,1,0:T(8,128)S(1)}) custom-call(s32[5]{0:T(128)S(1)} %concatenate.114.info_ref, bf16[320,768]{1,0:T(8,128)(2,1)S(1)} %get-tuple-element.122.q_ref, bf16[1280,1536]{1,0:T(8,128)(2,1)S(1)} %fusion.k_ref.v_ref, bf16[1280,1536]{1,0:T(8,128)(2,1)S(1)} %fusion.k_ref.v_ref), custom_call_target="tpu_custom_call" | custom-call | flops 5033164800 | bytes 4915200 | tf_op jit(solution)/shard_map/attention_forward/pallas_call | solution.py:190
  87.9 10.2 %attention_forward.4 = (bf16[320,768]{1,0:T(8,128)(2,1)S(1)}, f32[3,8,1280]{2,1,0:T(8,128)S(1)}) custom-call(s32[5]{0:T(128)S(1)} %concatenate.119.info_ref, bf16[320,768]{1,0:T(8,128)(2,1)S(1)} %get-tuple-element.121.q_ref, bf16[1280,1536]{1,0:T(8,128)(2,1)S(1)} %fusion.1.k_ref.v_ref, bf16[1280,1536]{1,0:T(8,128)(2,1)S(1)} %fusion.1.k_ref.v_ref), custom_call_target="tpu_custom_call" | custom-call | flops 5033164800 | bytes 4915200 | tf_op jit(solution)/shard_map/attention_forward/pallas_call | solution.py:190
  99.0 10.4 %attention_forward.5 = (bf16[320,768]{1,0:T(8,128)(2,1)S(1)}, f32[3,8,1280]{2,1,0:T(8,128)S(1)}) custom-call(s32[5]{0:T(128)S(1)} %concatenate.123.info_ref, bf16[320,768]{1,0:T(8,128)(2,1)S(1)} %get-tuple-element.120.q_ref, bf16[1280,1536]{1,0:T(8,128)(2,1)S(1)} %fusion.2.k_ref.v_ref, bf16[1280,1536]{1,0:T(8,128)(2,1)S(1)} %fusion.2.k_ref.v_ref), custom_call_target="tpu_custom_call" | custom-call | flops 5033164800 | bytes 4915200 | tf_op jit(solution)/shard_map/attention_forward/pallas_call | solution.py:190
  112.3 14.9 %multiply_convert_fusion.1 = (bf16[960,3072]{1,0:T(8,128)(2,1)S(1)}, f32[960,3072]{1,0:T(8,128)}) fusion(f32[3072]{0:T(1024)S(1)} %copy-done.76, bf16[768,3072]{1,0:T(8,128)(2,1)S(1)} %bitcast.139, f32[768]{0:T(1024)S(1)} %get-tuple-element.81, f32[768]{0:T(1024)S(1)} %get-tuple-element.161, f32[960]{0:T(1024)S(1)} %add_rsqrt_fusion.1, ...), kind=kOutput, calls=%fused_computation.3 | convolution fusion | flops 4599152640 | bytes 25391616 | tf_op jit(solution)/shard_map/dot_general | solution.py:28
  127.2 4.8 add_convert_fusion.4
  133.7 59.8 %refine.1 = (bf16[3,16,80,256]{3,2,1,0:T(8,128)(2,1)}, f32[3,8,48,256]{3,2,1,0:T(8,128)}, bf16[4,2304,256]{2,1,0:T(8,128)(2,1)}, f32[4,256]{1,0:T(4,128)}, f32[2,3,256]{2,1,0:T(4,128)}) custom-call(f32[3,8,48,256]{3,2,1,0:T(8,128)} %pad.10.field_ref, bf16[4,2304,256]{2,1,0:T(8,128)(2,1)} %weight_ref.1, f32[4,256]{1,0:T(4,128)} %bias_ref.1, ...), custom_call_target="tpu_custom_call" | custom-call | flops 13589544960 | bytes 20971520 | tf_op jit(solution)/shard_map/refine/pallas_call | solution.py:622
  200.0 6.9 %convolution_convert_fusion.1 = bf16[3072,768]{1,0:T(8,128)(2,1)} fusion(bf16[960,3072]{1,0:T(8,128)(2,1)S(1)} %copy-done.90, bf16[960,768]{1,0:T(8,128)(2,1)S(1)} %get-tuple-element.84), kind=kOutput, calls=%fused_computation.25 | convolution fusion | flops 4532207616 | bytes 12091392 | tf_op jit(solution)/shard_map/dot_general | solution.py:28
  207.0 16.2 %fusion.107 = (bf16[3072]{0:T(1024)(128)(2,1)S(1)}, bf16[960,3072]{1,0:T(8,128)(2,1)}) fusion(f32[960,3072]{1,0:T(8,128)} %get-tuple-element.149, f32[3072]{0:T(1024)S(1)} %copy-done.76, bf16[960,768]{1,0:T(8,128)(2,1)S(1)} %get-tuple-element.84, bf16[3072,768]{1,0:T(8,128)(2,1)S(1)} %bitcast.137), kind=kOutput, calls=%fused_computation.239 | convolution fusion | flops 4612420608 | bytes 23906304 | tf_op jit(solution)/shard_map/dot_general | solution.py:28
  223.2 9.6 %multiply_reduce_fusion = (bf16[768]{0:T(1024)(128)(2,1)S(1)}, f32[960]{0:T(1024)S(1)}, f32[960]{0:T(1024)S(1)}, bf16[768]{0:T(1024)(128)(2,1)S(1)}, f32[960,768]{1,0:T(8,128)S(1)}) fusion(f32[960]{0:T(1024)S(1)} %add_rsqrt_fusion.1, f32[960]{0:T(1024)S(1)} %broadcast_multiply_fusion.5, f32[960,768]{1,0:T(8,128)S(1)} %bitcast_add_fusion, ...), kind=kOutput, calls=%fused_computation.51 | convolution fusion | flops 4537217024 | bytes 16539648 | tf_op jit(solution)/shard_map/dot_general | solution.py:28
  232.8 8.0 %convolution_convert_fusion = bf16[768,3072]{1,0:T(8,128)(2,1)} fusion(bf16[960,3072]{1,0:T(8,128)(2,1)S(1)} %copy-done.88, f32[768]{0:T(1024)S(1)} %get-tuple-element.81, f32[768]{0:T(1024)S(1)} %get-tuple-element.161, f32[960,768]{1,0:T(8,128)S(1)} %bitcast_add_fusion, f32[960]{0:T(1024)S(1)} %add_rsqrt_fusion.1, f32[960]{0:T(1024)S(1)} %broadcast_multiply_fusion.5, ...), kind=kOutput, calls=%fused_computation.24 | convolution fusion | flops 4536631296 | bytes 13582848 | tf_op jit(solution)/shard_map/dot_general | solution.py:28
  247.4 19.2 %attention_backward.5 = (bf16[320,768]{1,0:T(8,128)(2,1)S(1)}, bf16[1280,768]{1,0:T(8,128)(2,1)S(1)}, bf16[1280,768]{1,0:T(8,128)(2,1)S(1)}) custom-call(s32[5]{0:T(128)S(1)} %concatenate.123.info_ref, bf16[320,768]{1,0:T(8,128)(2,1)S(1)} %copy-done.10, bf16[1280,1536]{1,0:T(8,128)(2,1)} %copy-done.36, bf16[1280,1536]{1,0:T(8,128)(2,1)} %copy-done.36, ...), custom_call_target="tpu_custom_call" | custom-call | flops 12582912000 | bytes 9830400 | tf_op jit(solution)/shard_map/attention_backward/pallas_call | solution.py:259
  268.6 19.1 %attention_backward.3 = (bf16[320,768]{1,0:T(8,128)(2,1)S(1)}, bf16[1280,768]{1,0:T(8,128)(2,1)S(1)}, bf16[1280,768]{1,0:T(8,128)(2,1)S(1)}) custom-call(s32[5]{0:T(128)S(1)} %copy-done.27, bf16[320,768]{1,0:T(8,128)(2,1)S(1)} %copy-done.8, bf16[1280,1536]{1,0:T(8,128)(2,1)} %copy-done.34, bf16[1280,1536]{1,0:T(8,128)(2,1)} %copy-done.34, ...), custom_call_target="tpu_custom_call" | custom-call | flops 12582912000 | bytes 9830400 | tf_op jit(solution)/shard_map/attention_backward/pallas_call | solution.py:259
  296.4 19.6 %attention_backward.4 = (bf16[320,768]{1,0:T(8,128)(2,1)S(1)}, bf16[1280,768]{1,0:T(8,128)(2,1)S(1)}, bf16[1280,768]{1,0:T(8,128)(2,1)S(1)}) custom-call(s32[5]{0:T(128)S(1)} %copy-done.25, bf16[320,768]{1,0:T(8,128)(2,1)S(1)} %copy-done.6, bf16[1280,1536]{1,0:T(8,128)(2,1)} %copy-done.35, bf16[1280,1536]{1,0:T(8,128)(2,1)} %copy-done.35, ...), custom_call_target="tpu_custom_call" | custom-call | flops 12582912000 | bytes 9830400 | tf_op jit(solution)/shard_map/attention_backward/pallas_call | solution.py:259
  327.2 9.8 %fusion.34 = bf16[768,768]{0,1:T(8,128)(2,1)} fusion(bf16[3840,768]{1,0:T(8,128)(2,1)} %get-tuple-element.123, bf16[1280,768]{1,0:T(8,128)(2,1)S(1)} %get-tuple-element.61, bf16[1280,768]{1,0:T(8,128)(2,1)} %copy-done.2, bf16[1280,768]{1,0:T(8,128)(2,1)} %copy-done.4), kind=kOutput, calls=%fused_computation.67 | convolution fusion | flops 4548132864 | bytes 12976128 | tf_op jit(solution)/shard_map/dot_general | solution.py:28
  344.3 6.3 %fusion.37 = bf16[768,768]{0,1:T(8,128)(2,1)} fusion(bf16[3840,768]{1,0:T(8,128)(2,1)S(1)} %bitcast.132, bf16[1280,768]{1,0:T(8,128)(2,1)S(1)} %copy-done.29, bf16[1280,768]{1,0:T(8,128)(2,1)S(1)} %copy-done.33, bf16[1280,768]{1,0:T(8,128)(2,1)S(1)} %copy-done.31), kind=kOutput, calls=%fused_computation.68 | convolution fusion | flops 4548132864 | bytes 12976128 | tf_op jit(solution)/shard_map/dot_general | solution.py:28
  359.5 5.8 %copy.49 = bf16[768,2304]{1,0:T(8,128)(2,1)} copy(bf16[768,2304]{0,1:T(8,128)(2,1)} %pad_maximum_fusion) | data formatting | bytes 7077888 | tf_op jit(solution)/shard_map/concatenate | solution.py:1138
  365.3 4.9 add_convert_fusion.3
  390.5 3.9 collective-permute-done.20
  396.6 12.3 %collective-permute-done.13 = bf16[160,768]{1,0:T(8,128)(2,1)S(1)} collective-permute-done((bf16[160,768]{1,0:T(8,128)(2,1)S(1)}, bf16[160,768]{1,0:T(8,128)(2,1)S(1)}, u32[]{:S(2)}, u32[]{:S(2)}) %collective-permute-start.13) | collective-permute-done | bytes 245792 | tf_op jit(solution)/shard_map/ppermute | solution.py:83
  427.1 105.7 %reduce_weights.1.held_ref = bf16[2,50,192,128]{3,2,1,0:T(8,128)(2,1)} custom-call(bf16[4,2,2,576,256]{4,3,2,1,0:T(8,128)(2,1)} %bitcast.118, bf16[2,2,192,256]{3,2,1,0:T(8,128)(2,1)} %bitcast.126, bf16[2,2,768,768]{3,2,1,0:T(8,128)(2,1)} %bitcast.119, bf16[2,2,192,3072]{3,2,1,0:T(8,128)(2,1)} %bitcast.120, bf16[2,2,192,768]{3,2,1,0:T(8,128)(2,1)} %bitcast.124, ...), custom_call_target="tpu_custom_call" | custom-call | tf_op jit(solution)/shard_map/reduce_weights/pallas_call | solution.py:959
  535.2 4.1 unpack.1
  543.9 5.4 fusion.29
  (417 shorter events, 171.4 us)
Async XLA Ops:
  6.6 30.3 %collective-permute-start.9 = (bf16[160,768]{1,0:T(8,128)(2,1)}, bf16[160,768]{1,0:T(8,128)(2,1)}, u32[]{:S(2)}, u32[]{:S(2)}) collective-permute-start(bf16[160,768]{1,0:T(8,128)(2,1)} %get-tuple-element.114), channel_id=1, source_target_pairs={{0,2},{1,3},{2,0},{3,1},{4,6},{5,7},{6,4},{7,5},{8,10},{9,11},{10,... | collective-permute-start | bytes 737288 | tf_op jit(solution)/shard_map/ppermute | solution.py:83
  9.7 25.7 %collective-permute-start.8 = (bf16[160,768]{1,0:T(8,128)(2,1)}, bf16[160,768]{1,0:T(8,128)(2,1)}, u32[]{:S(2)}, u32[]{:S(2)}) collective-permute-start(bf16[160,768]{1,0:T(8,128)(2,1)} %get-tuple-element.115), channel_id=1, source_target_pairs={{0,1},{1,0},{2,3},{3,2},{4,5},{5,4},{6,7},{7,6},{8,9},{9,8},{10,11... | collective-permute-start | bytes 737288 | tf_op jit(solution)/shard_map/ppermute | solution.py:83
  11.2 21.0 %collective-permute-start.5 = (bf16[160,768]{1,0:T(8,128)(2,1)}, bf16[160,768]{1,0:T(8,128)(2,1)S(1)}, u32[]{:S(2)}, u32[]{:S(2)}) collective-permute-start(bf16[160,768]{1,0:T(8,128)(2,1)} %get-tuple-element.116), channel_id=1, source_target_pairs={{0,2},{1,3},{2,0},{3,1},{4,6},{5,7},{6,4},{7,5},{8,10},{9,11},{10,... | collective-permute-start | bytes 737288 | tf_op jit(solution)/shard_map/ppermute | solution.py:83
  11.7 14.7 %collective-permute-start.1 = (bf16[160,768]{1,0:T(8,128)(2,1)}, bf16[160,768]{1,0:T(8,128)(2,1)S(1)}, u32[]{:S(2)}, u32[]{:S(2)}) collective-permute-start(bf16[160,768]{1,0:T(8,128)(2,1)} %get-tuple-element.118), channel_id=1, source_target_pairs={{0,2},{1,3},{2,0},{3,1},{4,6},{5,7},{6,4},{7,5},{8,10},{9,11},{10,... | collective-permute-start | bytes 737288 | tf_op jit(solution)/shard_map/ppermute | solution.py:83
  13.2 10.0 %collective-permute-start = (bf16[160,768]{1,0:T(8,128)(2,1)}, bf16[160,768]{1,0:T(8,128)(2,1)}, u32[]{:S(2)}, u32[]{:S(2)}) collective-permute-start(bf16[160,768]{1,0:T(8,128)(2,1)} %get-tuple-element.119), channel_id=1, source_target_pairs={{0,1},{1,0},{2,3},{3,2},{4,5},{5,4},{6,7},{7,6},{8,9},{9,8},{10,11... | collective-permute-start | bytes 737288 | tf_op jit(solution)/shard_map/ppermute | solution.py:83
  23.1 6.5 %collective-permute-start.4 = (bf16[160,768]{1,0:T(8,128)(2,1)}, bf16[160,768]{1,0:T(8,128)(2,1)S(1)}, u32[]{:S(2)}, u32[]{:S(2)}) collective-permute-start(bf16[160,768]{1,0:T(8,128)(2,1)} %get-tuple-element.117), channel_id=1, source_target_pairs={{0,1},{1,0},{2,3},{3,2},{4,5},{5,4},{6,7},{7,6},{8,9},{9,8},{10,11... | collective-permute-start | bytes 737288 | tf_op jit(solution)/shard_map/ppermute | solution.py:83
  26.4 19.7 %collective-permute-start.3 = (bf16[320,768]{1,0:T(8,128)(2,1)S(1)}, bf16[320,768]{1,0:T(8,128)(2,1)S(1)}, u32[]{:S(2)}, u32[]{:S(2)}) collective-permute-start(bf16[320,768]{1,0:T(8,128)(2,1)S(1)} %pad_maximum_fusion.3), channel_id=1, source_target_pairs={{0,2},{1,3},{2,0},{3,1},{4,6},{5,7},{6,4},{7,5},{8,10},{9,11},{10,... | collective-permute-start | bytes 1474568 | tf_op jit(solution)/shard_map/ppermute | solution.py:83
  29.6 14.2 %collective-permute-start.2 = (bf16[320,768]{1,0:T(8,128)(2,1)S(1)}, bf16[320,768]{1,0:T(8,128)(2,1)S(1)}, u32[]{:S(2)}, u32[]{:S(2)}) collective-permute-start(bf16[320,768]{1,0:T(8,128)(2,1)S(1)} %pad_maximum_fusion.2), channel_id=1, source_target_pairs={{0,1},{1,0},{2,3},{3,2},{4,5},{5,4},{6,7},{7,6},{8,9},{9,8},{10,11... | collective-permute-start | bytes 1474568 | tf_op jit(solution)/shard_map/ppermute | solution.py:83
  32.1 22.9 %collective-permute-start.7 = (bf16[320,768]{1,0:T(8,128)(2,1)S(1)}, bf16[320,768]{1,0:T(8,128)(2,1)S(1)}, u32[]{:S(2)}, u32[]{:S(2)}) collective-permute-start(bf16[320,768]{1,0:T(8,128)(2,1)S(1)} %pad_maximum_fusion.5), channel_id=1, source_target_pairs={{0,2},{1,3},{2,0},{3,1},{4,6},{5,7},{6,4},{7,5},{8,10},{9,11},{10,... | collective-permute-start | bytes 1474568 | tf_op jit(solution)/shard_map/ppermute | solution.py:83
  35.4 19.0 %collective-permute-start.6 = (bf16[320,768]{1,0:T(8,128)(2,1)S(1)}, bf16[320,768]{1,0:T(8,128)(2,1)S(1)}, u32[]{:S(2)}, u32[]{:S(2)}) collective-permute-start(bf16[320,768]{1,0:T(8,128)(2,1)S(1)} %pad_maximum_fusion.4), channel_id=1, source_target_pairs={{0,1},{1,0},{2,3},{3,2},{4,5},{5,4},{6,7},{7,6},{8,9},{9,8},{10,11... | collective-permute-start | bytes 1474568 | tf_op jit(solution)/shard_map/ppermute | solution.py:83
  36.9 43.6 %collective-permute-start.11 = (bf16[320,768]{1,0:T(8,128)(2,1)S(1)}, bf16[320,768]{1,0:T(8,128)(2,1)S(1)}, u32[]{:S(2)}, u32[]{:S(2)}) collective-permute-start(bf16[320,768]{1,0:T(8,128)(2,1)S(1)} %pad_maximum_fusion.7), channel_id=1, source_target_pairs={{0,2},{1,3},{2,0},{3,1},{4,6},{5,7},{6,4},{7,5},{8,10},{9,11},{10,... | collective-permute-start | bytes 1474568 | tf_op jit(solution)/shard_map/ppermute | solution.py:83
  43.8 36.0 %collective-permute-start.10 = (bf16[320,768]{1,0:T(8,128)(2,1)S(1)}, bf16[320,768]{1,0:T(8,128)(2,1)S(1)}, u32[]{:S(2)}, u32[]{:S(2)}) collective-permute-start(bf16[320,768]{1,0:T(8,128)(2,1)S(1)} %pad_maximum_fusion.6), channel_id=1, source_target_pairs={{0,1},{1,0},{2,3},{3,2},{4,5},{5,4},{6,7},{7,6},{8,9},{9,8},{10,11... | collective-permute-start | bytes 1474568 | tf_op jit(solution)/shard_map/ppermute | solution.py:83
  370.4 25.4 %collective-permute-start.14 = (bf16[320,768]{1,0:T(8,128)(2,1)S(1)}, bf16[320,768]{1,0:T(8,128)(2,1)S(1)}, u32[]{:S(2)}, u32[]{:S(2)}) collective-permute-start(bf16[320,768]{1,0:T(8,128)(2,1)S(1)} %pad_maximum_fusion.9), channel_id=1, source_target_pairs={{0,1},{1,0},{2,3},{3,2},{4,5},{5,4},{6,7},{7,6},{8,9},{9,8},{10,11... | collective-permute-start | bytes 1474568 | tf_op jit(solution)/shard_map/ppermute | solution.py:83
  372.5 11.5 %collective-permute-start.12 = (bf16[320,768]{1,0:T(8,128)(2,1)S(1)}, bf16[320,768]{1,0:T(8,128)(2,1)S(1)}, u32[]{:S(2)}, u32[]{:S(2)}) collective-permute-start(bf16[320,768]{1,0:T(8,128)(2,1)S(1)} %pad_maximum_fusion.8), channel_id=1, source_target_pairs={{0,2},{1,3},{2,0},{3,1},{4,6},{5,7},{6,4},{7,5},{8,10},{9,11},{10,... | collective-permute-start | bytes 1474568 | tf_op jit(solution)/shard_map/ppermute | solution.py:83
  375.8 13.4 %collective-permute-start.16 = (bf16[320,768]{1,0:T(8,128)(2,1)S(1)}, bf16[320,768]{1,0:T(8,128)(2,1)S(1)}, u32[]{:S(2)}, u32[]{:S(2)}) collective-permute-start(bf16[320,768]{1,0:T(8,128)(2,1)S(1)} %pad_maximum_fusion.10), channel_id=1, source_target_pairs={{0,2},{1,3},{2,0},{3,1},{4,6},{5,7},{6,4},{7,5},{8,10},{9,11},{10,... | collective-permute-start | bytes 1474568 | tf_op jit(solution)/shard_map/ppermute | solution.py:83
  378.5 15.9 %collective-permute-start.20 = (bf16[320,768]{1,0:T(8,128)(2,1)S(1)}, bf16[320,768]{1,0:T(8,128)(2,1)S(1)}, u32[]{:S(2)}, u32[]{:S(2)}) collective-permute-start(bf16[320,768]{1,0:T(8,128)(2,1)S(1)} %pad_maximum_fusion.12), channel_id=1, source_target_pairs={{0,2},{1,3},{2,0},{3,1},{4,6},{5,7},{6,4},{7,5},{8,10},{9,11},{10,... | collective-permute-start | bytes 1474568 | tf_op jit(solution)/shard_map/ppermute | solution.py:83
  381.4 28.6 %collective-permute-start.18 = (bf16[320,768]{1,0:T(8,128)(2,1)S(1)}, bf16[320,768]{1,0:T(8,128)(2,1)S(1)}, u32[]{:S(2)}, u32[]{:S(2)}) collective-permute-start(bf16[320,768]{1,0:T(8,128)(2,1)S(1)} %pad_maximum_fusion.11), channel_id=1, source_target_pairs={{0,1},{1,0},{2,3},{3,2},{4,5},{5,4},{6,7},{7,6},{8,9},{9,8},{10,11... | collective-permute-start | bytes 1474568 | tf_op jit(solution)/shard_map/ppermute | solution.py:83
  383.9 28.8 %collective-permute-start.22 = (bf16[320,768]{1,0:T(8,128)(2,1)S(1)}, bf16[320,768]{1,0:T(8,128)(2,1)S(1)}, u32[]{:S(2)}, u32[]{:S(2)}) collective-permute-start(bf16[320,768]{1,0:T(8,128)(2,1)S(1)} %pad_maximum_fusion.13), channel_id=1, source_target_pairs={{0,1},{1,0},{2,3},{3,2},{4,5},{5,4},{6,7},{7,6},{8,9},{9,8},{10,11... | collective-permute-start | bytes 1474568 | tf_op jit(solution)/shard_map/ppermute | solution.py:83
  389.2 19.8 %collective-permute-start.13 = (bf16[160,768]{1,0:T(8,128)(2,1)S(1)}, bf16[160,768]{1,0:T(8,128)(2,1)S(1)}, u32[]{:S(2)}, u32[]{:S(2)}) collective-permute-start(bf16[160,768]{1,0:T(8,128)(2,1)S(1)} %add_convert_fusion.17), channel_id=1, source_target_pairs={{0,1},{1,0},{2,3},{3,2},{4,5},{5,4},{6,7},{7,6},{8,9},{9,8},{10,11... | collective-permute-start | bytes 737288 | tf_op jit(solution)/shard_map/ppermute | solution.py:83
  394.5 17.1 %collective-permute-start.17 = (bf16[160,768]{1,0:T(8,128)(2,1)S(1)}, bf16[160,768]{1,0:T(8,128)(2,1)S(1)}, u32[]{:S(2)}, u32[]{:S(2)}) collective-permute-start(bf16[160,768]{1,0:T(8,128)(2,1)S(1)} %add_convert_fusion.13), channel_id=1, source_target_pairs={{0,1},{1,0},{2,3},{3,2},{4,5},{5,4},{6,7},{7,6},{8,9},{9,8},{10,11... | collective-permute-start | bytes 737288 | tf_op jit(solution)/shard_map/ppermute | solution.py:83
  395.8 18.4 %collective-permute-start.21 = (bf16[160,768]{1,0:T(8,128)(2,1)S(1)}, bf16[160,768]{1,0:T(8,128)(2,1)S(1)}, u32[]{:S(2)}, u32[]{:S(2)}) collective-permute-start(bf16[160,768]{1,0:T(8,128)(2,1)S(1)} %add_convert_fusion.9), channel_id=1, source_target_pairs={{0,1},{1,0},{2,3},{3,2},{4,5},{5,4},{6,7},{7,6},{8,9},{9,8},{10,11... | collective-permute-start | bytes 737288 | tf_op jit(solution)/shard_map/ppermute | solution.py:83
  409.1 6.3 %collective-permute-start.15 = (bf16[160,768]{1,0:T(8,128)(2,1)S(1)}, bf16[160,768]{1,0:T(8,128)(2,1)S(1)}, u32[]{:S(2)}, u32[]{:S(2)}) collective-permute-start(bf16[160,768]{1,0:T(8,128)(2,1)S(1)} %get-tuple-element.90), channel_id=1, source_target_pairs={{0,2},{1,3},{2,0},{3,1},{4,6},{5,7},{6,4},{7,5},{8,10},{9,11},{10,... | collective-permute-start | bytes 737288 | tf_op jit(solution)/shard_map/ppermute | solution.py:83
  411.7 6.3 %collective-permute-start.19 = (bf16[160,768]{1,0:T(8,128)(2,1)S(1)}, bf16[160,768]{1,0:T(8,128)(2,1)S(1)}, u32[]{:S(2)}, u32[]{:S(2)}) collective-permute-start(bf16[160,768]{1,0:T(8,128)(2,1)S(1)} %get-tuple-element.96), channel_id=1, source_target_pairs={{0,2},{1,3},{2,0},{3,1},{4,6},{5,7},{6,4},{7,5},{8,10},{9,11},{10,... | collective-permute-start | bytes 737288 | tf_op jit(solution)/shard_map/ppermute | solution.py:83
  414.4 6.3 %collective-permute-start.23 = (bf16[160,768]{1,0:T(8,128)(2,1)S(1)}, bf16[160,768]{1,0:T(8,128)(2,1)S(1)}, u32[]{:S(2)}, u32[]{:S(2)}) collective-permute-start(bf16[160,768]{1,0:T(8,128)(2,1)S(1)} %get-tuple-element.102), channel_id=1, source_target_pairs={{0,2},{1,3},{2,0},{3,1},{4,6},{5,7},{6,4},{7,5},{8,10},{9,11},{10,... | collective-permute-start | bytes 737288 | tf_op jit(solution)/shard_map/ppermute | solution.py:83
  (99 other events, 986.3 us)

commit v2 on v1

--- a/solution.py
+++ b/solution.py
@@ -107,36 +107,6 @@
     for j in range(1 << bits):
         blocks += [halves[0][j], halves[1][j]]
     return jnp.concatenate(blocks)
-
-
-def scatter_blocks(whole):
-    bits = axis_bits("rows")
-    count = 1 << bits
-    block = whole.shape[0] // count
-    half = block // 2
-    results = []
-    for which, order in ((0, range(bits - 1, -1, -1)), (1, range(bits))):
-        held = {
-            j: whole[j * block + which * half : j * block + (which + 1) * half]
-            for j in range(count)
-        }
-        for bit in order:
-            sent_keys = sorted(key for key in held if key >> bit & 1)
-            sent = (
-                jnp.concatenate([held[key] for key in sent_keys])
-                if len(sent_keys) > 1
-                else held[sent_keys[0]]
-            )
-            got = swap(sent, "rows", 1 << bit)
-            held = {
-                key ^ (1 << bit): held[key ^ (1 << bit)].astype(F32)
-                + got[place * half : (place + 1) * half].astype(F32)
-                for place, key in enumerate(sent_keys)
-            }
-            if len(held) > 1:
-                held = {key: value.astype(BF) for key, value in held.items()}
-        results.append(held[0])
-    return jnp.concatenate(results)
 
 
 def add_low(first, second):
@@ -212,81 +182,6 @@
     )(info, queries, keyvals, keyvals)
 
 
-def attention_backward_kernel(
-    info_ref, q_ref, k_ref, v_ref, g_ref, o_ref, lse_ref, dq_ref, dk_ref, dv_ref, q4, g4, acc, *, kb
-):
-    t, n = q_ref.shape[0], k_ref.shape[0]
-    q4[...] = spread_heads(q_ref[...] * jnp.asarray(HEAD_DIM**-0.5, BF))
-    grads = spread_heads(g_ref[...])
-    g4[...] = grads
-    outs = jnp.concatenate([o_ref[...].astype(F32)] * HEADS_PER_GROUP, axis=0)
-    product = grads.astype(F32) * outs
-    high = product.astype(BF)
-    low = (product - high.astype(F32)).astype(BF)
-    ones = jnp.ones((8, GROUP), BF)
-    dots = (mm(ones, high, NT) + mm(ones, low, NT))[:1]
-    lse = lse_ref[0, :1, :]
-    acc[...] = jnp.zeros_like(acc)
-
-    def step(b, carry):
-        at = pl.ds(pl.multiple_of(b * kb, kb), kb)
-        keys, values = k_ref[at, :], v_ref[at, :]
-        index = b * kb + lax.broadcasted_iota(jnp.int32, (kb, 1), 0)
-        bias = key_bias(index, 0, n, t, info_ref)
-        scores = mm(keys, q4[...], NT)
-        probs = jnp.exp2((scores * LOG2E + bias) - lse)
-        grad_probs = mm(values, g4[...], NT)
-        grad_scores = (probs * (grad_probs - dots)).astype(BF)
-        dv_ref[at, :] = mm(probs.astype(BF), g4[...]).astype(BF)
-        dk_ref[at, :] = mm(grad_scores, q4[...]).astype(BF)
-        acc[...] += mm(grad_scores, keys, TN)
-        return carry
-
-    lax.fori_loop(0, n // kb, step, 0)
-    out = jnp.zeros((t, GROUP), F32)
-    for h in range(HEADS_PER_GROUP):
-        out = jnp.where(head_mask((t, GROUP), h), acc[pl.ds(h * t, t), :], out)
-    dq_ref[...] = (out * HEAD_DIM**-0.5).astype(BF)
-
-
-def attention_backward(info, queries, keyvals, grads, outs, lse):
-    t, d = queries.shape
-    n = keyvals.shape[0]
-    groups = d // GROUP
-    rows4 = HEADS_PER_GROUP * t
-    query_spec = pl.BlockSpec((t, GROUP), lambda i: (0, i))
-    key_spec = pl.BlockSpec((n, GROUP), lambda i: (0, i))
-    return pl.pallas_call(
-        functools.partial(attention_backward_kernel, kb=n // 2),
-        grid=(groups,),
-        in_specs=[
-            pl.BlockSpec(memory_space=pltpu.SMEM),
-            query_spec,
-            key_spec,
-            pl.BlockSpec((n, GROUP), lambda i: (0, i + groups)),
-            query_spec,
-            query_spec,
-            pl.BlockSpec((1, 8, rows4), lambda i: (i, 0, 0)),
-        ],
-        out_specs=[query_spec, key_spec, key_spec],
-        out_shape=[
-            jax.ShapeDtypeStruct((t, d), BF),
-            jax.ShapeDtypeStruct((n, d), BF),
-            jax.ShapeDtypeStruct((n, d), BF),
-        ],
-        scratch_shapes=[
-            pltpu.VMEM((rows4, GROUP), BF),
-            pltpu.VMEM((rows4, GROUP), BF),
-            pltpu.VMEM((rows4, GROUP), F32),
-        ],
-        compiler_params=pltpu.CompilerParams(vmem_limit_bytes=48 << 20),
-        cost_estimate=pl.CostEstimate(
-            flops=40 * t * n * d, bytes_accessed=8 * t * d + 8 * n * d, transcendentals=12 * t * n
-        ),
-        name="attention_backward",
-    )(info, queries, keyvals, keyvals, grads, outs, lse)
-
-
 WIDE = 48
 EDGES = 10
 FIELD_EDGE, TALL_EDGE = 4, 5
@@ -319,7 +214,10 @@
     items,
     rows,
     count,
+    depth,
 ):
+    bits = (count - 1).bit_length()
+    per_share = 9 * field_ref.shape[-1] // count // depth
     me = lax.axis_index("rows")
     here = lax.axis_index("items")
     channels = field_ref.shape[-1]
@@ -562,7 +460,14 @@
             block = jnp.concatenate(
                 [lhs(acts.at[conv], item, kr, rows) for item in range(items)], axis=0
             )
-            dw_ref[conv, pl.ds(kr * 3 * channels, 3 * channels), :] = mm(block, middle, TN).astype(BF)
+            weight = mm(block, middle, TN).astype(BF)
+            pieces = 3 * channels // depth
+            for k in range(pieces):
+                share, place = divmod(kr * pieces + k, per_share)
+                at = tuple(share >> b & 1 for b in range(bits - 1, -1, -1))
+                dw_ref[(conv,) + at + (slice(None), pl.ds(place * channels, channels))] = weight[
+                    k * depth : (k + 1) * depth
+                ]
         ones = jnp.ones((8, flat), BF)
         db_ref[pl.ds(conv, 1), :] = mm(ones, middle)[:1]
 
@@ -613,20 +518,25 @@
                 copy(e, side).wait_send()
 
 
-def refine(field, conv_weights, conv_biases, factor, offset, cotangent):
+def refine(field, conv_weights, conv_biases, factor, offset, cotangent, depth):
     items, rows, _, channels = field.shape
     count = lax.axis_size("rows")
     padded = jnp.pad(field, ((0, 0), (0, 0), (0, WIDE - PC), (0, 0)))
     vmem = pl.BlockSpec(memory_space=pltpu.VMEM)
     pixels = items * rows * PC
     outs = pl.pallas_call(
-        functools.partial(refine_kernel, items=items, rows=rows, count=count),
+        functools.partial(refine_kernel, items=items, rows=rows, count=count, depth=depth),
         in_specs=[vmem] * 6,
         out_specs=[vmem] * 5,
         out_shape=[
             jax.ShapeDtypeStruct((items, 2 * rows, 2 * PC, channels), BF),
             jax.ShapeDtypeStruct((items, rows, WIDE, channels), F32),
-            jax.ShapeDtypeStruct(conv_weights.shape, BF),
+            jax.ShapeDtypeStruct(
+                conv_weights.shape[:1]
+                + (2,) * axis_bits("rows")
+                + (depth, conv_weights.shape[1] // count // depth * channels),
+                BF,
+            ),
             jax.ShapeDtypeStruct(conv_biases.shape, F32),
             jax.ShapeDtypeStruct((2, items, channels), F32),
         ],
@@ -657,8 +567,6 @@
 
 
 MESH = pl.DeviceIdType.MESH
-STRIP = 256
-LAG = 3
 
 
 def flip(index, bit):
@@ -666,8 +574,9 @@
 
 
 class Reducer:
-    def __init__(self, chunks, depth, row_bits, item_bits):
-        self.chunks, self.depth = chunks, depth
+    def __init__(self, chunks, depth, strip, row_bits, item_bits, space, lag):
+        self.chunks, self.depth, self.lanes = chunks, depth, strip // 2
+        self.space, self.lag = space, lag
         self.row_bits, self.item_bits = row_bits, item_bits
         self.orders = (tuple(range(row_bits - 1, -1, -1)), tuple(range(row_bits)))
         self.far = max(item_bits - 2, 0)
@@ -677,27 +586,35 @@
         c, half = self.chunks, self.depth // 2
         shares = (2,) * self.row_bits
         slots = [
-            pltpu.VMEM((c,) + shares + (self.depth, 128), BF),
-            pltpu.VMEM((c,) + shares + (self.depth, 128), BF),
+            pltpu.VMEM((c,) + shares + (self.depth, self.lanes), BF),
+            pltpu.VMEM((2,) + shares + (self.depth, self.lanes), BF),
         ]
         for stage in range(self.row_bits):
             for _ in (0, 1):
-                slots.append(pltpu.VMEM((c,) + (2,) * (self.row_bits - 1 - stage) + (half, 128), BF))
-        slots.append(pltpu.VMEM((c, half, 128), BF))
+                slots.append(pltpu.VMEM((c,) + (2,) * (self.row_bits - 1 - stage) + (half, self.lanes), BF))
+        slots.append(pltpu.VMEM((c, half, self.lanes), BF))
         for _ in range(self.far):
-            slots.append(pltpu.VMEM((c, half, 128), BF))
-            slots.append(pltpu.VMEM((c, half, 128), BF))
-        arrivals = 1 + 1 + 2 * self.row_bits + 1 + self.far + 1 + 1
+            slots.append(pltpu.VMEM((c, half, self.lanes), BF))
+            slots.append(pltpu.VMEM((c, half, self.lanes), BF))
+        arrivals = 1 + 2 * self.row_bits + 1 + self.far + 1 + 1
         sends = 1 + 2 * self.row_bits + 1 + self.far + 1 + 1
-        return slots + [pltpu.SemaphoreType.DMA((arrivals, c)), pltpu.SemaphoreType.DMA((sends,))]
+        return slots + [
+            pltpu.VMEM((2, c, self.depth, self.lanes), BF),
+            pltpu.SemaphoreType.DMA((2,)),
+            pltpu.SemaphoreType.DMA((arrivals, c)),
+            pltpu.SemaphoreType.DMA((sends,)),
+        ]
+
+    def slots(self):
+        return len(self.scratch())
 
     def out_shape(self):
-        return jax.ShapeDtypeStruct((2, self.chunks, self.depth, 128), BF)
-
-    def bind(self, out_ref, slots):
+        return jax.ShapeDtypeStruct((2, self.chunks, self.depth, self.lanes), BF)
+
+    def bind(self, out_ref, slots, sources=None, held=None):
         slots = list(slots)
-        self.out = out_ref
-        self.mine, self.core_in = slots[0], slots[1]
+        self.result, self.sources, self.held = out_ref, sources, held
+        self.total, self.ring = slots[0], slots[1]
         self.row_in = [
             (slots[2 + 2 * stage], slots[3 + 2 * stage]) for stage in range(self.row_bits)
         ]
@@ -705,7 +622,7 @@
         self.near_in = rest[0]
         self.far_out = [rest[1 + 2 * k] for k in range(self.far)]
         self.far_in = [rest[2 + 2 * k] for k in range(self.far)]
-        self.recv_sem, self.send_sem = rest[-2], rest[-1]
+        self.out, self.ring_sem, self.recv_sem, self.send_sem = rest[-4:]
         self.me = lax.axis_index("rows")
         self.at = lax.axis_index("items")
         self.core = self.at % 2
@@ -731,14 +648,62 @@
             device_id_type=MESH,
         )
 
-    def first(self, view, column, chunk):
-        lead = (slice(None),) * (self.row_bits + 1)
-        theirs = view.at[lead + (pl.ds(pl.multiple_of(column + (1 - self.core) * 128, 128), 128),)]
-        ours = view.at[lead + (pl.ds(pl.multiple_of(column + self.core * 128, 128), 128),)]
-        self.remote(
-            theirs, self.core_in.at[chunk], 0, 0, chunk, (flip(self.at, 0), self.me)
-        ).start()
-        pltpu.make_async_copy(ours, self.mine.at[chunk], self.recv_sem.at[1, chunk]).start()
+    def strip(self, ref, index, mine):
+        side = self.core if mine else 1 - self.core
+        lanes = pl.ds(pl.multiple_of(side * self.lanes, self.lanes), self.lanes)
+        return ref.at[(index,) + (slice(None),) * (self.row_bits + 1) + (lanes,)]
+
+    def core_copy(self, source, chunk):
+        return self.remote(
+            source, self.total.at[chunk], 0, 0, chunk, (flip(self.at, 0), self.me)
+        )
+
+    def begin(self):
+        base = 0
+        for ref in self.sources:
+
+            def go(index, carry, ref=ref, base=base):
+                self.core_copy(self.strip(ref, index, False), base + index).start()
+                return carry
+
+            lax.fori_loop(0, ref.shape[0], go, 0)
+            base += ref.shape[0]
+        self.fetch(0)
+
+    def begin_held(self, chunk):
+        self.core_copy(self.strip(self.held, chunk, False), chunk).start()
+
+    def fetch(self, chunk):
+        base = 0
+        for ref in self.sources:
+
+            @pl.when((chunk >= base) & (chunk < base + ref.shape[0]))
+            def _(ref=ref, base=base):
+                index = jnp.clip(chunk - base, 0, ref.shape[0] - 1)
+                pltpu.make_async_copy(
+                    self.strip(ref, index, True),
+                    self.ring.at[chunk % 2],
+                    self.ring_sem.at[chunk % 2],
+                ).start()
+
+            base += ref.shape[0]
+
+    def add_mine(self, chunk):
+        if self.held is not None:
+            block = self.held[chunk]
+            side = (slice(None),) * (self.row_bits + 1)
+            block = jnp.where(
+                self.core == 0,
+                block[side + (slice(0, self.lanes),)],
+                block[side + (slice(self.lanes, None),)],
+            )
+        else:
+            slot = chunk % 2
+            pltpu.make_async_copy(
+                self.total.at[chunk], self.ring.at[slot], self.ring_sem.at[slot]
+            ).wait()
+            block = self.ring[slot]
+        self.total[chunk] = add_low(self.total[chunk], block)
 
     def bit(self, which):
         return self.me // (1 << which) % 2
@@ -757,11 +722,11 @@
         return pl.ds(half * depth, depth)
 
     def row_copy(self, stage, half, chunk):
-        source = self.mine.at[(chunk,) + self.shares(half, stage, True) + (self.rows(half),)]
+        source = self.total.at[(chunk,) + self.shares(half, stage, True) + (self.rows(half),)]
         return self.remote(
             source,
             self.row_in[stage][half].at[chunk],
-            2 + 2 * stage + half,
+            1 + 2 * stage + half,
             1 + 2 * stage + half,
             chunk,
             (self.at, flip(self.me, self.orders[half][stage])),
@@ -777,9 +742,9 @@
 
     def near_copy(self, chunk):
         return self.remote(
-            self.mine.at[self.own(chunk, self.near_rows(False))],
+            self.total.at[self.own(chunk, self.near_rows(False))],
             self.near_in.at[chunk],
-            2 + 2 * self.row_bits,
+            1 + 2 * self.row_bits,
             1 + 2 * self.row_bits,
             chunk,
             (flip(self.at, 1), self.me),
@@ -789,7 +754,7 @@
         return self.remote(
             self.far_out[k].at[chunk],
             self.far_in[k].at[chunk],
-            3 + 2 * self.row_bits + k,
+            2 + 2 * self.row_bits + k,
             2 + 2 * self.row_bits + k,
             chunk,
             (flip(self.at, 2 + k), self.me),
@@ -800,7 +765,7 @@
         return self.remote(
             place,
             place,
-            3 + 2 * self.row_bits + self.far,
+            2 + 2 * self.row_bits + self.far,
             2 + 2 * self.row_bits + self.far,
             chunk,
             (flip(self.at, 1), self.me),
@@ -811,7 +776,7 @@
         return self.remote(
             place,
             place,
-            4 + 2 * self.row_bits + self.far,
+            3 + 2 * self.row_bits + self.far,
             3 + 2 * self.row_bits + self.far,
             chunk,
             (flip(self.at, 0), self.me),
@@ -820,13 +785,14 @@
     def phase(self, number, chunk):
         bits, half = self.row_bits, self.depth // 2
         if number == 0:
-            self.remote(
-                self.core_in.at[chunk], self.core_in.at[chunk], 0, 0, chunk, (flip(self.at, 0), self.me)
-            ).wait_recv()
-            pltpu.make_async_copy(
-                self.core_in.at[chunk], self.mine.at[chunk], self.recv_sem.at[1, chunk]
-            ).wait()
-            self.mine[chunk] = add_low(self.mine[chunk], self.core_in[chunk])
+            self.core_copy(self.total.at[chunk], chunk).wait_recv()
+            self.add_mine(chunk)
+            if self.sources is not None:
+
+                @pl.when(chunk + 1 < self.chunks)
+                def _():
+                    self.fetch(chunk + 1)
+
             for side in (0, 1):
                 self.row_copy(0, side, chunk).start()
         elif number <= bits:
@@ -834,7 +800,7 @@
             for side in (0, 1):
                 self.row_copy(stage, side, chunk).wait_recv()
                 at = (chunk,) + self.shares(side, stage, False) + (self.rows(side),)
-                self.mine[at] = add_low(self.mine[at], self.row_in[stage][side][chunk])
+                self.total[at] = add_low(self.total[at], self.row_in[stage][side][chunk])
                 if stage + 1 < bits:
                     self.row_copy(stage + 1, side, chunk).start()
             if stage + 1 == bits:
@@ -842,7 +808,7 @@
         elif number == bits + 1:
             self.near_copy(chunk).wait_recv()
             total = add_low(
-                self.mine[self.own(chunk, self.near_rows(True))], self.near_in[chunk]
+                self.total[self.own(chunk, self.near_rows(True))], self.near_in[chunk]
             )
             self.pass_on(0, chunk, total)
         elif number <= bits + 1 + self.far:
@@ -868,7 +834,7 @@
         self.remote(
             place,
             place,
-            3 + 2 * self.row_bits + self.far,
+            2 + 2 * self.row_bits + self.far,
             2 + 2 * self.row_bits + self.far,
             chunk,
             (flip(self.at, 1), self.me),
@@ -879,7 +845,7 @@
         self.remote(
             place,
             place,
-            4 + 2 * self.row_bits + self.far,
+            3 + 2 * self.row_bits + self.far,
             3 + 2 * self.row_bits + self.far,
             chunk,
             (flip(self.at, 0), self.me),
@@ -887,21 +853,22 @@
 
     def step(self, t):
         for number in range(self.phases - 1, -1, -1):
-            chunk = t - LAG * number
-
-            @pl.when((chunk >= 0) & (chunk < self.chunks))
-            def _():
+            place = t - self.lag * number
+            chunk = place // self.space
+
+            @pl.when((place >= 0) & (place % self.space == 0) & (chunk < self.chunks))
+            def _(number=number, chunk=chunk):
                 self.phase(number, jnp.clip(chunk, 0, self.chunks - 1))
 
     @property
     def steps(self):
-        return self.chunks + LAG * (self.phases - 1)
+        return (self.chunks - 1) * self.space + self.lag * (self.phases - 1) + 1
 
     def finish(self):
         def drain(sem, ref):
             pltpu.make_async_copy(ref, ref, self.send_sem.at[sem]).wait()
 
-        drain(0, self.core_in)
+        drain(0, self.total)
         for stage in range(self.row_bits):
             for side in (0, 1):
                 drain(1 + 2 * stage + side, self.row_in[stage][side])
@@ -911,105 +878,676 @@
             drain(base + 1 + k, self.far_in[k])
         drain(base + 1 + self.far, self.near_in)
         drain(base + 2 + self.far, self.out.at[0])
-
-
-def chunk_list(arrays, depth):
-    found = []
-    for number, array in enumerate(arrays):
-        rows, columns = array.shape[-2:]
-        lead = array.shape[0] if array.ndim == 3 else None
-        for outer in range(lead or 1):
-            for row in range(0, rows // lax.axis_size("rows"), depth):
-                for column in range(0, columns, STRIP):
-                    found.append((number, outer if lead else None, row, column))
-    return found
-
-
-def reduce_kernel(*refs, reducer, table, arrays):
-    sources, out_ref, slots = refs[:arrays], refs[arrays], refs[arrays + 1 :]
-    reducer.bind(out_ref, slots)
-    reducer.greet()
-    lead = (slice(None),) * reducer.row_bits
-    for chunk, (number, outer, row, column) in enumerate(table):
-        ref = sources[number] if outer is None else sources[number].at[outer]
-        reducer.first(ref.at[lead + (pl.ds(row, reducer.depth), slice(None))], column, chunk)
-
-    def step(t, carry):
-        reducer.step(t)
-        return carry
-
-    lax.fori_loop(0, reducer.steps, step, 0)
-    reducer.finish()
-
-
-def share_views(arrays):
-    bits = axis_bits("rows")
-    views = []
-    for array in arrays:
-        lead = array.shape[:-2]
-        views.append(
-            array.reshape(lead + (2,) * bits + (array.shape[-2] >> bits, array.shape[-1]))
-        )
-    return views
-
-
-def reduce_all(arrays, depth, collective_id):
-    table = chunk_list(arrays, depth)
-    reducer = Reducer(len(table), depth, axis_bits("rows"), axis_bits("items"))
-    out = pl.pallas_call(
-        functools.partial(reduce_kernel, reducer=reducer, table=table, arrays=len(arrays)),
-        in_specs=[pl.BlockSpec(memory_space=pl.ANY)] * len(arrays),
-        out_specs=pl.BlockSpec(memory_space=pltpu.VMEM),
-        out_shape=reducer.out_shape(),
-        scratch_shapes=reducer.scratch(),
-        compiler_params=pltpu.CompilerParams(
-            vmem_limit_bytes=58 << 20, collective_id=collective_id, has_side_effects=True
-        ),
-        name="reduce_weights",
-    )(*share_views(arrays))
-    return unpack(out, arrays, table, depth)
-
-
-def unpack_kernel(held_ref, *refs, table, depth, outs):
+        copy = pltpu.make_async_copy(self.out, self.result, self.ring_sem.at[0])
+        copy.start()
+        copy.wait()
+
+
+def unpack_kernel(held_ref, *refs, table, outs):
     targets, (wide, sem) = refs[:outs], refs[outs:]
-
-    def copy(chunk, number, outer, row, column):
+    depth = wide.shape[1]
+
+    def copy(place, chunk, first, size, number, outer, row, column):
         target = targets[number] if outer is None else targets[number].at[outer]
         return pltpu.make_async_copy(
-            wide.at[chunk],
-            target.at[pl.ds(row, depth), pl.ds(column, STRIP)],
-            sem.at[chunk],
+            wide.at[chunk, :, pl.ds(first, size)],
+            target.at[pl.ds(row, depth), pl.ds(column, size)],
+            sem.at[place],
         )
 
-    for chunk, entry in enumerate(table):
-        wide[chunk] = jnp.concatenate(
-            [held_ref[0, chunk].astype(F32), held_ref[1, chunk].astype(F32)], axis=1
-        )
-        copy(chunk, *entry).start()
-    for chunk, entry in enumerate(table):
-        copy(chunk, *entry).wait()
-
-
-def unpack(out, arrays, table, depth):
-    count = lax.axis_size("rows")
-    shapes = [
-        jax.ShapeDtypeStruct(
-            array.shape[:-2] + (array.shape[-2] // count, array.shape[-1]), F32
-        )
-        for array in arrays
-    ]
+    done = set()
+    for place, entry in enumerate(table):
+        chunk = entry[0]
+        if chunk not in done:
+            done.add(chunk)
+            wide[chunk] = jnp.concatenate(
+                [held_ref[0, chunk].astype(F32), held_ref[1, chunk].astype(F32)], axis=1
+            )
+        copy(place, *entry).start()
+    for place, entry in enumerate(table):
+        copy(place, *entry).wait()
+
+
+def unpack(out, table, shapes):
+    chunks, depth, lanes = out.shape[1:]
     return pl.pallas_call(
-        functools.partial(unpack_kernel, table=table, depth=depth, outs=len(arrays)),
+        functools.partial(unpack_kernel, table=table, outs=len(shapes)),
         in_specs=[pl.BlockSpec(memory_space=pltpu.VMEM)],
-        out_specs=[pl.BlockSpec(memory_space=pl.ANY)] * len(arrays),
-        out_shape=shapes,
+        out_specs=[pl.BlockSpec(memory_space=pl.ANY)] * len(shapes),
+        out_shape=[jax.ShapeDtypeStruct(shape, F32) for shape in shapes],
         scratch_shapes=[
-            pltpu.VMEM((len(table), depth, STRIP), F32),
+            pltpu.VMEM((chunks, depth, 2 * lanes), F32),
             pltpu.SemaphoreType.DMA((len(table),)),
         ],
         compiler_params=pltpu.CompilerParams(vmem_limit_bytes=40 << 20),
         name="unpack",
     )(out)
+
+
+def all_sum_kernel(value_ref, out_ref, piece, landed, over, send_sem, recv_sem, *, count, others):
+    at, me = lax.axis_index("items"), lax.axis_index("rows")
+    barrier = pltpu.get_barrier_semaphore()
+    row_peers = [(at, (me + k) % count) for k in range(1, count)]
+    item_peers = [((at + k) % others, me) for k in range(1, others)]
+    for peer in row_peers + item_peers:
+        pl.semaphore_signal(barrier, inc=1, device_id=peer, device_id_type=MESH)
+    pl.semaphore_wait(barrier, count + others - 2)
+
+    def row_copy(k):
+        return pltpu.make_async_remote_copy(
+            src_ref=value_ref.at[row_peers[k][1]],
+            dst_ref=landed.at[k],
+            send_sem=send_sem.at[k],
+            recv_sem=recv_sem.at[k],
+            device_id=row_peers[k],
+            device_id_type=MESH,
+        )
+
+    def item_copy(k):
+        return pltpu.make_async_remote_copy(
+            src_ref=piece,
+            dst_ref=over.at[k],
+            send_sem=send_sem.at[count - 1 + k],
+            recv_sem=recv_sem.at[count - 1 + k],
+            device_id=item_peers[k],
+            device_id_type=MESH,
+        )
+
+    for k in range(count - 1):
+        row_copy(k).start()
+    total = value_ref[me]
+    for k in range(count - 1):
+        row_copy(k).wait_recv()
+        total = total + landed[k]
+    piece[...] = total
+    for k in range(others - 1):
+        item_copy(k).start()
+    for k in range(others - 1):
+        item_copy(k).wait_recv()
+        total = total + over[k]
+    out_ref[...] = total
+    for k in range(count - 1):
+        row_copy(k).wait_send()
+    for k in range(others - 1):
+        item_copy(k).wait_send()
+
+
+def all_sum(value, collective_id):
+    count, others = lax.axis_size("rows"), lax.axis_size("items")
+    vmem = pl.BlockSpec(memory_space=pltpu.VMEM)
+    block = value.shape[1:]
+    return pl.pallas_call(
+        functools.partial(all_sum_kernel, count=count, others=others),
+        in_specs=[vmem],
+        out_specs=vmem,
+        out_shape=jax.ShapeDtypeStruct(block, F32),
+        scratch_shapes=[
+            pltpu.VMEM(block, F32),
+            pltpu.VMEM((count - 1,) + block, F32),
+            pltpu.VMEM((others - 1,) + block, F32),
+            pltpu.SemaphoreType.DMA((count + others - 2,)),
+            pltpu.SemaphoreType.DMA((count + others - 2,)),
+        ],
+        compiler_params=pltpu.CompilerParams(collective_id=collective_id, has_side_effects=True),
+        name="sum_small",
+    )(value)
+
+
+def shares_of(bits):
+    return (2,) * bits
+
+
+def mlp_backward_kernel(
+    tap_grad_ref,
+    cot_ref,
+    out_tokens_ref,
+    normed_ref,
+    resid_ref,
+    attended_ref,
+    gain_ref,
+    tap_w_ref,
+    out_w_ref,
+    hidden_ref,
+    slope_ref,
+    fc1_ref,
+    fc2_ref,
+    tap_dw_ref,
+    out_dw_ref,
+    fc1_dw_ref,
+    fc2_dw_ref,
+    resid_grad_ref,
+    attended_grad_ref,
+    wide_sums_ref,
+    fc1_sums_ref,
+    out_grad,
+    low_grad,
+    pre_grad,
+    back,
+    *,
+    blocks,
+    row_block,
+    bits,
+):
+    step = pl.program_id(0)
+    tokens, width = low_grad.shape
+    count = 1 << bits
+    depth = width // count
+    shares = shares_of(bits)
+    pieces = [pl.ds(k * row_block, row_block) for k in range(tokens // row_block)]
+
+    @pl.when(step == 0)
+    def _():
+        total = jnp.zeros((1, width), F32)
+        tap_total = jnp.zeros((1, tap_grad_ref.shape[1]), F32)
+        for piece in pieces:
+            tap_part = tap_grad_ref[piece, :]
+            value = cot_ref[piece, :].astype(F32) + mm(tap_part, tap_w_ref[...], NT)
+            out_grad[piece, :] = value
+            low = value.astype(BF)
+            low_grad[piece, :] = low
+            back[piece, :] = jnp.zeros((row_block, width), F32)
+            total = total + jnp.sum(low.astype(F32), axis=0, keepdims=True)
+            tap_total = tap_total + jnp.sum(tap_part.astype(F32), axis=0, keepdims=True)
+        wide_sums_ref[pl.ds(0, 1), :] = total
+        wide_sums_ref[pl.ds(4, 1), :] = jnp.concatenate(
+            [tap_total] * (width // tap_total.shape[1]), axis=1
+        )
+        weight = mm(out_tokens_ref[...], tap_grad_ref[...], TN).astype(BF)
+        weight = jnp.concatenate(
+            [weight, jnp.zeros((width, width - weight.shape[1]), BF)], axis=1
+        )
+        tap_dw_ref[0] = weight.reshape(shares + (depth, width))
+
+    def rows_of(number):
+        return pl.ds(pl.multiple_of(number * row_block, row_block), row_block)
+
+    def inward(number, sums):
+        piece = rows_of(number)
+        grads = mm(low_grad[piece, :], fc2_ref[...], NT) * slope_ref[piece, :].astype(F32)
+        low = grads.astype(BF)
+        pre_grad[piece, :] = low
+        return sums + jnp.sum(low.astype(F32), axis=0, keepdims=True)
+
+    fc1_sums_ref[...] = lax.fori_loop(
+        0, len(pieces), inward, jnp.zeros((1, pre_grad.shape[1]), F32)
+    )
+    weight = mm(hidden_ref[...], low_grad[...], TN).astype(BF)
+    per_share = weight.shape[0] // depth * blocks // count
+    for place in range(weight.shape[0] // depth):
+        fc2_dw_ref[place % per_share, place // per_share] = weight[
+            place * depth : (place + 1) * depth
+        ]
+    weight = mm(normed_ref[...], pre_grad[...], TN).astype(BF)
+    fc1_dw_ref[0] = weight.reshape(shares + (depth, width))
+
+    def outward(number, carry):
+        piece = rows_of(number)
+        back[piece, :] += mm(pre_grad[piece, :], fc1_ref[...], NT)
+        return carry
+
+    lax.fori_loop(0, len(pieces), outward, 0)
+
+    @pl.when(step == blocks - 1)
+    def _():
+        gain = gain_ref[...]
+        gain_total = jnp.zeros((1, width), F32)
+        shift_total = jnp.zeros((1, width), F32)
+        total = jnp.zeros((1, width), F32)
+        for piece in pieces:
+            grads = back[piece, :]
+            unit, rstd = norm_stats(resid_ref[piece, :])
+            scaled = grads * gain
+            mean_one = jnp.mean(scaled, axis=-1, keepdims=True)
+            mean_two = jnp.mean(scaled * unit, axis=-1, keepdims=True)
+            value = out_grad[piece, :] + rstd * (scaled - mean_one - unit * mean_two)
+            resid_grad_ref[piece, :] = value
+            low = value.astype(BF)
+            low_grad[piece, :] = low
+            gain_total = gain_total + jnp.sum(grads * unit, axis=0, keepdims=True)
+            shift_total = shift_total + jnp.sum(grads, axis=0, keepdims=True)
+            total = total + jnp.sum(low.astype(F32), axis=0, keepdims=True)
+            attended_grad_ref[piece, :] = mm(low, out_w_ref[...], NT).astype(BF)
+        wide_sums_ref[pl.ds(1, 1), :] = gain_total
+        wide_sums_ref[pl.ds(2, 1), :] = shift_total
+        wide_sums_ref[pl.ds(3, 1), :] = total
+        weight = mm(attended_ref[...], low_grad[...], TN).astype(BF)
+        out_dw_ref[0] = weight.reshape(shares + (depth, width))
+
+
+def mlp_backward(
+    grad_tap,
+    cotangent,
+    out_tokens,
+    normed,
+    resid,
+    attended,
+    gain,
+    tap_weight,
+    out_weight,
+    hidden,
+    slope,
+    fc1_weight,
+    fc2_weight,
+    row_block,
+):
+    tokens, width = resid.shape
+    inner = hidden.shape[1]
+    bits = axis_bits("rows")
+    count = 1 << bits
+    depth = width // count
+    blocks = inner // width
+    vmem = pl.BlockSpec(memory_space=pltpu.VMEM)
+    column = pl.BlockSpec((tokens, width), lambda i: (0, i))
+    fc2_chunks = inner // count // depth
+    shares = shares_of(bits)
+    share_step = count // blocks
+    outs = pl.pallas_call(
+        functools.partial(
+            mlp_backward_kernel,
+            blocks=blocks,
+            row_block=row_block,
+            bits=bits,
+        ),
+        grid=(blocks,),
+        in_specs=[vmem] * 9
+        + [
+            column,
+            column,
+            pl.BlockSpec((width, width), lambda i: (0, i)),
+            pl.BlockSpec((width, width), lambda i: (i, 0)),
+        ],
+        out_specs=[
+            vmem,
+            vmem,
+            pl.BlockSpec((1,) + shares + (depth, width), lambda i: (i,) + (0,) * (bits + 2)),
+            pl.BlockSpec((fc2_chunks, share_step, depth, width), lambda i: (0, i, 0, 0)),
+            vmem,
+            vmem,
+            vmem,
+            pl.BlockSpec((1, width), lambda i: (0, i)),
+        ],
+        out_shape=[
+            jax.ShapeDtypeStruct((1,) + shares + (depth, width), BF),
+            jax.ShapeDtypeStruct((1,) + shares + (depth, width), BF),
+            jax.ShapeDtypeStruct((blocks,) + shares + (depth, width), BF),
+            jax.ShapeDtypeStruct((fc2_chunks, count, depth, width), BF),
+            jax.ShapeDtypeStruct((tokens, width), F32),
+            jax.ShapeDtypeStruct((tokens, width), BF),
+            jax.ShapeDtypeStruct((8, width), F32),
+            jax.ShapeDtypeStruct((1, inner), F32),
+        ],
+        scratch_shapes=[
+            pltpu.VMEM((tokens, width), F32),
+            pltpu.VMEM((tokens, width), BF),
+            pltpu.VMEM((tokens, width), BF),
+            pltpu.VMEM((tokens, width), F32),
+        ],
+        compiler_params=pltpu.CompilerParams(vmem_limit_bytes=60 << 20),
+        cost_estimate=pl.CostEstimate(
+            flops=8 * tokens * width * inner, bytes_accessed=40 << 20, transcendentals=0
+        ),
+        name="mlp_backward",
+    )(
+        grad_tap,
+        cotangent,
+        out_tokens,
+        normed,
+        resid,
+        attended,
+        gain,
+        tap_weight,
+        out_weight,
+        hidden,
+        slope,
+        fc1_weight,
+        fc2_weight,
+    )
+    return outs
+
+
+class Scatter:
+    def __init__(self, bits, tokens, width, items):
+        self.bits, self.tokens, self.width, self.items = bits, tokens, width, items
+        self.orders = (tuple(range(bits - 1, -1, -1)), tuple(range(bits)))
+
+    def scratch(self):
+        slots = [pltpu.VMEM((2,) * self.bits + (self.tokens, self.width), BF)]
+        for stage in range(self.bits):
+            for _ in (0, 1):
+                slots.append(
+                    pltpu.VMEM(
+                        (self.items,)
+                        + (2,) * (self.bits - 1 - stage)
+                        + (self.tokens // 2, self.width),
+                        BF,
+                    )
+                )
+        return slots + [
+            pltpu.SemaphoreType.DMA((self.bits, 2)),
+            pltpu.SemaphoreType.DMA((self.items, self.bits, 2)),
+        ]
+
+    def bind(self, slots):
+        self.held = slots[0]
+        self.landed = [(slots[1 + 2 * s], slots[2 + 2 * s]) for s in range(self.bits)]
+        self.send_sem, self.recv_sem = slots[-2:]
+
+    def place(self, half, stage, bit_value):
+        index = [slice(None)] * self.bits
+        for done in self.orders[half][:stage]:
+            index[self.bits - 1 - done] = 0
+        index[self.bits - 1 - self.orders[half][stage]] = bit_value
+        size = self.tokens // 2
+        return tuple(index) + (pl.ds(half * size, size),)
+
+    def copy(self, item, stage, half):
+        me, at = lax.axis_index("rows"), lax.axis_index("items")
+        return pltpu.make_async_remote_copy(
+            src_ref=self.held.at[self.place(half, stage, 1)],
+            dst_ref=self.landed[stage][half].at[item],
+            send_sem=self.send_sem.at[stage, half],
+            recv_sem=self.recv_sem.at[item, stage, half],
+            device_id=(at, flip(me, self.orders[half][stage])),
+            device_id_type=MESH,
+        )
+
+    def start(self, item):
+        for half in (0, 1):
+            self.copy(item, 0, half).start()
+
+    def advance(self, item, stage, finish):
+        for half in (0, 1):
+            self.copy(item, stage, half).wait_recv()
+            at = self.place(half, stage, 0)
+            if stage + 1 < self.bits:
+                self.held[at] = add_low(self.held[at], self.landed[stage][half][item])
+                self.copy(item, stage + 1, half).start()
+            else:
+                finish(
+                    at[-1],
+                    self.held[at].astype(F32) + self.landed[stage][half][item].astype(F32),
+                )
+
+    def drain(self, item):
+        for stage in range(self.bits):
+            for half in (0, 1):
+                self.copy(item, stage, half).wait_send()
+
+
+def attention_backward_kernel(
+    valid_ref,
+    q_ref,
+    k_ref,
+    v_ref,
+    g_ref,
+    o_ref,
+    lse_ref,
+    normed_ref,
+    wq_ref,
+    wk_ref,
+    wv_ref,
+    *refs,
+    reducer,
+    late,
+    scatter,
+    groups,
+    items,
+    kb,
+    rounds,
+    sources,
+):
+    early_sources = refs[:sources]
+    grad_ref, sums_ref, early_out, late_out = refs[sources : sources + 4]
+    slots = list(refs[sources + 4 :])
+    q4, g4, acc, dkv, back, held = slots[:6]
+    del slots[:6]
+    early_slots = slots[: reducer.slots()]
+    del slots[: reducer.slots()]
+    late_slots = slots[: late.slots()]
+    del slots[: late.slots()]
+    reducer.bind(early_out, early_slots, sources=early_sources)
+    late.bind(late_out, late_slots, held=held)
+    scatter.bind(slots)
+    step = pl.program_id(0)
+    item, group = step // groups, step % groups
+    t, n = q_ref.shape[1], k_ref.shape[1]
+    width = back.shape[1]
+    depth = width // (1 << reducer.row_bits)
+    shares = shares_of(reducer.row_bits)
+    me = lax.axis_index("rows")
+
+    @pl.when(step == 0)
+    def _():
+        reducer.greet()
+        reducer.begin()
+        sums_ref[...] = jnp.zeros_like(sums_ref)
+
+    q4[...] = spread_heads(q_ref[0] * jnp.asarray(HEAD_DIM**-0.5, BF))
+    grads = spread_heads(g_ref[0])
+    g4[...] = grads
+    outs = jnp.concatenate([o_ref[0].astype(F32)] * HEADS_PER_GROUP, axis=0)
+    product = grads.astype(F32) * outs
+    high = product.astype(BF)
+    low = (product - high.astype(F32)).astype(BF)
+    ones = jnp.ones((8, GROUP), BF)
+    dots = (mm(ones, high, NT) + mm(ones, low, NT))[:1]
+    lse = lse_ref[0, 0, :1, :]
+    acc[...] = jnp.zeros_like(acc)
+    limit = valid_ref[item] * PC
+
+    def turn(number):
+        now = step * rounds + number
+        reducer.step(now)
+        late.step(now - ((items - 1) * groups + 1) * rounds)
+
+    inner = n // kb
+    each = rounds // inner
+
+    def block_step(b, carry):
+        at = pl.ds(pl.multiple_of(b * kb, kb), kb)
+        keys, values = k_ref[0, at, :], v_ref[0, at, :]
+        index = b * kb + lax.broadcasted_iota(jnp.int32, (kb, 1), 0)
+        position = index + key_shift(index, n, t, me)
+        bias = jnp.where(position < limit, 0.0, MASKED).astype(F32)
+        scores = mm(keys, q4[...], NT)
+        probs = jnp.exp2((scores * LOG2E + bias) - lse)
+        grad_probs = mm(values, g4[...], NT)
+        grad_scores = (probs * (grad_probs - dots)).astype(BF)
+        dkv[at, pl.ds(GROUP, GROUP)] = mm(probs.astype(BF), g4[...]).astype(BF)
+        dkv[at, pl.ds(0, GROUP)] = mm(grad_scores, q4[...]).astype(BF)
+        acc[...] += mm(grad_scores, keys, TN)
+
+        def rest(k, inner_carry):
+            turn(b * each + k)
+            return inner_carry
+
+        lax.fori_loop(0, each, rest, 0)
+        return carry
+
+    lax.fori_loop(0, inner, block_step, 0)
+    out = jnp.zeros((t, GROUP), F32)
+    for h in range(HEADS_PER_GROUP):
+        out = jnp.where(head_mask((t, GROUP), h), acc[pl.ds(h * t, t), :], out)
+    dq = (out * HEAD_DIM**-0.5).astype(BF)
+
+    for stage in range(scatter.bits):
+
+        @pl.when((group == stage) & (item > 0))
+        def _(stage=stage):
+            def finish(rows, value):
+                grad_ref[item - 1, rows, :] += value
+
+            scatter.advance(item - 1, stage, finish)
+
+    row_piece = n // 4
+    both = jnp.concatenate([wk_ref[...], wv_ref[...]], axis=1)
+
+    def project(k, carry):
+        at = pl.ds(pl.multiple_of(k * row_piece, row_piece), row_piece)
+        value = mm(dkv[at, :], both, NT)
+        back[at, :] = jnp.where(group == 0, value, back[at, :] + value)
+        return carry
+
+    lax.fori_loop(0, 4, project, 0)
+    value = mm(dq, wq_ref[...], NT)
+    grad_ref[item] = jnp.where(group == 0, value, grad_ref[item] + value)
+
+    part = jnp.concatenate(
+        [mm(normed_ref[0, pl.ds(0, t), :], dq, TN), mm(normed_ref[0], dkv[...], TN)], axis=1
+    ).reshape(shares + (depth, width))
+    before = held[group].astype(F32)
+    held[group] = jnp.where(item == 0, part, before + part).astype(BF)
+    sums_ref[group, pl.ds(0, 1), :] += jnp.sum(dq.astype(F32), axis=0, keepdims=True)
+    sums_ref[group, pl.ds(1, 1), :] += jnp.sum(
+        dkv[:, pl.ds(GROUP, GROUP)].astype(F32), axis=0, keepdims=True
+    )
+
+    @pl.when(item == items - 1)
+    def _():
+        late.begin_held(group)
+
+    @pl.when(group == groups - 1)
+    def _():
+        @pl.when(item > 0)
+        def _():
+            scatter.drain(item - 1)
+
+        for j in range(1 << scatter.bits):
+            index = tuple(j >> b & 1 for b in range(scatter.bits - 1, -1, -1))
+            scatter.held[index] = back[pl.ds(j * t, t), :].astype(BF)
+        scatter.start(item)
+
+    @pl.when(step == items * groups - 1)
+    def _():
+        start = ((items - 1) * groups + 1) * rounds
+
+        def rest(now, carry):
+            @pl.when(now < reducer.steps)
+            def _():
+                reducer.step(now)
+
+            late.step(now - start)
+            return carry
+
+        last = items * groups * rounds
+        end = start + late.steps
+        lax.fori_loop(last, last + late.lag, rest, 0)
+        for stage in range(scatter.bits):
+
+            def finish(rows, value):
+                grad_ref[items - 1, rows, :] += value
+
+            scatter.advance(items - 1, stage, finish)
+        lax.fori_loop(last + late.lag, max(end, reducer.steps), rest, 0)
+        scatter.drain(items - 1)
+        reducer.finish()
+        late.finish()
+
+
+def key_shift(index, length, block, me):
+    start = jnp.full_like(index, me * block)
+    for j in range(1, length // block):
+        other = me
+        for bit in range(j.bit_length()):
+            if j >> bit & 1:
+                other = flip(other, bit)
+        start = jnp.where(index >= j * block, (other - j) * block, start)
+    return start
+
+
+def attention_backward(
+    valid_rows, queries, keyvals, grads, outs, lse, normed, qkv_weight, packed, collective_id
+):
+    items, t, d = queries.shape
+    n = keyvals.shape[1]
+    groups = d // GROUP
+    bits = axis_bits("rows")
+    depth = d >> bits
+    rows4 = HEADS_PER_GROUP * t
+    rounds = 8
+    reducer = Reducer(
+        sum(a.shape[0] for a in packed), depth, d, bits, axis_bits("items"), 4, 5
+    )
+    late = Reducer(groups, depth, d, bits, axis_bits("items"), rounds, 4)
+    scatter = Scatter(bits, t, d, items)
+    query_spec = pl.BlockSpec((1, t, GROUP), lambda i: (i // groups, 0, i % groups))
+    vmem = pl.BlockSpec(memory_space=pltpu.VMEM)
+
+    def weight_spec(kind):
+        return pl.BlockSpec((d, GROUP), lambda i: (0, kind * groups + i % groups))
+
+    def key_spec(kind):
+        return pl.BlockSpec((1, n, GROUP), lambda i: (i // groups, 0, kind * groups + i % groups))
+
+    outs = pl.pallas_call(
+        functools.partial(
+            attention_backward_kernel,
+            reducer=reducer,
+            late=late,
+            scatter=scatter,
+            groups=groups,
+            items=items,
+            kb=n // 4,
+            rounds=rounds,
+            sources=len(packed),
+        ),
+        grid=(items * groups,),
+        in_specs=[
+            pl.BlockSpec(memory_space=pltpu.SMEM),
+            query_spec,
+            key_spec(0),
+            key_spec(1),
+            query_spec,
+            query_spec,
+            pl.BlockSpec((1, 1, 8, rows4), lambda i: (i // groups, i % groups, 0, 0)),
+            pl.BlockSpec((1, n, d), lambda i: (i // groups, 0, 0), pipeline_mode=pl.Buffered(1)),
+            weight_spec(0),
+            weight_spec(1),
+            weight_spec(2),
+        ]
+        + [pl.BlockSpec(memory_space=pl.ANY)] * len(packed),
+        out_specs=[vmem] * 2 + [pl.BlockSpec(memory_space=pl.ANY)] * 2,
+        out_shape=[
+            jax.ShapeDtypeStruct((items, t, d), F32),
+            jax.ShapeDtypeStruct((groups, 8, GROUP), F32),
+            reducer.out_shape(),
+            late.out_shape(),
+        ],
+        scratch_shapes=[
+            pltpu.VMEM((rows4, GROUP), BF),
+            pltpu.VMEM((rows4, GROUP), BF),
+            pltpu.VMEM((rows4, GROUP), F32),
+            pltpu.VMEM((n, 2 * GROUP), BF),
+            pltpu.VMEM((n, d), F32),
+            pltpu.VMEM((groups,) + shares_of(bits) + (depth, d), BF),
+        ]
+        + reducer.scratch()
+        + late.scratch()
+        + scatter.scratch(),
+        compiler_params=pltpu.CompilerParams(
+            vmem_limit_bytes=63 << 20, collective_id=collective_id, has_side_effects=True
+        ),
+        cost_estimate=pl.CostEstimate(
+            flops=100 * items * t * n * d,
+            bytes_accessed=40 << 20,
+            transcendentals=12 * items * t * n,
+        ),
+        name="attention_backward",
+    )(
+        valid_rows,
+        queries,
+        keyvals,
+        keyvals,
+        grads,
+        outs,
+        lse,
+        normed,
+        qkv_weight,
+        qkv_weight,
+        qkv_weight,
+        *packed,
+    )
+    return outs
 
 
 def shards(
@@ -1087,106 +1625,128 @@
     shift_pick = jnp.dot(choose, table_shift, precision=highest)
     factor = 1.0 + flag_value * (gain_pick - 1.0)
     offset = flag_value * shift_pick
+    depth = width // row_count
     joined, grad_field, conv_grads, grad_conv_biases, table_sums = refine(
-        field, conv_weights, conv_biases, factor, offset, joined_cotangent
+        field, conv_weights, conv_biases, factor, offset, joined_cotangent, depth
     )
     grad_table_gain = jnp.dot(choose.T, flag_value * table_sums[0], precision=highest)
     grad_table_shift = jnp.dot(choose.T, flag_value * table_sums[1], precision=highest)
-    grad_field = grad_field[:, :, :PC]
-    grad_tap = (grad_field.reshape(-1, channels) * token_valid).astype(BF)
-    tap_grad = mm(output_low, grad_tap, TN).astype(BF)
-    grad_tap_bias = jnp.sum(grad_tap.astype(F32), axis=0)
-    grad_output = token_cotangent.reshape(-1, width).astype(F32) + mm(grad_tap, tap_weight, NT)
-    grad_mlp = grad_output.astype(BF)
-    fc2_grad = mm(hidden, grad_mlp, TN).astype(BF)
-    grad_fc2_bias = jnp.sum(grad_mlp.astype(F32), axis=0)
-    grad_pre = (mm(grad_mlp, fc2_weight, NT) * hidden_slope.astype(F32)).astype(BF)
-    fc1_grad = mm(normed_two, grad_pre, TN).astype(BF)
-    grad_fc1_bias = jnp.sum(grad_pre.astype(F32), axis=0)
-    grad_normed_two = mm(grad_pre, fc1_weight, NT)
-    grad_resid_norm, grad_gain_two, grad_shift_two = norm_back(
-        resid, norm_gains[1], grad_normed_two
+
+    grad_tap = (grad_field[:, :, :PC].reshape(-1, channels) * token_valid).astype(BF)
+    (
+        tap_grads,
+        out_grads,
+        fc1_grads,
+        fc2_grads,
+        grad_resid,
+        grad_attended,
+        wide_sums,
+        fc1_sums,
+    ) = mlp_backward(
+        grad_tap,
+        token_cotangent.reshape(-1, width),
+        output_low,
+        normed_two,
+        resid,
+        attended_flat,
+        norm_gains[1:2],
+        tap_weight,
+        out_weight,
+        hidden,
+        hidden_slope,
+        fc1_weight,
+        fc2_weight,
+        tok_here,
     )
-    grad_resid = grad_output + grad_resid_norm
-    grad_branch = grad_resid.astype(BF)
-    out_grad = mm(attended_flat, grad_branch, TN).astype(BF)
-    grad_out_bias = jnp.sum(grad_branch.astype(F32), axis=0)
-    grad_attended = mm(grad_branch, out_weight, NT).astype(BF)
-
-    grads_q, grads_k, grads_v, grads_in = [], [], [], []
-    for i in range(items_here):
-        here = slice(i * tok_here, (i + 1) * tok_here)
-        grad_q, grad_k, grad_v = attention_backward(
-            infos[i], queries[i], keyvals[i], grad_attended[here], attended[i], lses[i]
-        )
-        partial = (
-            mm(grad_k, qkv_weight[:, width : 2 * width], NT)
-            + mm(grad_v, qkv_weight[:, 2 * width :], NT)
-        ).astype(BF)
-        own = mm(grad_q, qkv_weight[:, :width], NT)
-        grads_in.append(scatter_blocks(partial) + own)
-        grads_q.append(grad_q)
-        grads_k.append(grad_k)
-        grads_v.append(grad_v)
-    grad_q = jnp.concatenate(grads_q)
-    every_norm = jnp.concatenate(normed_all)
-    every_k = jnp.concatenate(grads_k)
-    every_v = jnp.concatenate(grads_v)
-    q_grad = mm(normed_one, grad_q, TN).astype(BF)
-    k_grad = mm(every_norm, every_k, TN).astype(BF)
-    v_grad = mm(every_norm, every_v, TN).astype(BF)
-    qkv_grad = jnp.concatenate([q_grad, k_grad, v_grad], axis=1)
-    grad_q_bias = jnp.sum(grad_q.astype(F32), axis=0)
-    grad_v_bias = jnp.sum(every_v.astype(F32), axis=0)
+    shares = shares_of(axis_bits("rows"))
+    fc2_grads = fc2_grads.reshape(fc2_grads.shape[:1] + shares + fc2_grads.shape[2:])
+    grads_in, qkv_sums, early_sum, late_sum = attention_backward(
+        valid_rows,
+        jnp.stack(queries),
+        jnp.stack(keyvals),
+        grad_attended.reshape(tokens.shape),
+        attended_flat.reshape(tokens.shape),
+        jnp.stack(lses),
+        jnp.stack(normed_all),
+        qkv_weight,
+        [conv_grads, tap_grads, fc2_grads, fc1_grads, out_grads],
+        3,
+    )
     grad_in_norm, grad_gain_one, grad_shift_one = norm_back(
-        flat_in, norm_gains[0], jnp.concatenate(grads_in)
+        flat_in, norm_gains[0], grads_in.reshape(-1, width)
     )
     grad_tokens = (grad_resid + grad_in_norm).reshape(tokens.shape)
 
+    groups = width // GROUP
+    inner = fc1_weight.shape[1]
+    kernels = conv_weights.shape[1]
+    convs = conv_weights.shape[0]
+    places = kernels // row_count // depth
+    fc2_chunks = inner // row_count // depth
+    blocks = inner // width
+    table = [
+        (conv, place * channels, channels, 0, conv, place * depth, 0)
+        for conv in range(convs)
+        for place in range(places)
+    ]
+    table += [(convs, 0, channels, 1, None, 0, 0)]
+    first = convs + 1
+    table += [(first + k, 0, width, 2, None, k * depth, 0) for k in range(fc2_chunks)]
+    first += fc2_chunks
+    table += [(first + k, 0, width, 3, None, 0, k * width) for k in range(blocks)]
+    table += [(first + blocks, 0, width, 4, None, 0, 0)]
+    share_conv, share_tap, share_fc2, share_fc1, share_out = unpack(
+        early_sum,
+        table,
+        [
+            (convs, kernels // row_count, channels),
+            (depth, channels),
+            (inner // row_count, width),
+            (depth, inner),
+            (depth, width),
+        ],
+    )
+    (share_qkv,) = unpack(
+        late_sum,
+        [
+            (group, kind * GROUP, GROUP, 0, None, 0, (kind * groups + group) * GROUP)
+            for group in range(groups)
+            for kind in range(3)
+        ],
+        [(depth, 3 * width)],
+    )
+
     small = [
-        (jnp.stack([grad_gain_one, grad_gain_two]), 1),
-        (jnp.stack([grad_shift_one, grad_shift_two]), 1),
-        (jnp.concatenate([grad_q_bias, grad_v_bias]), 0),
-        (grad_out_bias, 0),
-        (grad_fc1_bias, 0),
-        (grad_fc2_bias, 0),
-        (grad_tap_bias, 0),
-        (grad_conv_biases, 1),
-        (grad_table_gain, 1),
-        (grad_table_shift, 1),
+        jnp.stack([grad_gain_one, wide_sums[1]]),
+        jnp.stack([grad_shift_one, wide_sums[2]]),
+        jnp.concatenate([qkv_sums[:, 0].reshape(-1), qkv_sums[:, 1].reshape(-1)]),
+        wide_sums[3],
+        fc1_sums[0],
+        wide_sums[0],
+        wide_sums[4, :channels],
+        grad_conv_biases,
+        grad_table_gain,
+        grad_table_shift,
     ]
-    packed, shapes = [], []
-    for array, dim in small:
-        if array.ndim == 1:
-            pieces = array.reshape(row_count, -1)
-        else:
-            pieces = jnp.swapaxes(
-                array.reshape(array.shape[0], row_count, -1), 0, 1
-            ).reshape(row_count, -1)
-        shapes.append((array.ndim, array.shape[0], pieces.shape[1]))
-        packed.append(pieces)
-    packed = jnp.concatenate(packed, axis=1)
-    depth = width // row_count
-    size = packed.shape[1]
-    packed = jnp.pad(packed, ((0, 0), (0, depth * STRIP - size))).astype(BF)
-    packed = packed.reshape(row_count * depth, STRIP)
-    (
-        share_conv,
-        share_tap,
-        share_fc2,
-        share_fc1,
-        share_out,
-        share_qkv,
-        summed,
-    ) = reduce_all(
-        [conv_grads, tap_grad, fc2_grad, fc1_grad, out_grad, qkv_grad, packed], depth, 1
+    packed = jnp.concatenate(
+        [
+            array.reshape(row_count, -1)
+            if array.ndim == 1
+            else jnp.swapaxes(array.reshape(array.shape[0], row_count, -1), 0, 1).reshape(
+                row_count, -1
+            )
+            for array in small
+        ],
+        axis=1,
     )
-    summed = summed.reshape(-1)
+    packed = jnp.pad(packed, ((0, 0), (0, -packed.shape[1] % 1024)))
+    summed = all_sum(packed.reshape(row_count, -1, 128), 4).reshape(-1)
     outs, place = [], 0
-    for ndim, lead, length in shapes:
-        piece = summed[place : place + length]
-        place += length
-        outs.append(piece if ndim == 1 else piece.reshape(lead, -1))
+    for array in small:
+        size = array.size // row_count
+        piece = summed[place : place + size]
+        place += size
+        outs.append(piece if array.ndim == 1 else piece.reshape(array.shape[0], -1))
     (
         out_gains,
         out_shifts,

time: 556 us -> 493 us (0.89)
  matrix products: 127 us -> 42.4 us
  Pallas kernels: 258 us -> 338 us
  local copies, waits for them, and re-layouts: 58.9 us -> 31.7 us
  waiting for transfers between devices: 35.9 us -> 13.9 us
  starting transfers between devices: 30.1 us -> 13.9 us
  other arithmetic: 36.3 us -> 43.8 us
    dot_general x28 -> x8, matrix products: 125 us -> 40.3 us  [mm(): return lax.dot_general(left, right, dims, preferred_element_type=F32)]
    pallas_call x5, Pallas kernels: 168 us -> 249 us  [the longest x1 191 us: attention_backward(): pl.pallas_call(functools.partial(attention_backward_kernel, reducer=reduc...]
    unnamed x233 -> x139, local copies, waits for them, and re-layouts: 40.2 us -> 12.1 us
    ppermute x24 -> x12, waiting for transfers between devices: 35.9 us -> 13.9 us  [swap(): return lax.ppermute(block, axis, [(i, i ^ mask) for i in range(count)])]
    another operation x2 -> x4, other arithmetic: 0.01 us -> 18 us  [the longest x1 10.3 us: shards(): jnp.stack(keyvals)]
    ppermute x24 -> x12, starting transfers between devices: 30.1 us -> 13.9 us  [swap(): return lax.ppermute(block, axis, [(i, i ^ mask) for i in range(count)])]
    reduce_sum x11 -> x0, other arithmetic: 13.4 us -> none  [the longest x4 4.15 us: shards(): grad_v_bias = jnp.sum(every_v.astype(F32), axis=0)]
    concatenate x5 -> x3, local copies, waits for them, and re-layouts: 6.69 us -> 0.15 us  [the longest x1 0.12 us: shards(): jnp.concatenate([array.reshape(row_count, -1) if array.ndim == 1 else jnp...]
  transfers between devices with their start and end apart: 24 -> 12, of which waited for: 12 -> 3; matrix products, arithmetic and copies ran while one was open for 8% -> 6% of each run, Pallas kernels for 2% -> 0%
where the time goes in v2:
time: 493 us; the launch traced here: 488 us
  Pallas kernels  338 us (69%)
  other arithmetic  43.8 us (9%)
  matrix products  42.4 us (9%)
  local copies, waits for them, and re-layouts  31.7 us (6%)
  starting transfers between devices  13.9 us (3%)
  waiting for transfers between devices  13.9 us (3%)
    pallas_call x1, Pallas kernels, attention_backward(): pl.pallas_call(functools.partial(attention_backward_kernel, reducer=reduc...  191 us
    pallas_call x1, Pallas kernels, refine(): pl.pallas_call(functools.partial(refine_kernel, items=items, rows=rows, c...  58.9 us
    pallas_call x1, Pallas kernels, mlp_backward(): pl.pallas_call(functools.partial(mlp_backward_kernel, blocks=blocks, row_...  40.9 us
    dot_general x8, matrix products, mm(): return lax.dot_general(left, right, dims, preferred_element_type=F32)  40.3 us
    pallas_call x3, Pallas kernels, attention_forward(): pl.pallas_call(attention_forward_kernel, grid=(groups,), in_specs=[pl.Blo...  30.8 us
    ppermute x12, waiting for transfers between devices, swap(): return lax.ppermute(block, axis, [(i, i ^ mask) for i in range(count)])  13.9 us
    ppermute x12, starting transfers between devices, swap(): return lax.ppermute(block, axis, [(i, i ^ mask) for i in range(count)])  13.9 us
    pallas_call x1, Pallas kernels, all_sum(): pl.pallas_call(functools.partial(all_sum_kernel, count=count, others=othe...  12.1 us
  transfers between devices with their start and end apart: 12, of which 3 were waited for; matrix products, arithmetic and copies ran while one was open for 6% of the time, Pallas kernels for 0%

profile of v2, /device:TPU:0, one launch (start us, length us, event | category | flops | bytes accessed | tf_op | source)
XLA Modules:
  0.0 488.2 jit_solution(4319498127956984096)
XLA Ops:
  7.0 3.0 collective-permute-start.9
  15.2 2.6 add_convert_fusion.3
  23.7 2.6 pad_maximum_fusion.2.q_ref
  40.8 5.0 %collective-permute-done.10 = bf16[320,768]{1,0:T(8,128)(2,1)S(1)} collective-permute-done((bf16[320,768]{1,0:T(8,128)(2,1)S(1)}, bf16[320,768]{1,0:T(8,128)(2,1)S(1)}, u32[]{:S(2)}, u32[]{:S(2)}) %collective-permute-start.10) | collective-permute-done | bytes 491552 | tf_op jit(solution)/shard_map/ppermute | solution.py:83
  47.0 3.7 fusion.2.k_ref.v_ref
  50.7 5.6 %collective-permute-done.6 = bf16[320,768]{1,0:T(8,128)(2,1)S(1)} collective-permute-done((bf16[320,768]{1,0:T(8,128)(2,1)S(1)}, bf16[320,768]{1,0:T(8,128)(2,1)S(1)}, u32[]{:S(2)}, u32[]{:S(2)}) %collective-permute-start.6) | collective-permute-done | bytes 491552 | tf_op jit(solution)/shard_map/ppermute | solution.py:83
  57.5 3.5 fusion.1.k_ref.v_ref
  61.0 3.3 collective-permute-done.2
  65.4 3.5 fusion.k_ref.v_ref
  68.9 10.2 %attention_forward.3 = (bf16[320,768]{1,0:T(8,128)(2,1)S(1)}, f32[3,8,1280]{2,1,0:T(8,128)S(1)}) custom-call(s32[5]{0:T(128)S(1)} %concatenate.61.info_ref, bf16[320,768]{1,0:T(8,128)(2,1)S(1)} %get-tuple-element.96.q_ref, bf16[1280,1536]{1,0:T(8,128)(2,1)S(1)} %fusion.k_ref.v_ref, bf16[1280,1536]{1,0:T(8,128)(2,1)S(1)} %fusion.k_ref.v_ref), custom_call_target="tpu_custom_call" | custom-call | flops 5033164800 | bytes 4915200 | tf_op jit(solution)/shard_map/attention_forward/pallas_call | solution.py:160
  79.2 10.2 %attention_forward.4 = (bf16[320,768]{1,0:T(8,128)(2,1)S(1)}, f32[3,8,1280]{2,1,0:T(8,128)S(1)}) custom-call(s32[5]{0:T(128)S(1)} %concatenate.66.info_ref, bf16[320,768]{1,0:T(8,128)(2,1)S(1)} %get-tuple-element.95.q_ref, bf16[1280,1536]{1,0:T(8,128)(2,1)S(1)} %fusion.1.k_ref.v_ref, bf16[1280,1536]{1,0:T(8,128)(2,1)S(1)} %fusion.1.k_ref.v_ref), custom_call_target="tpu_custom_call" | custom-call | flops 5033164800 | bytes 4915200 | tf_op jit(solution)/shard_map/attention_forward/pallas_call | solution.py:160
  89.5 10.4 %attention_forward.5 = (bf16[320,768]{1,0:T(8,128)(2,1)S(1)}, f32[3,8,1280]{2,1,0:T(8,128)S(1)}) custom-call(s32[5]{0:T(128)S(1)} %concatenate.70.info_ref, bf16[320,768]{1,0:T(8,128)(2,1)S(1)} %get-tuple-element.94.q_ref, bf16[1280,1536]{1,0:T(8,128)(2,1)S(1)} %fusion.2.k_ref.v_ref, bf16[1280,1536]{1,0:T(8,128)(2,1)S(1)} %fusion.2.k_ref.v_ref), custom_call_target="tpu_custom_call" | custom-call | flops 5033164800 | bytes 4915200 | tf_op jit(solution)/shard_map/attention_forward/pallas_call | solution.py:160
  101.1 3.0 fusion.23.resid_ref
  109.4 17.5 %add_convert_fusion = (bf16[960,3072]{1,0:T(8,128)(2,1)}, bf16[960,3072]{1,0:T(8,128)(2,1)S(1)}) fusion(f32[3072]{0:T(1024)S(1)} %copy-done.50, bf16[960,768]{1,0:T(8,128)(2,1)S(1)} %add_convert_fusion.2.normed_ref, bf16[768,3072]{1,0:T(8,128)(2,1)} %fc1_ref.1), kind=kOutput, calls=%fused_computation.2 | convolution fusion | flops 4606525440 | bytes 18001920 | tf_op jit(solution)/shard_map/dot_general | solution.py:28
  127.0 5.8 %add_convert_fusion.1 = (bf16[960,768]{1,0:T(8,128)(2,1)}, f32[960,768]{1,0:T(8,128)S(1)}) fusion(f32[960,768]{1,0:T(8,128)S(1)} %copy-done.10, f32[768]{0:T(1024)S(1)} %copy-done.43, bf16[960,3072]{1,0:T(8,128)(2,1)S(1)} %get-tuple-element.90.hidden_ref, bf16[3072,768]{1,0:T(8,128)(2,1)S(1)} %bitcast.125), kind=kOutput, calls=%fused_computation.34 | convolution fusion | flops 4532060160 | bytes 17992704 | tf_op jit(solution)/shard_map/dot_general | solution.py:28
  134.7 58.9 %refine.1 = (bf16[3,16,80,256]{3,2,1,0:T(8,128)(2,1)}, f32[3,8,48,256]{3,2,1,0:T(8,128)}, bf16[4,2,2,192,768]{4,3,2,1,0:T(8,128)(2,1)}, f32[4,256]{1,0:T(4,128)}, f32[2,3,256]{2,1,0:T(4,128)}) custom-call(f32[3,8,48,256]{3,2,1,0:T(8,128)} %pad.9.field_ref, bf16[4,2304,256]{2,1,0:T(8,128)(2,1)} %weight_ref.1, f32[4,256]{1,0:T(4,128)} %bias_ref.1, ...), custom_call_target="tpu_custom_call" | custom-call | flops 13589544960 | bytes 20971520 | tf_op jit(solution)/shard_map/refine/pallas_call | solution.py:527
  195.8 40.9 %mlp_backward.1 = (bf16[1,2,2,192,768]{4,3,2,1,0:T(8,128)(2,1)}, bf16[1,2,2,192,768]{4,3,2,1,0:T(8,128)(2,1)}, bf16[4,2,2,192,768]{4,3,2,1,0:T(8,128)(2,1)}, bf1...) custom-call(bf16[960,256]{1,0:T(8,128)(2,1)} %fusion.30.tap_grad_ref, ...), custom_call_target="tpu_custom_call" | custom-call | flops 18119393280 | bytes 41943040 | tf_op jit(solution)/shard_map/mlp_backward/pallas_call | solution.py:1144
  240.1 10.3 %pad_maximum_fusion.k_ref.v_ref = bf16[3,1280,1536]{2,1,0:T(8,128)(2,1)} fusion(bf16[1,1280,1536]{2,1,0:T(8,128)(2,1)S(1)} %bitcast.107, bf16[1,1280,1536]{2,1,0:T(8,128)(2,1)} %bitcast.108, bf16[1,1280,1536]{2,1,0:T(8,128)(2,1)} %bitcast.109), kind=kLoop, calls=%fused_computation.1 | loop fusion | flops 11796480 | bytes 23592960 | tf_op jit(solution)/shard_map/stack | solution.py:1666
  250.5 3.3 pad_maximum_fusion.1.normed_ref
  253.8 190.9 %attention_backward.1 = (f32[3,320,768]{2,1,0:T(8,128)}, f32[3,8,256]{2,1,0:T(8,128)}, bf16[2,14,192,384]{3,2,1,0:T(8,128)(2,1)}, bf16[2,3,192,384]{3,2,1,0:T(8,128)(2,1)}) custom-call(s32[3]{0:T(128)} %valid_ref.1, bf16[3,320,768]{2,1,0:T(8,128)(2,1)} %pad_maximum_fusion.2.q_ref, bf16[3,1280,1536]{2,1,0:T(8,128)(2,1)} %pad_maximum_fusion.k_ref.v_ref, ...), custom_call_target="tpu_custom_call" | custom-call | flops 94371840000 | bytes 41943040 | tf_op jit(solution)/shard_map/attention_backward/pallas_call | solution.py:1482
  445.7 3.7 fusion.12
  453.2 12.1 %sum_small.1 = f32[32,128]{1,0:T(8,128)} custom-call(f32[4,32,128]{2,1,0:T(8,128)} %bitcast.118), custom_call_target="tpu_custom_call" | custom-call | tf_op jit(solution)/shard_map/sum_small/pallas_call | solution.py:979
  474.8 3.4 unpack.3
  481.0 5.5 %fusion.6 = f32[960,768]{1,0:T(8,128)} fusion(f32[960,768]{1,0:T(8,128)} %get-tuple-element.52, f32[3,320,768]{2,1,0:T(8,128)} %get-tuple-element.62, bf16[3,320,768]{2,1,0:T(8,128)(2,1)S(1)} %copy-done.12, f32[960]{0:T(1024)S(1)} %div.38, f32[960]{0:T(1024)S(1)} %div.36, f32[768]{0:T(1024)S(1)} %copy-done.30, f32[960]{0:T(1024)S(1)} %copy-done.36, ...), kind=kLoop, calls=%fused_computation.17 | loop fusion | flops 6635520 | bytes 10340352 | tf_op jit(solution)/shard_map/add | solution.py:1678
  (250 shorter events, 65.1 us)
Async XLA Ops:
  0.7 18.4 %copy-start = (f32[8,256]{1,0:T(8,128)S(1)}, f32[8,256]{1,0:T(8,128)}, u32[]{:S(2)}) copy-start(f32[8,256]{1,0:T(8,128)} %param.41) | copy-start | bytes 24580
  7.0 19.3 %collective-permute-start.9 = (bf16[160,768]{1,0:T(8,128)(2,1)}, bf16[160,768]{1,0:T(8,128)(2,1)}, u32[]{:S(2)}, u32[]{:S(2)}) collective-permute-start(bf16[160,768]{1,0:T(8,128)(2,1)} %get-tuple-element.97), channel_id=1, source_target_pairs={{0,2},{1,3},{2,0},{3,1},{4,6},{5,7},{6,4},{7,5},{8,10},{9,11},{10,... | collective-permute-start | bytes 737288 | tf_op jit(solution)/shard_map/ppermute | solution.py:83
  10.0 19.0 %collective-permute-start.8 = (bf16[160,768]{1,0:T(8,128)(2,1)}, bf16[160,768]{1,0:T(8,128)(2,1)}, u32[]{:S(2)}, u32[]{:S(2)}) collective-permute-start(bf16[160,768]{1,0:T(8,128)(2,1)} %get-tuple-element.98), channel_id=1, source_target_pairs={{0,1},{1,0},{2,3},{3,2},{4,5},{5,4},{6,7},{7,6},{8,9},{9,8},{10,11... | collective-permute-start | bytes 737288 | tf_op jit(solution)/shard_map/ppermute | solution.py:83
  11.5 19.5 %collective-permute-start.5 = (bf16[160,768]{1,0:T(8,128)(2,1)}, bf16[160,768]{1,0:T(8,128)(2,1)}, u32[]{:S(2)}, u32[]{:S(2)}) collective-permute-start(bf16[160,768]{1,0:T(8,128)(2,1)} %get-tuple-element.99), channel_id=1, source_target_pairs={{0,2},{1,3},{2,0},{3,1},{4,6},{5,7},{6,4},{7,5},{8,10},{9,11},{10,... | collective-permute-start | bytes 737288 | tf_op jit(solution)/shard_map/ppermute | solution.py:83
  12.0 20.2 %collective-permute-start.4 = (bf16[160,768]{1,0:T(8,128)(2,1)}, bf16[160,768]{1,0:T(8,128)(2,1)}, u32[]{:S(2)}, u32[]{:S(2)}) collective-permute-start(bf16[160,768]{1,0:T(8,128)(2,1)} %get-tuple-element.100), channel_id=1, source_target_pairs={{0,1},{1,0},{2,3},{3,2},{4,5},{5,4},{6,7},{7,6},{8,9},{9,8},{10,11... | collective-permute-start | bytes 737288 | tf_op jit(solution)/shard_map/ppermute | solution.py:83
  12.2 24.0 %collective-permute-start.1 = (bf16[160,768]{1,0:T(8,128)(2,1)}, bf16[160,768]{1,0:T(8,128)(2,1)}, u32[]{:S(2)}, u32[]{:S(2)}) collective-permute-start(bf16[160,768]{1,0:T(8,128)(2,1)} %get-tuple-element.101), channel_id=1, source_target_pairs={{0,2},{1,3},{2,0},{3,1},{4,6},{5,7},{6,4},{7,5},{8,10},{9,11},{10,... | collective-permute-start | bytes 737288 | tf_op jit(solution)/shard_map/ppermute | solution.py:83
  26.3 13.5 %collective-permute-start = (bf16[160,768]{1,0:T(8,128)(2,1)S(1)}, bf16[160,768]{1,0:T(8,128)(2,1)S(1)}, u32[]{:S(2)}, u32[]{:S(2)}) collective-permute-start(bf16[160,768]{1,0:T(8,128)(2,1)S(1)} %copy-done.24), channel_id=1, source_target_pairs={{0,1},{1,0},{2,3},{3,2},{4,5},{5,4},{6,7},{7,6},{8,9},{9,8},{10,11... | collective-permute-start | bytes 737288 | tf_op jit(solution)/shard_map/ppermute | solution.py:83
  29.0 16.8 %collective-permute-start.10 = (bf16[320,768]{1,0:T(8,128)(2,1)S(1)}, bf16[320,768]{1,0:T(8,128)(2,1)S(1)}, u32[]{:S(2)}, u32[]{:S(2)}) collective-permute-start(bf16[320,768]{1,0:T(8,128)(2,1)S(1)} %pad_maximum_fusion.7), channel_id=1, source_target_pairs={{0,1},{1,0},{2,3},{3,2},{4,5},{5,4},{6,7},{7,6},{8,9},{9,8},{10,11... | collective-permute-start | bytes 1474568 | tf_op jit(solution)/shard_map/ppermute | solution.py:83
  31.0 14.9 %collective-permute-start.11 = (bf16[320,768]{1,0:T(8,128)(2,1)S(1)}, bf16[320,768]{1,0:T(8,128)(2,1)S(1)}, u32[]{:S(2)}, u32[]{:S(2)}) collective-permute-start(bf16[320,768]{1,0:T(8,128)(2,1)S(1)} %pad_maximum_fusion.8), channel_id=1, source_target_pairs={{0,2},{1,3},{2,0},{3,1},{4,6},{5,7},{6,4},{7,5},{8,10},{9,11},{10,... | collective-permute-start | bytes 1474568 | tf_op jit(solution)/shard_map/ppermute | solution.py:83
  32.2 24.2 %collective-permute-start.6 = (bf16[320,768]{1,0:T(8,128)(2,1)S(1)}, bf16[320,768]{1,0:T(8,128)(2,1)S(1)}, u32[]{:S(2)}, u32[]{:S(2)}) collective-permute-start(bf16[320,768]{1,0:T(8,128)(2,1)S(1)} %pad_maximum_fusion.5), channel_id=1, source_target_pairs={{0,1},{1,0},{2,3},{3,2},{4,5},{5,4},{6,7},{7,6},{8,9},{9,8},{10,11... | collective-permute-start | bytes 1474568 | tf_op jit(solution)/shard_map/ppermute | solution.py:83
  36.2 20.2 %collective-permute-start.7 = (bf16[320,768]{1,0:T(8,128)(2,1)S(1)}, bf16[320,768]{1,0:T(8,128)(2,1)S(1)}, u32[]{:S(2)}, u32[]{:S(2)}) collective-permute-start(bf16[320,768]{1,0:T(8,128)(2,1)S(1)} %pad_maximum_fusion.6), channel_id=1, source_target_pairs={{0,2},{1,3},{2,0},{3,1},{4,6},{5,7},{6,4},{7,5},{8,10},{9,11},{10,... | collective-permute-start | bytes 1474568 | tf_op jit(solution)/shard_map/ppermute | solution.py:83
  39.9 24.4 %collective-permute-start.2 = (bf16[320,768]{1,0:T(8,128)(2,1)S(1)}, bf16[320,768]{1,0:T(8,128)(2,1)S(1)}, u32[]{:S(2)}, u32[]{:S(2)}) collective-permute-start(bf16[320,768]{1,0:T(8,128)(2,1)S(1)} %pad_maximum_fusion.3), channel_id=1, source_target_pairs={{0,1},{1,0},{2,3},{3,2},{4,5},{5,4},{6,7},{7,6},{8,9},{9,8},{10,11... | collective-permute-start | bytes 1474568 | tf_op jit(solution)/shard_map/ppermute | solution.py:83
  45.8 18.5 %collective-permute-start.3 = (bf16[320,768]{1,0:T(8,128)(2,1)S(1)}, bf16[320,768]{1,0:T(8,128)(2,1)S(1)}, u32[]{:S(2)}, u32[]{:S(2)}) collective-permute-start(bf16[320,768]{1,0:T(8,128)(2,1)S(1)} %pad_maximum_fusion.4), channel_id=1, source_target_pairs={{0,2},{1,3},{2,0},{3,1},{4,6},{5,7},{6,4},{7,5},{8,10},{9,11},{10,... | collective-permute-start | bytes 1474568 | tf_op jit(solution)/shard_map/ppermute | solution.py:83
  50.7 38.7 %copy-start.3 = (bf16[1280,1536]{1,0:T(8,128)(2,1)}, bf16[1280,1536]{1,0:T(8,128)(2,1)S(1)}, u32[]{:S(2)}) copy-start(bf16[1280,1536]{1,0:T(8,128)(2,1)S(1)} %fusion.2.k_ref.v_ref) | copy-start | bytes 11796484
  61.0 18.2 %copy-start.5 = (bf16[1280,1536]{1,0:T(8,128)(2,1)}, bf16[1280,1536]{1,0:T(8,128)(2,1)S(1)}, u32[]{:S(2)}) copy-start(bf16[1280,1536]{1,0:T(8,128)(2,1)S(1)} %fusion.1.k_ref.v_ref) | copy-start | bytes 11796484
  108.8 18.1 %slice-start = ((s8[4718592]{0:T(1024)(128)(4,1)}), s8[4194304]{0:T(1024)(128)(4,1)S(1)}, s32[]{:S(2)}) async-start(s8[4718592]{0:T(1024)(128)(4,1)} %bitcast.124), calls=%async_computation | async-start | bytes 8388608
  109.4 17.6 %copy-start.23 = (bf16[960,768]{1,0:T(8,128)(2,1)}, bf16[960,768]{1,0:T(8,128)(2,1)S(1)}, u32[]{:S(2)}) copy-start(bf16[960,768]{1,0:T(8,128)(2,1)S(1)} %add_convert_fusion.2.normed_ref) | copy-start | bytes 4423684
  109.4 17.6 %copy-start.43 = (f32[768]{0:T(1024)S(1)}, f32[768]{0:T(1024)}, u32[]{:S(2)}) copy-start(f32[768]{0:T(1024)} %param.35) | copy-start | bytes 9220
  109.4 17.6 %slice-start.1 = ((s8[4718592]{0:T(1024)(128)(4,1)}), s8[524288]{0:T(1024)(128)(4,1)S(1)}, s32[]{:S(2)}) async-start(s8[4718592]{0:T(1024)(128)(4,1)} %bitcast.124), calls=%async_computation.1 | async-start | bytes 1048576
  195.8 44.3 %copy-start.4 = (bf16[1280,1536]{1,0:T(8,128)(2,1)S(1)}, bf16[1280,1536]{1,0:T(8,128)(2,1)}, u32[]{:S(2)}) copy-start(bf16[1280,1536]{1,0:T(8,128)(2,1)} %copy-done.3) | copy-start | bytes 11796484
  253.8 191.9 %copy-start.28 = (f32[3,320]{1,0:T(4,128)S(1)}, f32[3,320]{1,0:T(4,128)}, u32[]{:S(2)}) copy-start(f32[3,320]{1,0:T(4,128)} %copy-done.27) | copy-start | bytes 11524
  253.8 191.9 %copy-start.30 = (f32[768]{0:T(1024)S(1)}, f32[768]{0:T(1024)}, u32[]{:S(2)}) copy-start(f32[768]{0:T(1024)} %copy-done.29) | copy-start | bytes 9220
  253.8 191.9 %copy-start.32 = (f32[3,320]{1,0:T(4,128)S(1)}, f32[3,320]{1,0:T(4,128)}, u32[]{:S(2)}) copy-start(f32[3,320]{1,0:T(4,128)} %copy-done.31) | copy-start | bytes 11524
  449.4 30.3 %copy-start.7 = (bf16[2,3,192,384]{3,2,1,0:T(8,128)(2,1)S(1)}, bf16[2,3,192,384]{3,2,1,0:T(8,128)(2,1)}, u32[]{:S(2)}) copy-start(bf16[2,3,192,384]{3,2,1,0:T(8,128)(2,1)} %get-tuple-element.68.held_ref) | copy-start | bytes 2654212
  (47 other events, 278.4 us)

commit v3 on v2

--- a/solution.py
+++ b/solution.py
@@ -78,35 +78,8 @@
     return result, jnp.sum(grad_out * unit, axis=0), jnp.sum(grad_out, axis=0)
 
 
-def swap(block, axis, mask):
-    count = lax.axis_size(axis)
-    return lax.ppermute(block, axis, [(i, i ^ mask) for i in range(count)])
-
-
 def axis_bits(axis):
     return (lax.axis_size(axis) - 1).bit_length()
-
-
-def gather_blocks(block):
-    bits = axis_bits("rows")
-    half = block.shape[0] // 2
-    halves = []
-    for order, part in (
-        (range(bits), block[:half]),
-        (range(bits - 1, -1, -1), block[half:]),
-    ):
-        held = {0: part}
-        for bit in order:
-            keys = sorted(held)
-            sent = jnp.concatenate([held[key] for key in keys]) if len(keys) > 1 else held[keys[0]]
-            got = swap(sent, "rows", 1 << bit)
-            for place, key in enumerate(keys):
-                held[key | (1 << bit)] = got[place * half : (place + 1) * half]
-        halves.append(held)
-    blocks = []
-    for j in range(1 << bits):
-        blocks += [halves[0][j], halves[1][j]]
-    return jnp.concatenate(blocks)
 
 
 def add_low(first, second):
@@ -124,62 +97,6 @@
         [jnp.where(head_mask(block.shape, h), block, zero) for h in range(HEADS_PER_GROUP)],
         axis=0,
     )
-
-
-def key_bias(index, dim, length, block, info_ref):
-    start = jnp.full_like(index, info_ref[1])
-    for j in range(1, length // block):
-        start = jnp.where(index >= j * block, info_ref[1 + j] - j * block, start)
-    return jnp.where(index + start < info_ref[0], 0.0, MASKED).astype(F32)
-
-
-def attention_forward_kernel(info_ref, q_ref, k_ref, v_ref, o_ref, lse_ref):
-    t, n = q_ref.shape[0], k_ref.shape[0]
-    bias = key_bias(lax.broadcasted_iota(jnp.int32, (1, n), 1), 1, n, t, info_ref)
-    keys, values = k_ref[...], v_ref[...]
-    queries = q_ref[...] * jnp.asarray(HEAD_DIM**-0.5, BF)
-    out = jnp.zeros((t, GROUP), F32)
-    for h in range(HEADS_PER_GROUP):
-        mask = head_mask((t, GROUP), h)
-        one = jnp.where(mask, queries, jnp.zeros_like(queries))
-        scores = mm(one, keys, NT) + bias
-        top = jnp.max(scores, axis=1, keepdims=True)
-        probs = jnp.exp2((scores - top) * LOG2E)
-        total = jnp.sum(probs, axis=1, keepdims=True)
-        weighted = mm(probs.astype(BF), values)
-        out = jnp.where(mask, weighted * (1.0 / total), out)
-        lse = top * LOG2E + jnp.log2(total)
-        lse_ref[0, :, pl.ds(h * t, t)] = jnp.transpose(jnp.broadcast_to(lse, (t, 128)))[:8]
-    o_ref[...] = out.astype(BF)
-
-
-def attention_forward(info, queries, keyvals):
-    t, d = queries.shape
-    n = keyvals.shape[0]
-    groups = d // GROUP
-    return pl.pallas_call(
-        attention_forward_kernel,
-        grid=(groups,),
-        in_specs=[
-            pl.BlockSpec(memory_space=pltpu.SMEM),
-            pl.BlockSpec((t, GROUP), lambda i: (0, i)),
-            pl.BlockSpec((n, GROUP), lambda i: (0, i)),
-            pl.BlockSpec((n, GROUP), lambda i: (0, i + groups)),
-        ],
-        out_specs=[
-            pl.BlockSpec((t, GROUP), lambda i: (0, i)),
-            pl.BlockSpec((1, 8, HEADS_PER_GROUP * t), lambda i: (i, 0, 0)),
-        ],
-        out_shape=[
-            jax.ShapeDtypeStruct((t, d), BF),
-            jax.ShapeDtypeStruct((groups, 8, HEADS_PER_GROUP * t), F32),
-        ],
-        compiler_params=pltpu.CompilerParams(vmem_limit_bytes=40 << 20),
-        cost_estimate=pl.CostEstimate(
-            flops=16 * t * n * d, bytes_accessed=4 * t * d + 4 * n * d, transcendentals=12 * t * n
-        ),
-        name="attention_forward",
-    )(info, queries, keyvals, keyvals)
 
 
 WIDE = 48
@@ -991,6 +908,240 @@
         compiler_params=pltpu.CompilerParams(collective_id=collective_id, has_side_effects=True),
         name="sum_small",
     )(value)
+
+
+class Gather:
+    def __init__(self, bits, items):
+        self.bits, self.items = bits, items
+        self.orders = (tuple(range(bits)), tuple(range(bits - 1, -1, -1)))
+
+    def bind(self, held, send_sem, recv_sem):
+        self.held, self.send_sem, self.recv_sem = held, send_sem, recv_sem
+
+    def place(self, item, half, stage, now):
+        order = self.orders[half]
+        index = [0] * self.bits
+        for done in order[:stage]:
+            index[self.bits - 1 - done] = slice(None)
+        index[self.bits - 1 - order[stage]] = now
+        size = self.held.shape[-2] // 2
+        return (item,) + tuple(index) + (pl.ds(half * size, size),)
+
+    def copy(self, item, stage, half):
+        me, at = lax.axis_index("rows"), lax.axis_index("items")
+        return pltpu.make_async_remote_copy(
+            src_ref=self.held.at[self.place(item, half, stage, 0)],
+            dst_ref=self.held.at[self.place(item, half, stage, 1)],
+            send_sem=self.send_sem.at[item, stage, half],
+            recv_sem=self.recv_sem.at[item, stage, half],
+            device_id=(at, flip(me, self.orders[half][stage])),
+            device_id_type=MESH,
+        )
+
+    def start(self, item, stage):
+        for half in (0, 1):
+            self.copy(item, stage, half).start()
+
+    def arrived(self, item, stage):
+        for half in (0, 1):
+            self.copy(item, stage, half).wait_recv()
+
+    def drain(self, item):
+        for stage in range(self.bits):
+            for half in (0, 1):
+                self.copy(item, stage, half).wait_send()
+
+
+def attention_forward_kernel(
+    valid_ref,
+    tokens_ref,
+    gain_ref,
+    shift_ref,
+    q_bias_ref,
+    v_bias_ref,
+    wq_ref,
+    wk_ref,
+    wv_ref,
+    q_ref,
+    k_ref,
+    v_ref,
+    o_ref,
+    lse_ref,
+    normed_ref,
+    held,
+    send_sem,
+    recv_sem,
+    copy_sem,
+    *,
+    gather,
+    groups,
+    items,
+):
+    gather.bind(held, send_sem, recv_sem)
+    step = pl.program_id(0)
+    item, group = step // groups, step % groups
+    t, width = held.shape[-2:]
+    n = k_ref.shape[1]
+    me, at = lax.axis_index("rows"), lax.axis_index("items")
+    bits = gather.bits
+    mine = (0,) * bits
+
+    def store(which):
+        held[(which,) + mine] = layer_norm(
+            tokens_ref[which].astype(F32), gain_ref[...], shift_ref[...]
+        ).astype(BF)
+
+    def keep(which):
+        return pltpu.make_async_copy(held.at[which], normed_ref.at[which], copy_sem.at[which])
+
+    @pl.when(step == 0)
+    def _():
+        store(0)
+        barrier = pltpu.get_barrier_semaphore()
+        for bit in range(bits):
+            pl.semaphore_signal(
+                barrier, inc=1, device_id=(at, flip(me, bit)), device_id_type=MESH
+            )
+        pl.semaphore_wait(barrier, bits)
+        gather.start(0, 0)
+        for which in range(1, items):
+            store(which)
+        for stage in range(1, bits):
+            gather.arrived(0, stage - 1)
+            gather.start(0, stage)
+        gather.start(1, 0)
+
+    @pl.when(group == 0)
+    def _():
+        gather.arrived(item, bits - 1)
+        keep(item).start()
+
+    limit = valid_ref[item] * PC
+    index = lax.broadcasted_iota(jnp.int32, (1, n), 1)
+    bias = jnp.where(index + key_shift(index, n, t, me) < limit, 0.0, MASKED).astype(F32)
+    every = held[item].reshape(n, width)
+    keys = mm(every, wk_ref[...]).astype(BF)
+    values = (mm(every, wv_ref[...]) + v_bias_ref[...]).astype(BF)
+    queries = (mm(held[(item,) + mine], wq_ref[...]) + q_bias_ref[...]).astype(BF)
+    k_ref[0] = keys
+    v_ref[0] = values
+    q_ref[0] = queries
+    queries = queries * jnp.asarray(HEAD_DIM**-0.5, BF)
+    out = jnp.zeros((t, GROUP), F32)
+    for h in range(HEADS_PER_GROUP):
+        mask = head_mask((t, GROUP), h)
+        one = jnp.where(mask, queries, jnp.zeros_like(queries))
+        scores = mm(one, keys, NT) + bias
+        top = jnp.max(scores, axis=1, keepdims=True)
+        probs = jnp.exp2((scores - top) * LOG2E)
+        total = jnp.sum(probs, axis=1, keepdims=True)
+        weighted = mm(probs.astype(BF), values)
+        out = jnp.where(mask, weighted * (1.0 / total), out)
+        lse = top * LOG2E + jnp.log2(total)
+        lse_ref[0, 0, :, pl.ds(h * t, t)] = jnp.transpose(jnp.broadcast_to(lse, (t, 128)))[:8]
+    o_ref[0] = out.astype(BF)
+
+    for stage in range(1, bits):
+
+        @pl.when((group == stage - 1) & (item + 1 < items))
+        def _(stage=stage):
+            gather.arrived(item + 1, stage - 1)
+            gather.start(item + 1, stage)
+
+    @pl.when((group == bits - 2) & (item + 2 < items))
+    def _():
+        gather.start(item + 2, 0)
+
+    @pl.when(step == items * groups - 1)
+    def _():
+        for which in range(items):
+            gather.drain(which)
+            keep(which).wait()
+
+
+def attention_forward(valid_rows, tokens, gain, shift, qkv_weight, q_bias, v_bias, collective_id):
+    items, t, d = tokens.shape
+    bits = axis_bits("rows")
+    n = t << bits
+    groups = d // GROUP
+    rows4 = HEADS_PER_GROUP * t
+    vmem = pl.BlockSpec(memory_space=pltpu.VMEM)
+
+    def weight_spec(kind):
+        return pl.BlockSpec((d, GROUP), lambda i: (0, kind * groups + i % groups))
+
+    bias_spec = pl.BlockSpec((1, GROUP), lambda i: (0, i % groups))
+    query_spec = pl.BlockSpec((1, t, GROUP), lambda i: (i // groups, 0, i % groups))
+    key_spec = pl.BlockSpec((1, n, GROUP), lambda i: (i // groups, 0, i % groups))
+    return pl.pallas_call(
+        functools.partial(
+            attention_forward_kernel, gather=Gather(bits, items), groups=groups, items=items
+        ),
+        grid=(items * groups,),
+        in_specs=[
+            pl.BlockSpec(memory_space=pltpu.SMEM),
+            vmem,
+            vmem,
+            vmem,
+            bias_spec,
+            bias_spec,
+            weight_spec(0),
+            weight_spec(1),
+            weight_spec(2),
+        ],
+        out_specs=[
+            query_spec,
+            key_spec,
+            key_spec,
+            query_spec,
+            pl.BlockSpec((1, 1, 8, rows4), lambda i: (i // groups, i % groups, 0, 0)),
+            pl.BlockSpec(memory_space=pl.ANY),
+        ],
+        out_shape=[
+            jax.ShapeDtypeStruct((items, t, d), BF),
+            jax.ShapeDtypeStruct((items, n, d), BF),
+            jax.ShapeDtypeStruct((items, n, d), BF),
+            jax.ShapeDtypeStruct((items, t, d), BF),
+            jax.ShapeDtypeStruct((items, groups, 8, rows4), F32),
+            jax.ShapeDtypeStruct((items,) + (2,) * bits + (t, d), BF),
+        ],
+        scratch_shapes=[
+            pltpu.VMEM((items,) + (2,) * bits + (t, d), BF),
+            pltpu.SemaphoreType.DMA((items, bits, 2)),
+            pltpu.SemaphoreType.DMA((items, bits, 2)),
+            pltpu.SemaphoreType.DMA((items,)),
+        ],
+        compiler_params=pltpu.CompilerParams(
+            vmem_limit_bytes=52 << 20, collective_id=collective_id, has_side_effects=True
+        ),
+        cost_estimate=pl.CostEstimate(
+            flops=60 * items * t * n * d,
+            bytes_accessed=40 << 20,
+            transcendentals=12 * items * t * n,
+        ),
+        name="attention_forward",
+    )(
+        valid_rows,
+        tokens,
+        gain,
+        shift,
+        q_bias,
+        v_bias,
+        qkv_weight,
+        qkv_weight,
+        qkv_weight,
+    )
+
+
+def key_shift(index, length, block, me):
+    start = jnp.full_like(index, me * block)
+    for j in range(1, length // block):
+        other = me
+        for bit in range(j.bit_length()):
+            if j >> bit & 1:
+                other = flip(other, bit)
+        start = jnp.where(index >= j * block, (other - j) * block, start)
+    return start
 
 
 def shares_of(bits):
@@ -1444,22 +1595,11 @@
         late.finish()
 
 
-def key_shift(index, length, block, me):
-    start = jnp.full_like(index, me * block)
-    for j in range(1, length // block):
-        other = me
-        for bit in range(j.bit_length()):
-            if j >> bit & 1:
-                other = flip(other, bit)
-        start = jnp.where(index >= j * block, (other - j) * block, start)
-    return start
-
-
 def attention_backward(
-    valid_rows, queries, keyvals, grads, outs, lse, normed, qkv_weight, packed, collective_id
+    valid_rows, queries, keys, values, grads, outs, lse, normed, qkv_weight, packed, collective_id
 ):
     items, t, d = queries.shape
-    n = keyvals.shape[1]
+    n = keys.shape[1]
     groups = d // GROUP
     bits = axis_bits("rows")
     depth = d >> bits
@@ -1476,8 +1616,7 @@
     def weight_spec(kind):
         return pl.BlockSpec((d, GROUP), lambda i: (0, kind * groups + i % groups))
 
-    def key_spec(kind):
-        return pl.BlockSpec((1, n, GROUP), lambda i: (i // groups, 0, kind * groups + i % groups))
+    key_spec = pl.BlockSpec((1, n, GROUP), lambda i: (i // groups, 0, i % groups))
 
     outs = pl.pallas_call(
         functools.partial(
@@ -1495,8 +1634,8 @@
         in_specs=[
             pl.BlockSpec(memory_space=pltpu.SMEM),
             query_spec,
-            key_spec(0),
-            key_spec(1),
+            key_spec,
+            key_spec,
             query_spec,
             query_spec,
             pl.BlockSpec((1, 1, 8, rows4), lambda i: (i // groups, i % groups, 0, 0)),
@@ -1536,8 +1675,8 @@
     )(
         valid_rows,
         queries,
-        keyvals,
-        keyvals,
+        keys,
+        values,
         grads,
         outs,
         lse,
@@ -1582,25 +1721,17 @@
     last_index = row_count - 1
 
     flat_in = tokens.reshape(-1, width).astype(F32)
-    normed_one = layer_norm(flat_in, norm_gains[0], norm_biases[0]).astype(BF)
-    normed_all = [
-        gather_blocks(normed_one[i * tok_here : (i + 1) * tok_here]) for i in range(items_here)
-    ]
-    starts = jnp.stack([(row_index ^ j) * tok_here for j in range(row_count)]).astype(jnp.int32)
-    infos = [
-        jnp.concatenate([valid_rows[i : i + 1] * PC, starts]) for i in range(items_here)
-    ]
-    key_weight = qkv_weight[:, width:]
-    key_shift = jnp.concatenate([jnp.zeros((width,), F32), qv_bias[width:]])
-    queries = (mm(normed_one, qkv_weight[:, :width]) + qv_bias[:width]).astype(BF)
-    queries = [queries[i * tok_here : (i + 1) * tok_here] for i in range(items_here)]
-    keyvals, attended, lses = [], [], []
-    for i in range(items_here):
-        keyvals.append((mm(normed_all[i], key_weight) + key_shift).astype(BF))
-        out, lse = attention_forward(infos[i], queries[i], keyvals[i])
-        attended.append(out)
-        lses.append(lse)
-    attended_flat = jnp.concatenate(attended)
+    queries, keys, values, attended, lses, normed_all = attention_forward(
+        valid_rows,
+        tokens,
+        norm_gains[:1],
+        norm_biases[:1],
+        qkv_weight,
+        qv_bias[None, :width],
+        qv_bias[None, width:],
+        5,
+    )
+    attended_flat = attended.reshape(-1, width)
     resid = flat_in + mm(attended_flat, out_weight) + out_bias
     normed_two = layer_norm(resid, norm_gains[1], norm_biases[1]).astype(BF)
     hidden_pre = mm(normed_two, fc1_weight) + fc1_bias
@@ -1662,12 +1793,13 @@
     fc2_grads = fc2_grads.reshape(fc2_grads.shape[:1] + shares + fc2_grads.shape[2:])
     grads_in, qkv_sums, early_sum, late_sum = attention_backward(
         valid_rows,
-        jnp.stack(queries),
-        jnp.stack(keyvals),
+        queries,
+        keys,
+        values,
         grad_attended.reshape(tokens.shape),
-        attended_flat.reshape(tokens.shape),
-        jnp.stack(lses),
-        jnp.stack(normed_all),
+        attended,
+        lses,
+        normed_all.reshape(keys.shape),
         qkv_weight,
         [conv_grads, tap_grads, fc2_grads, fc1_grads, out_grads],
         3,

time: 493 us -> 457 us (0.927)
  Pallas kernels: 338 us -> 379 us
  other arithmetic: 43.8 us -> 11 us
  starting transfers between devices: 13.9 us -> 0 us
  waiting for transfers between devices: 13.9 us -> 0 us
  matrix products: 42.4 us -> 29.3 us
    pallas_call x3 -> x1, Pallas kernels: 30.8 us -> 70.3 us  [attention_forward(): pl.pallas_call(functools.partial(attention_forward_kernel, gather=Gather(...]
    another operation x4 -> x0, other arithmetic: 18 us -> none  [the longest x1 10.3 us: shards(): jnp.stack(keyvals)]
    ppermute x12 -> x0, waiting for transfers between devices: 13.9 us -> none  [swap(): return lax.ppermute(block, axis, [(i, i ^ mask) for i in range(count)])]
    ppermute x12 -> x0, starting transfers between devices: 13.9 us -> none  [swap(): return lax.ppermute(block, axis, [(i, i ^ mask) for i in range(count)])]
    dot_general x8 -> x4, matrix products: 40.3 us -> 27.2 us  [mm(): return lax.dot_general(left, right, dims, preferred_element_type=F32)]
    concatenate x6 -> x0, other arithmetic: 5.51 us -> none  [gather_blocks(): jnp.concatenate([held[key] for key in keys])]
    unnamed x139 -> x67, local copies, waits for them, and re-layouts: 12.1 us -> 10.5 us
  transfers between devices with their start and end apart: 12 -> 0, of which waited for: 3 -> 0; matrix products, arithmetic and copies ran while one was open for 6% -> 0% of each run, Pallas kernels for 0% -> 0%
where the time goes in v3:
time: 457 us; the launch traced here: 448 us
  Pallas kernels  379 us (83%)
  matrix products  29.3 us (6%)
  local copies, waits for them, and re-layouts  27.4 us (6%)
  other arithmetic  11 us (2%)
    pallas_call x1, Pallas kernels, attention_backward(): pl.pallas_call(functools.partial(attention_backward_kernel, reducer=reduc...  191 us
    pallas_call x1, Pallas kernels, attention_forward(): pl.pallas_call(functools.partial(attention_forward_kernel, gather=Gather(...  70.3 us
    pallas_call x1, Pallas kernels, refine(): pl.pallas_call(functools.partial(refine_kernel, items=items, rows=rows, c...  59.6 us
    pallas_call x1, Pallas kernels, mlp_backward(): pl.pallas_call(functools.partial(mlp_backward_kernel, blocks=blocks, row_...  40.9 us
    dot_general x4, matrix products, mm(): return lax.dot_general(left, right, dims, preferred_element_type=F32)  27.2 us
    pallas_call x1, Pallas kernels, all_sum(): pl.pallas_call(functools.partial(all_sum_kernel, count=count, others=othe...  12.2 us
    unnamed x67, local copies, waits for them, and re-layouts  10.5 us

profile of v3, /device:TPU:0, one launch (start us, length us, event | category | flops | bytes accessed | tf_op | source)
XLA Modules:
  0.0 448.1 jit_solution(11089566956127580763)
XLA Ops:
  0.7 2.0 slice_reduce_fusion.6
  4.1 70.3 %attention_forward.1 = (bf16[3,320,768]{2,1,0:T(8,128)(2,1)S(1)}, bf16[3,1280,768]{2,1,0:T(8,128)(2,1)}, bf16[3,1280,768]{2,1,0:T(8,128)(2,1)}, bf16[3,320,768]{...) custom-call(s32[3]{0:T(128)S(1)} %copy-done.4, bf16[3,320,768]{2,1,0:T(8,128)(2,1)} %tokens_ref.1, ...), custom_call_target="tpu_custom_call" | custom-call | flops 56623104000 | bytes 41943040 | tf_op jit(solution)/shard_map/attention_forward/pallas_call | solution.py:1076
  74.4 1.1 copy-done.6
  76.3 2.7 fusion.14.resid_ref
  80.3 2.1 copy-done.22
  82.4 15.5 %add_convert_fusion = (bf16[960,3072]{1,0:T(8,128)(2,1)}, bf16[960,3072]{1,0:T(8,128)(2,1)S(1)}) fusion(f32[3072]{0:T(1024)S(1)} %copy-done.24, bf16[960,768]{1,0:T(8,128)(2,1)S(1)} %add_convert_fusion.2.normed_ref, bf16[768,3072]{1,0:T(8,128)(2,1)S(1)} %copy-done.22), kind=kOutput, calls=%fused_computation.1 | convolution fusion | flops 4606525440 | bytes 18001920 | tf_op jit(solution)/shard_map/dot_general | solution.py:28
  98.0 6.4 %add_convert_fusion.1 = (bf16[960,768]{1,0:T(8,128)(2,1)}, f32[960,768]{1,0:T(8,128)}) fusion(f32[960,768]{1,0:T(8,128)S(1)} %fusion.14.resid_ref, f32[768]{0:T(1024)S(1)} %copy-done.19, bf16[960,3072]{1,0:T(8,128)(2,1)S(1)} %get-tuple-element.88.hidden_ref, bf16[3072,768]{1,0:T(8,128)(2,1)S(1)} %bitcast.87), kind=kOutput, calls=%fused_computation.23 | convolution fusion | flops 4532060160 | bytes 17992704 | tf_op jit(solution)/shard_map/dot_general | solution.py:28
  104.8 2.5 fusion.17
  107.3 1.2 pad.8.field_ref
  110.0 59.6 %refine.1 = (bf16[3,16,80,256]{3,2,1,0:T(8,128)(2,1)}, f32[3,8,48,256]{3,2,1,0:T(8,128)}, bf16[4,2,2,192,768]{4,3,2,1,0:T(8,128)(2,1)}, f32[4,256]{1,0:T(4,128)}, f32[2,3,256]{2,1,0:T(4,128)}) custom-call(f32[3,8,48,256]{3,2,1,0:T(8,128)} %pad.8.field_ref, bf16[4,2304,256]{2,1,0:T(8,128)(2,1)} %weight_ref.1, f32[4,256]{1,0:T(4,128)} %bias_ref.1, ...), custom_call_target="tpu_custom_call" | custom-call | flops 13589544960 | bytes 20971520 | tf_op jit(solution)/shard_map/refine/pallas_call | solution.py:444
  169.7 1.3 slice.96
  171.9 40.9 %mlp_backward.1 = (bf16[1,2,2,192,768]{4,3,2,1,0:T(8,128)(2,1)}, bf16[1,2,2,192,768]{4,3,2,1,0:T(8,128)(2,1)}, bf16[4,2,2,192,768]{4,3,2,1,0:T(8,128)(2,1)}, bf1...) custom-call(bf16[960,256]{1,0:T(8,128)(2,1)} %fusion.20.tap_grad_ref, ...), custom_call_target="tpu_custom_call" | custom-call | flops 18119393280 | bytes 41943040 | tf_op jit(solution)/shard_map/mlp_backward/pallas_call | solution.py:1295
  212.9 191.2 %attention_backward.1 = (f32[3,320,768]{2,1,0:T(8,128)}, f32[3,8,256]{2,1,0:T(8,128)}, bf16[2,14,192,384]{3,2,1,0:T(8,128)(2,1)}, bf16[2,3,192,384]{3,2,1,0:T(8,128)(2,1)}) custom-call(s32[3]{0:T(128)} %valid_ref.3, bf16[3,320,768]{2,1,0:T(8,128)(2,1)} %copy-done.6, bf16[3,1280,768]{2,1,0:T(8,128)(2,1)} %get-tuple-element.52.k_ref, ...), custom_call_target="tpu_custom_call" | custom-call | flops 94371840000 | bytes 41943040 | tf_op jit(solution)/shard_map/attention_backward/pallas_call | solution.py:1621
  404.1 2.2 copy-done.2
  406.3 3.4 unpack.3
  412.4 1.6 fusion.9
  418.0 12.2 %sum_small.1 = f32[32,128]{1,0:T(8,128)} custom-call(f32[4,32,128]{2,1,0:T(8,128)} %bitcast.81), custom_call_target="tpu_custom_call" | custom-call | tf_op jit(solution)/shard_map/sum_small/pallas_call | solution.py:896
  432.2 1.4 slice_bitcast_fusion
  434.8 1.4 slice.119
  436.2 1.3 fusion.33
  437.5 1.2 slice.121
  439.0 5.4 %fusion.3 = f32[960,768]{1,0:T(8,128)} fusion(f32[960,768]{1,0:T(8,128)} %get-tuple-element.50, f32[3,320,768]{2,1,0:T(8,128)} %get-tuple-element.62, bf16[3,320,768]{2,1,0:T(8,128)(2,1)S(1)} %copy-done.10, f32[960]{0:T(1024)S(1)} %div.36, f32[960]{0:T(1024)S(1)} %div.34, f32[960]{0:T(1024)S(1)} %div.33, f32[768]{0:T(1024)S(1)} %copy-done.15, f32[960]{0:T(1024)S(1)} %rsqrt.22), kind=kLoop, calls=%fused_computation.9 | loop fusion | flops 6635520 | bytes 10340352 | tf_op jit(solution)/shard_map/add | solution.py:1810
  444.4 1.3 unpack.2
  446.6 1.3 copy.54
  (128 shorter events, 17.3 us)
Async XLA Ops:
  0.7 107.8 %copy-start = (f32[8,256]{1,0:T(8,128)S(1)}, f32[8,256]{1,0:T(8,128)}, u32[]{:S(2)}) copy-start(f32[8,256]{1,0:T(8,128)} %param.41) | copy-start | bytes 24580
  4.1 72.2 %copy-start.9 = (bf16[3,320,768]{2,1,0:T(8,128)(2,1)S(1)}, bf16[3,320,768]{2,1,0:T(8,128)(2,1)}, u32[]{:S(2)}) copy-start(bf16[3,320,768]{2,1,0:T(8,128)(2,1)} %tokens_ref.1) | copy-start | bytes 4423684
  4.1 72.2 %copy-start.23 = (bf16[768,768]{1,0:T(8,128)(2,1)S(1)}, bf16[768,768]{1,0:T(8,128)(2,1)}, u32[]{:S(2)}) copy-start(bf16[768,768]{1,0:T(8,128)(2,1)} %out_w_ref.1) | copy-start | bytes 3538948
  4.1 72.2 %copy-start.26 = (f32[768]{0:T(1024)S(1)}, f32[768]{0:T(1024)}, u32[]{:S(2)}) copy-start(f32[768]{0:T(1024)} %param.31) | copy-start | bytes 9220
  79.0 25.7 %copy-start.8 = (f32[960,768]{1,0:T(8,128)}, f32[960,768]{1,0:T(8,128)S(1)}, u32[]{:S(2)}) copy-start(f32[960,768]{1,0:T(8,128)S(1)} %fusion.14.resid_ref) | copy-start | bytes 8847364
  79.8 18.1 %slice-start = ((s8[4718592]{0:T(1024)(128)(4,1)}), s8[4194304]{0:T(1024)(128)(4,1)S(1)}, s32[]{:S(2)}) async-start(s8[4718592]{0:T(1024)(128)(4,1)} %bitcast.86), calls=%async_computation | async-start | bytes 8388608
  82.4 15.5 %copy-start.13 = (bf16[960,768]{1,0:T(8,128)(2,1)}, bf16[960,768]{1,0:T(8,128)(2,1)S(1)}, u32[]{:S(2)}) copy-start(bf16[960,768]{1,0:T(8,128)(2,1)S(1)} %add_convert_fusion.2.normed_ref) | copy-start | bytes 4423684
  82.4 15.5 %copy-start.19 = (f32[768]{0:T(1024)S(1)}, f32[768]{0:T(1024)}, u32[]{:S(2)}) copy-start(f32[768]{0:T(1024)} %param.35) | copy-start | bytes 9220
  82.4 15.5 %slice-start.1 = ((s8[4718592]{0:T(1024)(128)(4,1)}), s8[524288]{0:T(1024)(128)(4,1)S(1)}, s32[]{:S(2)}) async-start(s8[4718592]{0:T(1024)(128)(4,1)} %bitcast.86), calls=%async_computation.1 | async-start | bytes 1048576
  97.9 6.5 %copy-start.29 = (bf16[960,3072]{1,0:T(8,128)(2,1)}, bf16[960,3072]{1,0:T(8,128)(2,1)S(1)}, u32[]{:S(2)}) copy-start(bf16[960,3072]{1,0:T(8,128)(2,1)S(1)} %get-tuple-element.88.hidden_ref) | copy-start | bytes 17694724
  97.9 6.5 %copy-start.5 = (s32[3]{0:T(128)S(1)}, s32[3]{0:T(128)}, u32[]{:S(2)}) copy-start(s32[3]{0:T(128)} %valid_ref.3) | copy-start | bytes 40
  97.9 6.8 %copy-start.14 = (bf16[768,256]{1,0:T(8,128)(2,1)S(1)}, bf16[768,256]{1,0:T(8,128)(2,1)}, u32[]{:S(2)}) copy-start(bf16[768,256]{1,0:T(8,128)(2,1)} %tap_w_ref.1) | copy-start | bytes 1179652
  97.9 6.8 %copy-start.21 = (f32[256]{0:T(256)S(1)}, f32[256]{0:T(256)}, u32[]{:S(2)}) copy-start(f32[256]{0:T(256)} %param.37) | copy-start | bytes 3076
  104.7 3.7 copy-start.27
  104.7 3.7 copy-start.28
  104.7 4.5 %copy-start.25 = (f32[8,256]{1,0:T(8,128)S(1)}, f32[8,256]{1,0:T(8,128)}, u32[]{:S(2)}) copy-start(f32[8,256]{1,0:T(8,128)} %param.40) | copy-start | bytes 24580
  406.3 4.3 copy-start.10
  406.3 5.2 %copy-start.15 = (f32[768]{0:T(1024)S(1)}, f32[768]{0:T(1024)}, u32[]{:S(2)}) copy-start(f32[768]{0:T(1024)} %get-tuple-element.109) | copy-start | bytes 9220
  410.9 3.2 copy-start.18
  410.9 4.2 copy-start.16
  410.9 5.2 %copy-start.17 = (f32[2,3,256]{2,1,0:T(4,128)S(1)}, f32[2,3,256]{2,1,0:T(4,128)}, u32[]{:S(2)}) copy-start(f32[2,3,256]{2,1,0:T(4,128)} %get-tuple-element.67) | copy-start | bytes 18436
  410.9 6.1 %copy-start.20 = (f32[4,256]{1,0:T(4,128)S(1)}, f32[4,256]{1,0:T(4,128)}, u32[]{:S(2)}) copy-start(f32[4,256]{1,0:T(4,128)} %get-tuple-element.66) | copy-start | bytes 12292
  439.0 5.4 %copy-start.3 = (bf16[2,3,192,384]{3,2,1,0:T(8,128)(2,1)S(1)}, bf16[2,3,192,384]{3,2,1,0:T(8,128)(2,1)}, u32[]{:S(2)}) copy-start(bf16[2,3,192,384]{3,2,1,0:T(8,128)(2,1)} %get-tuple-element.68.held_ref) | copy-start | bytes 2654212
  444.4 3.5 copy-start.1
  (8 other events, 14.5 us)
